TPU v7x, 256 devices: a whole 4x4x8 slice. The times are simulated.
256 devices in a mesh: aux: 32 (over z, x_lo, core), row: 8 (over y, x_hi).
Axes of the slice: x: 4 (x_hi: 2, x_lo: 2; x = x_hi * 2 + x_lo), y: 4, z: 8, core: 2. Of those that a mesh axis runs over, the one named last changes fastest.
Arguments:
- three_center: bfloat16 [1536, 8, 64, 512], P('aux', 'row'), may hold values from -2 to 2
- coefficients: bfloat16 [1024, 10240], P('aux'), may hold values from -6 to 6
- col_tiles: int32 [8, 8], P('row'), may hold values from 0 to 159, as said below
- tile_count: int32 [8], P('row'), may hold values from 1 to 8, as said below
Outputs:
- exchange_tiles: float32 [512, 512], P('row', 'aux')
- exchange_diagonal: float32 [512], P('row')
Inputs may be any that keep to these rules, and one draw needn't show every extreme that they name: `col_tiles`: the slots of one row tile name different column tiles. `tile_count`: some row tile has all 8 slots live.
All inputs are finite; a program needn't handle non-finite values.
Results may differ from a plain program's by a relative error of at most 0.0034.
Values may be sent and summed in bfloat16 or wider, within the bound.
No kernel may reach another device: no remote copies, remote signals or barrier semaphores. Data moves between devices by JAX's collectives and lax.ppermute only.
A program may use at most 128 MiB of HBM per device.

v0:
```python
import jax
import jax.numpy as jnp
from jax import lax
from jax.sharding import PartitionSpec as P


def select_tiles(coefficient_block, tile_lists, entry_counts, tile_width):
    ntiles = coefficient_block.shape[1] // tile_width
    slot_count = tile_lists.shape[1]
    tiled = coefficient_block.reshape(coefficient_block.shape[0], ntiles, tile_width)
    chosen_tiles = jnp.take(tiled, tile_lists.reshape(-1), axis=1)
    chosen_tiles = chosen_tiles.reshape(
        coefficient_block.shape[0], tile_lists.shape[0], slot_count, tile_width
    )
    active_tiles = jnp.arange(slot_count, dtype=jnp.int32)[None, :] < entry_counts[:, None]
    chosen_tiles = jnp.where(
        active_tiles[None, :, :, None], chosen_tiles, jnp.zeros((), jnp.bfloat16)
    )
    chosen_tiles = chosen_tiles.reshape(
        coefficient_block.shape[0], tile_lists.shape[0], slot_count * tile_width
    )
    return chosen_tiles.transpose(1, 0, 2)


def transform(integrals, chosen_tiles):
    result = jnp.einsum(
        "qrmk,rik->qrmi", integrals, chosen_tiles, preferred_element_type=jnp.float32
    )
    return result.reshape(result.shape[0], result.shape[1] * result.shape[2], result.shape[3])


def local(three_center, coefficients, col_tiles, tile_count):
    tile_width = three_center.shape[2]
    naux = lax.axis_size("aux")
    nrow = lax.axis_size("row")
    norb = coefficients.shape[0] * naux
    part = transform(
        three_center,
        select_tiles(
            lax.all_gather(coefficients, "aux", axis=0, tiled=True),
            col_tiles,
            tile_count,
            tile_width,
        ),
    )
    half = part
    half = half.astype(jnp.bfloat16)
    widened = half.astype(jnp.float32)
    local_norms = jnp.sum(widened * widened, axis=(0, 2))
    total_aux = three_center.shape[0] * naux
    norms = lax.psum(local_norms, "aux")
    exchange_diagonal = norms / jnp.float32(total_aux * norb)
    spread = lax.all_to_all(half, "row", split_axis=2, concat_axis=1, tiled=True)
    partial_k = lax.dot_general(
        spread, spread, (((0, 2), (0, 2)), ((), ())), preferred_element_type=jnp.float32
    )
    total_rows = partial_k.shape[0]
    summed = lax.psum_scatter(partial_k, "row", scatter_dimension=0, tiled=True)
    summed = lax.psum_scatter(summed, "aux", scatter_dimension=1, tiled=True)
    row_height = total_rows // nrow
    col_width = total_rows // naux
    row_ids = lax.axis_index("row") * row_height + jnp.arange(row_height, dtype=jnp.int32)
    col_ids = lax.axis_index("aux") * col_width + jnp.arange(col_width, dtype=jnp.int32)
    on_diagonal = row_ids[:, None] == col_ids[None, :]
    summed = jnp.where(on_diagonal, jnp.zeros((), jnp.float32), summed)
    exchange_tiles = summed / jnp.sqrt(jnp.float32(total_aux * norb))
    return (exchange_tiles, exchange_diagonal)


def solution(mesh):
    in_specs = (P("aux", "row", None, None), P("aux", None), P("row", None), P("row"))
    out_specs = (P("row", "aux"), P("row"))
    return jax.shard_map(local, mesh=mesh, in_specs=in_specs, out_specs=out_specs, check_vma=False)
```

profile of v0, /device:TPU:2, one launch (start us, length us, event | category | flops | bytes accessed | tf_op | source)
XLA Modules:
  0.0 519.1 jit_solution(7777839475672518186)
XLA Ops:
  7.2 0.0 copy-start
  7.2 0.0 all-gather.2.cloned.1.call-start
  7.2 0.7 all-gather.2.cloned.1.call-update
  7.9 0.0 reduce-scatter.5.cloned.1.call-start
  8.8 0.7 fusion.1
  9.4 0.7 compare_and_fusion
  10.1 123.5 %all-gather.2.cloned.1.call-done = bf16[1024,10240]{1,0:T(8,128)(2,1)} async-done(((bf16[32,10240]{1,0:T(8,128)(2,1)}), bf16[1024,10240]{1,0:T(8,128)(2,1)}) %all-gather.2.cloned.1.call-update) | async-done | bytes 20971536 | tf_op jit(solution)/shard_map/all_gather | solution.py:40
  133.6 28.0 %copy.12 = bf16[1024,10240]{0,1:T(8,128)(2,1)} copy(bf16[1024,10240]{1,0:T(8,128)(2,1)} %all-gather.2.cloned.1.call-done) | data formatting | bytes 41943040 | tf_op jit(solution)/shard_map/all_gather | solution.py:40
  161.6 8.5 %gather_fusion = bf16[8,1024,64]{1,2,0:T(8,128)(2,1)} fusion(bf16[1024,160,64]{0,2,1:T(8,128)(2,1)} %bitcast.40, s32[1024]{0:T(1024)S(1)} %pad_clamp_fusion), kind=kCustom, calls=%fused_computation | custom fusion | bytes 2097184 | tf_op jit(solution)/shard_map/jit(_take)/gather | solution.py:11
  170.1 1.4 select_select_fusion
  171.5 0.0 copy-done
  171.5 5.8 %multiply_reduce_fusion = (f32[64]{0:T(128)S(1)}, bf16[48,64,1024]{2,1,0:T(8,128)(2,1)}) fusion(bf16[1024,512,1]{0,1,2:T(8,128)(2,1)S(1)} %bitcast.43, bf16[48,1,64,512]{3,2,1,0:T(8,128)(2,1)S(1)} %copy-done), kind=kOutput, calls=%fused_computation.1 | convolution fusion | flops 3233808384 | bytes 10486016 | tf_op jit(solution)/shard_map/qrmk,rik->qrmi/dot_general | solution.py:26
  177.3 15.7 %copy.14 = bf16[48,64,1024]{1,0,2:T(8,128)(2,1)} copy(bf16[48,64,1024]{2,1,0:T(8,128)(2,1)} %get-tuple-element.9) | data formatting | bytes 12582912 | tf_op jit(solution)/shard_map/convert_element_type | solution.py:47
  193.0 13.8 %reshape.149 = bf16[8,2,196608]{2,1,0:T(2,128)(2,1)} reshape(bf16[1024,48,64]{2,1,0:T(8,128)(2,1)} %bitcast.38) | data formatting | bytes 12582912
  206.8 79.7 %all_to_all.18 = bf16[8,2,196608]{2,1,0:T(2,128)(2,1)} all-to-all(bf16[8,2,196608]{2,1,0:T(2,128)(2,1)} %reshape.149), channel_id=1, replica_groups=mesh['aux'=32,'row'=8] {'row'}, dimensions={0} | all-to-all | bytes 12582912 | tf_op jit(solution)/shard_map/all_to_all | solution.py:53
  286.5 13.3 %reshape.150 = bf16[1024,48,64]{2,1,0:T(8,128)(2,1)} reshape(bf16[8,2,196608]{2,1,0:T(2,128)(2,1)} %all_to_all.18) | data formatting | bytes 12582912
  299.8 14.1 %copy.15 = bf16[48,64,8,128]{3,1,2,0:T(8,128)(2,1)} copy(bf16[48,64,8,128]{1,0,3,2:T(8,128)(2,1)} %bitcast.39) | data formatting | bytes 12582912 | tf_op jit(solution)/shard_map/all_to_all | solution.py:53
  313.9 0.0 copy-start.1
  313.9 9.2 %convolution_bitcast_fusion = f32[512,512]{1,0:T(8,128)} fusion(bf16[48,512,128]{2,1,0:T(8,128)(2,1)} %bitcast.41), kind=kOutput, calls=%fused_computation.4 | convolution fusion | flops 3221225472 | bytes 7340032 | tf_op jit(solution)/shard_map/dot_general | solution.py:54
  323.1 0.0 reduce-scatter.5.cloned.1.call-update
  323.1 0.0 reduce-scatter.7.cloned.1.call-start
  323.2 73.5 %reduce-scatter.5.cloned.1.call-done = f32[64,512]{1,0:T(8,128)} async-done(((f32[512,512]{1,0:T(8,128)}), f32[64,512]{1,0:T(8,128)}) %reduce-scatter.5.cloned.1.call-update) | async-done | bytes 131088 | tf_op jit(solution)/shard_map/reduce_scatter | solution.py:58
  396.7 1.7 copy.19
  398.4 0.0 reduce-scatter.7.cloned.1.call-update
  398.5 51.2 %psum.7 = f32[64]{0:T(128)S(1)} all-reduce(f32[64]{0:T(128)S(1)} %get-tuple-element.8), channel_id=1, replica_groups=mesh['aux'=32,'row'=8] {'aux'}, use_global_device_ids=true, to_apply=%region_3.4 | all-reduce | flops 64 | bytes 512 | tf_op jit(solution)/shard_map/psum | solution.py:51
  449.7 0.5 broadcast_multiply_fusion
  450.2 60.9 %reduce-scatter.7.cloned.1.call-done = f32[16,64]{1,0:T(8,128)} async-done(((f32[512,64]{1,0:T(8,128)}), f32[16,64]{1,0:T(8,128)}) %reduce-scatter.7.cloned.1.call-update) | async-done | bytes 4112
  511.0 0.8 copy.20
  511.8 0.1 select_multiply_fusion
  511.9 0.7 copy.16
  512.6 0.0 copy-done.1
  (3 shorter events, 0.0 us)
Async XLA Ops:
  7.2 164.4 %copy-start = (bf16[48,1,64,512]{3,2,1,0:T(8,128)(2,1)S(1)}, bf16[48,1,64,512]{3,2,1,0:T(8,128)(2,1)}, u32[]{:S(2)}) copy-start(bf16[48,1,64,512]{3,2,1,0:T(8,128)(2,1)} %param.4) | copy-start | bytes 9437188
  7.2 126.4 %all-gather.2.cloned.1.call-start = ((), (), s32[]{:S(2)}) async-start(), calls=%async_computation.3 | async-start | bytes 21626880 | tf_op jit(solution)/shard_map/all_gather | solution.py:40
  7.9 388.8 %reduce-scatter.5.cloned.1.call-start = ((), (), s32[]{:S(2)}) async-start(), calls=%async_computation.4 | async-start | bytes 1179648 | tf_op jit(solution)/shard_map/reduce_scatter | solution.py:58
  313.9 198.7 %copy-start.1 = (bf16[48,1,64,512]{3,2,1,0:T(8,128)(2,1)S(1)}, bf16[48,1,64,512]{3,2,1,0:T(8,128)(2,1)}, u32[]{:S(2)}) copy-start(bf16[48,1,64,512]{3,2,1,0:T(8,128)(2,1)} %param.4) | copy-start | bytes 9437188
  323.1 188.0 %reduce-scatter.7.cloned.1.call-start = ((), (), s32[]{:S(2)}) async-start(), calls=%async_computation.5 | async-start | bytes 270336
Sparse Core Ops, SparseCore 0:
  9.9 123.6 all-gather.1
  323.2 73.4 reduce-scatter.4
  399.3 111.6 reduce-scatter.6
where the time goes:
time: 525 us; the launch traced here: 519 us
  waiting for transfers between devices  259 us (49%)
  blocking collectives  131 us (25%)
  local copies, waits for them, and re-layouts  96.6 us (18%)
  matrix products  14.9 us (3%)
  between operations  14.6 us (3%)
    all_gather x1, waiting for transfers between devices, local(): lax.all_gather(coefficients, 'aux', axis=0, tiled=True)  124 us
    all_to_all x1, blocking collectives, local(): lax.all_to_all(half, 'row', split_axis=2, concat_axis=1, tiled=True)  79.7 us
    reduce_scatter x1, waiting for transfers between devices, local(): summed = lax.psum_scatter(partial_k, 'row', scatter_dimension=0, tiled=True)  73.5 us
    unnamed x4, waiting for transfers between devices  61.6 us
    psum x1, blocking collectives, local(): norms = lax.psum(local_norms, 'aux')  51.2 us
    unnamed x9, local copies, waits for them, and re-layouts  30.3 us
    all_gather x1, local copies, waits for them, and re-layouts, local(): lax.all_gather(coefficients, 'aux', axis=0, tiled=True)  28 us
    convert_element_type x1, local copies, waits for them, and re-layouts, local(): half = half.astype(jnp.bfloat16)  15.7 us
  transfers between devices with their start and end apart: 3, of which 3 were waited for; matrix products, arithmetic and copies ran while one was open for 0% of the time, Pallas kernels for 0%

commit v1 on v0

v1 whole, which is shorter than its diff:
```python
import functools

import jax
import jax.numpy as jnp
from jax import lax
from jax.experimental import pallas as pl
from jax.experimental.pallas import tpu as pltpu
from jax.sharding import Mesh, PartitionSpec as P

ROW = ("y", "xh")
AUX = ("z", "xl", "c")


def pick_kernel(copies, width, col_ref, count_ref, coef_ref, out_ref):
    slots = col_ref.shape[0]
    for pair in range(slots // 2):
        halves = []
        for s in (2 * pair, 2 * pair + 1):
            tile = col_ref[s]
            start = pl.multiple_of((tile // 2) * (2 * width), 2 * width)
            both = coef_ref[:, pl.ds(start, 2 * width)].astype(jnp.float32)
            want = s % 2
            swapped = pltpu.roll(both, width, 1)
            keep = jnp.full(both.shape, tile % 2, jnp.int32) == want
            live = jnp.full(both.shape, s, jnp.int32) < count_ref[0]
            halves.append(jnp.where(live, jnp.where(keep, both, swapped), 0.0))
        lane = lax.broadcasted_iota(jnp.int32, halves[0].shape, 1)
        merged = jnp.where(lane < width, halves[0], halves[1]).astype(out_ref.dtype)
        for n in range(copies):
            out_ref[n, :, pair * 2 * width : (pair + 1) * 2 * width] = merged


def pick(coefficients, cols, count, copies, width):
    norb = coefficients.shape[0]
    slots = cols.shape[0]
    return pl.pallas_call(
        functools.partial(pick_kernel, copies, width),
        out_shape=jax.ShapeDtypeStruct((copies, norb, slots * width), coefficients.dtype),
        in_specs=[
            pl.BlockSpec(memory_space=pltpu.SMEM),
            pl.BlockSpec(memory_space=pltpu.SMEM),
            pl.BlockSpec(memory_space=pltpu.VMEM),
        ],
        out_specs=pl.BlockSpec(memory_space=pltpu.VMEM),
        name="pick",
    )(cols, count, coefficients)


def exchange_kernel(ncore, naux, core_ref, own_ref, other_ref, picked_ref, keep_ref, send_ref, half, total):
    t = pl.program_id(0)
    ntiles = pl.num_programs(0)
    _, nq, height, width = own_ref.shape
    norb = picked_ref.shape[0] * picked_ref.shape[2] * picked_ref.shape[3]
    picked = picked_ref[...].reshape(norb, width)
    start = pl.multiple_of(t * height, height)
    for block, ref in enumerate((own_ref, other_ref)):
        result = lax.dot_general(
            ref[...].reshape(nq * height, width),
            picked,
            (((1,), (1,)), ((), ())),
            preferred_element_type=jnp.float32,
        ).astype(jnp.bfloat16)
        for q in range(nq):
            col = (block * nq + q) * norb
            half[pl.ds(start, height), col : col + norb] = result[q * height : (q + 1) * height]

    @pl.when(t == ntiles - 1)
    def _():
        rows = total.shape[0]
        step = rows // 2
        for i in range(2):
            for j in range(2):
                total[i * step : (i + 1) * step, j * step : (j + 1) * step] = lax.dot_general(
                    half[i * step : (i + 1) * step, :],
                    half[j * step : (j + 1) * step, :],
                    (((1,), (1,)), ((), ())),
                    preferred_element_type=jnp.float32,
                )
        whole = total[...]
        on_diagonal = lax.broadcasted_iota(jnp.int32, whole.shape, 0) == lax.broadcasted_iota(
            jnp.int32, whole.shape, 1
        )
        diagonal = jnp.sum(jnp.where(on_diagonal, whole, 0.0), axis=0, keepdims=True)
        cols = rows // naux
        nrow = rows // height
        hc = cols // 2
        low = lax.broadcasted_iota(jnp.int32, (hc, 2 * height), 1) < height
        low1 = lax.broadcasted_iota(jnp.int32, (1, 2 * height), 1) < height
        per = hc + 1
        for which, out_ref in ((0, keep_ref), (1, send_ref)):
            core = core_ref[0] if which == 0 else 1 - core_ref[0]
            for a in range(naux // ncore):
                first = pl.multiple_of((a * ncore + core) * cols, cols)
                for pair in range(nrow // 2):
                    lanes = slice(pair * 2 * height, (pair + 1) * 2 * height)
                    top = total[pl.ds(first, hc), lanes]
                    bottom = total[pl.ds(pl.multiple_of(first + hc, hc), hc), lanes]
                    d = diagonal[:, lanes]
                    even = jnp.where(low, top, pltpu.roll(bottom, height, 1))
                    odd = jnp.where(low, pltpu.roll(top, height, 1), bottom)
                    base = (a * nrow + 2 * pair) * per
                    out_ref[base : base + hc, :] = even
                    out_ref[base + hc : base + per, :] = jnp.where(low1, d, 0.0)
                    out_ref[base + per : base + per + hc, :] = odd
                    out_ref[base + per + hc : base + 2 * per, :] = jnp.where(low1, pltpu.roll(d, height, 1), 0.0)


def exchange(core, own, other, picked, ncore, naux):
    ntiles, nq, height, width = own.shape
    nz, _, nxl, norb, _ = picked.shape
    rows = ntiles * height
    cols = rows // naux
    messages = (naux // ncore) * ntiles
    shape = jax.ShapeDtypeStruct((messages * (cols // 2 + 1), 2 * height), jnp.float32)
    all_orb = nz * nxl * norb
    return pl.pallas_call(
        functools.partial(exchange_kernel, ncore, naux),
        out_shape=(shape, shape),
        grid_spec=pltpu.PrefetchScalarGridSpec(
            num_scalar_prefetch=1,
            grid=(ntiles,),
            in_specs=[
                pl.BlockSpec((1, nq, height, width), lambda t, c: (t, 0, 0, 0)),
                pl.BlockSpec((1, nq, height, width), lambda t, c: (t, 0, 0, 0)),
                pl.BlockSpec((nz, 1, nxl, norb, width), lambda t, c: (0, t, 0, 0, 0)),
            ],
            out_specs=[pl.BlockSpec(shape.shape, lambda t, c: (0, 0))] * 2,
            scratch_shapes=[
                pltpu.VMEM((rows, 2 * nq * all_orb), jnp.bfloat16),
                pltpu.VMEM((rows, rows), jnp.float32),
            ],
        ),
        compiler_params=pltpu.CompilerParams(
            dimension_semantics=("arbitrary",), vmem_limit_bytes=56 * 1024 * 1024
        ),
        cost_estimate=pl.CostEstimate(
            flops=4 * nq * rows * all_orb * (width + rows), bytes_accessed=12 << 20, transcendentals=0
        ),
        name="exchange",
    )(core, own, other, picked)


def finish_kernel(scale_diagonal, scale_tiles, per, place_ref, got_ref, tiles_ref, diagonal_ref):
    messages = got_ref.shape[0] // per
    hc = per - 1
    cols, height = tiles_ref.shape
    total = got_ref[0:per, :]
    for n in range(1, messages):
        total = total + got_ref[n * per : (n + 1) * per, :]
    top = total[:hc]
    flat = jnp.concatenate([top, pltpu.roll(top, height, 1)], axis=0)[:, :height]
    n = place_ref[1] * cols + lax.broadcasted_iota(jnp.int32, flat.shape, 0)
    m = place_ref[0] * height + lax.broadcasted_iota(jnp.int32, flat.shape, 1)
    tiles_ref[...] = jnp.where(m == n, 0.0, flat) / scale_tiles
    diagonal_ref[...] = total[hc:per, :height] / scale_diagonal


def finish(got, place, height, cols, count):
    per = cols // 2 + 1
    return pl.pallas_call(
        functools.partial(finish_kernel, float(count), float(count) ** 0.5, per),
        out_shape=(
            jax.ShapeDtypeStruct((cols, height), jnp.float32),
            jax.ShapeDtypeStruct((1, height), jnp.float32),
        ),
        in_specs=[pl.BlockSpec(memory_space=pltpu.SMEM), pl.BlockSpec(memory_space=pltpu.VMEM)],
        out_specs=[pl.BlockSpec(memory_space=pltpu.VMEM)] * 2,
        name="finish",
    )(place, got)


def local(three_center, coefficients, col_tiles, tile_count):
    nq, _, height, width = three_center.shape
    nz, nxl, ncore = (lax.axis_size(a) for a in AUX)
    nrow = lax.axis_size("y") * lax.axis_size("xh")
    naux = nz * nxl * ncore
    norb = coefficients.shape[0]
    rows = nrow * height
    cols = rows // naux
    core = lax.axis_index("c")

    picks = pick(coefficients, col_tiles.reshape(-1), tile_count, nrow * nxl, height)
    picks = lax.all_to_all(picks, ROW + ("xl",), 0, 0, tiled=True)
    picked = lax.all_gather(picks, "z", axis=0, tiled=True)
    picked = picked.reshape(nz, nrow, nxl, norb, width)

    integrals = three_center.reshape(nq, height, width)
    integrals, picks = lax.optimization_barrier((integrals, picks))
    own = lax.all_to_all(integrals, ROW, 0, 0, tiled=True)
    own = own.reshape(nrow, nq // nrow, height, width)
    other = lax.ppermute(own, "c", [(0, 1), (1, 0)])

    keep, send = exchange(core.reshape(1), own, other, picked, ncore, naux)
    mine = keep + lax.ppermute(send, "c", [(0, 1), (1, 0)])
    got = lax.all_to_all(mine, ("z", "xl") + ROW, 0, 0, tiled=True)

    row = lax.axis_index(ROW)
    place = jnp.stack([row, lax.axis_index(AUX)]).astype(jnp.int32)
    tiles, diagonal = finish(got, place, height, cols, nq * naux * norb * naux)
    return tiles.T, diagonal.reshape(height)


def solution(mesh):
    fine = Mesh(mesh.devices.reshape(8, 2, 2, 4, 2), AUX + ROW)
    in_specs = (P(AUX, ROW, None, None), P(AUX, None), P(ROW, None), P(ROW))
    out_specs = (P(ROW, AUX), P(ROW))
    return jax.shard_map(local, mesh=fine, in_specs=in_specs, out_specs=out_specs, check_vma=False)
```

time: 525 us -> 153 us (0.29)
  waiting for transfers between devices: 259 us -> 45.3 us
  local copies, waits for them, and re-layouts: 96.6 us -> 1.92 us
  blocking collectives: 131 us -> 59.9 us
  Pallas kernels: 0 us -> 17.3 us
  matrix products: 14.9 us -> 0 us
  starting transfers between devices: 0.12 us -> 11.1 us
    all_gather x1, waiting for transfers between devices: 124 us -> 7.01 us  [local(): picked = lax.all_gather(picks, 'z', axis=0, tiled=True)]
    reduce_scatter x1 -> x0, waiting for transfers between devices: 73.5 us -> none  [local(): summed = lax.psum_scatter(partial_k, 'row', scatter_dimension=0, tiled=True)]
    unnamed x4 -> x1, waiting for transfers between devices: 61.6 us -> 0.02 us
    psum x1 -> x0, blocking collectives: 51.2 us -> none  [local(): norms = lax.psum(local_norms, 'aux')]
    unnamed x9 -> x2, local copies, waits for them, and re-layouts: 30.3 us -> 0.01 us
    all_to_all x0 -> x1, waiting for transfers between devices: none -> 30.3 us  [local(): got = lax.all_to_all(mine, ('z', 'xl') + ROW, 0, 0, tiled=True)]
    all_gather x1 -> x0, local copies, waits for them, and re-layouts: 28 us -> none  [local(): lax.all_gather(coefficients, 'aux', axis=0, tiled=True)]
    all_to_all x1 -> x2, blocking collectives: 79.7 us -> 59.9 us  [the longest x1 42.2 us: local(): own = lax.all_to_all(integrals, ROW, 0, 0, tiled=True)]
  transfers between devices with their start and end apart: 3 -> 4, of which waited for: 3 -> 4; matrix products, arithmetic and copies ran while one was open for 0% -> 0% of each run, Pallas kernels for 0% -> 0%
where the time goes in v1:
time: 153 us; the launch traced here: 152 us
  blocking collectives  59.9 us (39%)
  waiting for transfers between devices  45.3 us (30%)
  Pallas kernels  17.3 us (11%)
  between operations  14.7 us (10%)
  starting transfers between devices  11.1 us (7%)
  local copies, waits for them, and re-layouts  1.92 us (1%)
  other arithmetic  1.74 us (1%)
    all_to_all x1, blocking collectives, local(): own = lax.all_to_all(integrals, ROW, 0, 0, tiled=True)  42.2 us
    all_to_all x1, waiting for transfers between devices, local(): got = lax.all_to_all(mine, ('z', 'xl') + ROW, 0, 0, tiled=True)  30.3 us
    all_to_all x1, blocking collectives, local(): picks = lax.all_to_all(picks, ROW + ('xl',), 0, 0, tiled=True)  17.7 us
    pallas_call x1, Pallas kernels, exchange(): pl.pallas_call(functools.partial(exchange_kernel, ncore, naux), out_shape...  13.4 us
    all_to_all x1, starting transfers between devices, local(): got = lax.all_to_all(mine, ('z', 'xl') + ROW, 0, 0, tiled=True)  11.1 us
    all_gather x1, waiting for transfers between devices, local(): picked = lax.all_gather(picks, 'z', axis=0, tiled=True)  7.01 us
    ppermute x1, waiting for transfers between devices, local(): other = lax.ppermute(own, 'c', [(0, 1), (1, 0)])  5.79 us
  transfers between devices with their start and end apart: 4, of which 4 were waited for; matrix products, arithmetic and copies ran while one was open for 0% of the time, Pallas kernels for 0%

profile of v1, /device:TPU:2, one launch (start us, length us, event | category | flops | bytes accessed | tf_op | source)
XLA Modules:
  0.0 152.0 jit_solution(8788433523344809807)
XLA Ops:
  7.2 0.0 all-gather.2.cloned.1.call-start
  7.9 2.1 %pick.1 = bf16[16,32,512]{2,1,0:T(8,128)(2,1)} custom-call(s32[8]{0:T(128)} %bitcast.12, s32[1]{0:T(128)S(6)} %copy.6.count_ref, bf16[32,10240]{1,0:T(8,128)(2,1)} %coef_ref.1), custom_call_target="tpu_custom_call" | custom-call | tf_op jit(solution)/shard_map/pick/pallas_call | solution.py:36
  9.9 17.7 %all_to_all.21 = bf16[16,32,512]{2,1,0:T(8,128)(2,1)} all-to-all(bf16[16,32,512]{2,1,0:T(8,128)(2,1)} %pick.1), channel_id=1, replica_groups=mesh['z'=8,'xl'=2,'c'=2,'y'=4,'xh'=2] {'y','xh','xl'}, dimensions={0} | all-to-all | bytes 1048576 | tf_op jit(solution)/shard_map/all_to_all | solution.py:183
  27.7 0.0 all-gather.2.cloned.1.call-update
  27.7 42.2 %all_to_all.22 = bf16[48,64,512]{2,1,0:T(8,128)(2,1)S(1)} all-to-all(bf16[48,64,512]{2,1,0:T(8,128)(2,1)} %bitcast.9), channel_id=1, replica_groups=mesh['z'=8,'xl'=2,'c'=2,'y'=4,'xh'=2] {'y','xh'}, dimensions={0} | all-to-all | bytes 6291456 | tf_op jit(solution)/shard_map/all_to_all | solution.py:189
  69.8 0.0 copy-start
  69.9 0.0 collective-permute-start
  69.9 5.8 %collective-permute-done.other_ref = bf16[8,6,64,512]{3,2,1,0:T(8,128)(2,1)} collective-permute-done((bf16[8,6,64,512]{3,2,1,0:T(8,128)(2,1)S(1)}, bf16[8,6,64,512]{3,2,1,0:T(8,128)(2,1)}, u32[]{:S(2)}, u32[]{:S(2)}) %collective-permute-start) | collective-permute-done | bytes 3145760 | tf_op jit(solution)/shard_map/ppermute | solution.py:191
  75.6 7.0 %all-gather.2.cloned.1.call-done = bf16[128,32,512]{2,1,0:T(8,128)(2,1)} async-done(((bf16[16,32,512]{2,1,0:T(8,128)(2,1)}), bf16[128,32,512]{2,1,0:T(8,128)(2,1)}) %all-gather.2.cloned.1.call-update) | async-done | bytes 4194320 | tf_op jit(solution)/shard_map/all_gather | solution.py:184
  82.7 0.0 copy-done
  82.7 13.4 %exchange.1 = (f32[1152,128]{1,0:T(8,128)}, f32[1152,128]{1,0:T(8,128)}) custom-call(s32[1]{0:T(128)} %bitcast.2.core_ref, bf16[8,6,64,512]{3,2,1,0:T(8,128)(2,1)} %bitcast.11, bf16[8,6,64,512]{3,2,1,0:T(8,128)(2,1)} %collective-permute-done.other_ref, bf16[8,8,2,32,512]{4,3,2,1,0:T(8,128)(2,1)} %bitcast.13), custom_call_target="tpu_custom_call" | custom-call | flops 6442450944 | bytes 12582912 | tf_op jit(solution)/shard_map/exchange/pallas_call | solution.py:116
  96.0 0.0 collective-permute-start.1
  96.0 2.2 %collective-permute-done.1 = f32[1152,128]{1,0:T(8,128)S(1)} collective-permute-done((f32[1152,128]{1,0:T(8,128)}, f32[1152,128]{1,0:T(8,128)S(1)}, u32[]{:S(2)}, u32[]{:S(2)}) %collective-permute-start.1) | collective-permute-done | bytes 589856 | tf_op jit(solution)/shard_map/ppermute | solution.py:194
  98.2 1.1 add.15
  99.3 1.0 all_to_all.15
  100.4 11.1 %all-to-all-start.2 = ((f32[128,9,128]{2,1,0:T(8,128)}), f32[128,9,128]{2,1,0:T(8,128)S(1)}, u32[]{:S(2)}, u32[]{:S(2)}) async-start(f32[128,9,128]{2,1,0:T(8,128)} %all_to_all.15), calls=%async_computation.2 | async-start | bytes 2097152 | tf_op jit(solution)/shard_map/all_to_all | solution.py:195
  111.5 0.6 pad_add_fusion.place_ref
  112.1 30.3 %all-to-all-done.2 = f32[128,9,128]{2,1,0:T(8,128)S(1)} async-done(((f32[128,9,128]{2,1,0:T(8,128)}), f32[128,9,128]{2,1,0:T(8,128)S(1)}, u32[]{:S(2)}, u32[]{:S(2)}) %all-to-all-start.2) | async-done | bytes 589856 | tf_op jit(solution)/shard_map/all_to_all | solution.py:195
  142.4 0.9 all_to_all.17.got_ref
  143.3 1.9 %finish.1 = (f32[16,64]{1,0:T(8,128)}, f32[1,64]{1,0:T(1,128)}) custom-call(s32[2]{0:T(128)} %pad_add_fusion.place_ref, f32[1152,128]{1,0:T(8,128)} %all_to_all.17.got_ref), custom_call_target="tpu_custom_call" | custom-call | tf_op jit(solution)/shard_map/finish/pallas_call | solution.py:160
Async XLA Ops:
  7.2 75.5 %all-gather.2.cloned.1.call-start = ((), (), s32[]{:S(2)}) async-start(), calls=%async_computation.3 | async-start | bytes 4718592 | tf_op jit(solution)/shard_map/all_gather | solution.py:184
  69.8 12.8 %copy-start = (bf16[48,64,512]{2,1,0:T(8,128)(2,1)}, bf16[48,64,512]{2,1,0:T(8,128)(2,1)S(1)}, u32[]{:S(2)}) copy-start(bf16[48,64,512]{2,1,0:T(8,128)(2,1)S(1)} %all_to_all.22) | copy-start | bytes 9437188
  69.9 5.8 %collective-permute-start = (bf16[8,6,64,512]{3,2,1,0:T(8,128)(2,1)S(1)}, bf16[8,6,64,512]{3,2,1,0:T(8,128)(2,1)}, u32[]{:S(2)}, u32[]{:S(2)}) collective-permute-start(bf16[8,6,64,512]{3,2,1,0:T(8,128)(2,1)S(1)} %bitcast.10), channel_id=1, source_target_pairs={{0,8},{8,0},{1,9},{9,1},{2,10},{10,2},{3,11},{11,3},{4,12},{12,4},... | collective-permute-start | bytes 9437192 | tf_op jit(solution)/shard_map/ppermute | solution.py:191
  96.0 2.2 %collective-permute-start.1 = (f32[1152,128]{1,0:T(8,128)}, f32[1152,128]{1,0:T(8,128)S(1)}, u32[]{:S(2)}, u32[]{:S(2)}) collective-permute-start(f32[1152,128]{1,0:T(8,128)} %get-tuple-element.9), channel_id=1, source_target_pairs={{0,8},{8,0},{1,9},{9,1},{2,10},{10,2},{3,11},{11,3},{4,12},{12,4},... | collective-permute-start | bytes 1769480 | tf_op jit(solution)/shard_map/ppermute | solution.py:194
  100.4 42.0 %all-to-all-start.2 = ((f32[128,9,128]{2,1,0:T(8,128)}), f32[128,9,128]{2,1,0:T(8,128)S(1)}, u32[]{:S(2)}, u32[]{:S(2)}) async-start(f32[128,9,128]{2,1,0:T(8,128)} %all_to_all.15), calls=%async_computation.2 | async-start | bytes 2097152 | tf_op jit(solution)/shard_map/all_to_all | solution.py:195
Sparse Core Ops, SparseCore 0:
  27.8 54.7 all-gather.1

commit v2 on v1

v2 whole, which is shorter than its diff:
```python
import functools

import jax
import jax.numpy as jnp
from jax import lax
from jax.experimental import pallas as pl
from jax.experimental.pallas import tpu as pltpu
from jax.sharding import Mesh, PartitionSpec as P

ROW = ("y", "xh")
AUX = ("z", "xl", "c")


def pick_kernel(copies, width, col_ref, count_ref, coef_ref, out_ref):
    slots = col_ref.shape[0]
    for pair in range(slots // 2):
        halves = []
        for s in (2 * pair, 2 * pair + 1):
            tile = col_ref[s]
            start = pl.multiple_of((tile // 2) * (2 * width), 2 * width)
            both = coef_ref[:, pl.ds(start, 2 * width)].astype(jnp.float32)
            want = s % 2
            swapped = pltpu.roll(both, width, 1)
            keep = jnp.full(both.shape, tile % 2, jnp.int32) == want
            live = jnp.full(both.shape, s, jnp.int32) < count_ref[0]
            halves.append(jnp.where(live, jnp.where(keep, both, swapped), 0.0))
        lane = lax.broadcasted_iota(jnp.int32, halves[0].shape, 1)
        merged = jnp.where(lane < width, halves[0], halves[1]).astype(out_ref.dtype)
        for n in range(copies):
            out_ref[n, :, pair * 2 * width : (pair + 1) * 2 * width] = merged


def pick(coefficients, cols, count, copies, width):
    norb = coefficients.shape[0]
    slots = cols.shape[0]
    return pl.pallas_call(
        functools.partial(pick_kernel, copies, width),
        out_shape=jax.ShapeDtypeStruct((copies, norb, slots * width), coefficients.dtype),
        in_specs=[
            pl.BlockSpec(memory_space=pltpu.SMEM),
            pl.BlockSpec(memory_space=pltpu.SMEM),
            pl.BlockSpec(memory_space=pltpu.VMEM),
        ],
        out_specs=pl.BlockSpec(memory_space=pltpu.VMEM),
        name="pick",
    )(cols, count, coefficients)


def gather_half(own_ref, other_ref, blocks, held, sem, half):
    ntiles, nq, height, width = own_ref.shape
    norb = len(blocks) * blocks[0].shape[1]
    copies = [pltpu.make_async_copy(ref, held.at[n], sem.at[n]) for n, ref in enumerate(blocks)]
    for copy in copies:
        copy.start()
    for copy in copies:
        copy.wait()

    def tile(t, _):
        picked = held[:, t].reshape(norb, width)
        start = pl.multiple_of(t * height, height)
        for block, ref in enumerate((own_ref, other_ref)):
            result = lax.dot_general(
                ref[t].reshape(nq * height, width),
                picked,
                (((1,), (1,)), ((), ())),
                preferred_element_type=jnp.float32,
            ).astype(jnp.bfloat16)
            for q in range(nq):
                col = (block * nq + q) * norb
                half[pl.ds(start, height), col : col + norb] = result[q * height : (q + 1) * height]
        return 0

    lax.fori_loop(0, ntiles, tile, 0)


def product(half, i, j, step):
    return lax.dot_general(
        half[i * step : (i + 1) * step, :],
        half[j * step : (j + 1) * step, :],
        (((1,), (1,)), ((), ())),
        preferred_element_type=jnp.float32,
    )


def early_kernel(own_ref, other_ref, *refs):
    *blocks, total_ref, held, sem, half = refs
    gather_half(own_ref, other_ref, blocks, held, sem, half)
    step = total_ref.shape[0] // 2
    for i, j in ((0, 0), (1, 1), (1, 0)):
        total_ref[i * step : (i + 1) * step, j * step : (j + 1) * step] = product(half, i, j, step)


def late_kernel(ncore, naux, core_ref, own_ref, other_ref, early_ref, *refs):
    *blocks, keep_ref, send_ref, held, sem, half, total = refs
    gather_half(own_ref, other_ref, blocks, held, sem, half)
    rows = total.shape[0]
    height = own_ref.shape[2]
    step = rows // 2
    for i, j in ((0, 0), (1, 1), (1, 0)):
        rest = early_ref[i * step : (i + 1) * step, j * step : (j + 1) * step]
        block = product(half, i, j, step) + rest
        total[i * step : (i + 1) * step, j * step : (j + 1) * step] = block
        if i != j:
            total[j * step : (j + 1) * step, i * step : (i + 1) * step] = block.T
    whole = total[...]
    on_diagonal = lax.broadcasted_iota(jnp.int32, whole.shape, 0) == lax.broadcasted_iota(
        jnp.int32, whole.shape, 1
    )
    diagonal = jnp.sum(jnp.where(on_diagonal, whole, 0.0), axis=0, keepdims=True)
    cols = rows // naux
    nrow = rows // height
    hc = cols // 2
    low = lax.broadcasted_iota(jnp.int32, (hc, 2 * height), 1) < height
    low1 = lax.broadcasted_iota(jnp.int32, (1, 2 * height), 1) < height
    per = hc + 1
    for which, out_ref in ((0, keep_ref), (1, send_ref)):
        core = core_ref[0] if which == 0 else 1 - core_ref[0]
        for a in range(naux // ncore):
            first = pl.multiple_of((a * ncore + core) * cols, cols)
            for pair in range(nrow // 2):
                lanes = slice(pair * 2 * height, (pair + 1) * 2 * height)
                top = total[pl.ds(first, hc), lanes]
                bottom = total[pl.ds(pl.multiple_of(first + hc, hc), hc), lanes]
                d = diagonal[:, lanes]
                even = jnp.where(low, top, pltpu.roll(bottom, height, 1))
                odd = jnp.where(low, pltpu.roll(top, height, 1), bottom)
                base = (a * nrow + 2 * pair) * per
                out_ref[base : base + hc, :] = even
                out_ref[base + hc : base + per, :] = jnp.where(low1, d, 0.0)
                out_ref[base + per : base + per + hc, :] = odd
                out_ref[base + per + hc : base + 2 * per, :] = jnp.where(low1, pltpu.roll(d, height, 1), 0.0)


def exchange(core, own, other, early, late, ncore, naux):
    ntiles, nq, height, width = own.shape
    norb = early[0].shape[1]
    rows = ntiles * height
    cols = rows // naux
    messages = (naux // ncore) * ntiles
    whole = pl.BlockSpec(memory_space=pltpu.VMEM)
    params = pltpu.CompilerParams(vmem_limit_bytes=32 * 1024 * 1024)
    own, other = (pltpu.with_memory_space_constraint(x, pltpu.VMEM) for x in (own, other))

    def cost(n):
        orb = n * norb
        return pl.CostEstimate(flops=4 * nq * rows * orb * (width + rows), bytes_accessed=1 << 20, transcendentals=0)

    def scratch(n):
        return [
            pltpu.VMEM((n, ntiles, norb, width), jnp.bfloat16),
            pltpu.SemaphoreType.DMA((n,)),
            pltpu.VMEM((rows, 2 * nq * n * norb), jnp.bfloat16),
        ]

    total = pl.pallas_call(
        early_kernel,
        out_shape=jax.ShapeDtypeStruct((rows, rows), jnp.float32),
        in_specs=[whole] * 2 + [pl.BlockSpec(memory_space=pl.ANY)] * len(early),
        out_specs=whole,
        scratch_shapes=scratch(len(early)),
        compiler_params=params,
        cost_estimate=cost(len(early)),
        name="early",
    )(own, other, *early)
    shape = jax.ShapeDtypeStruct((messages * (cols // 2 + 1), 2 * height), jnp.float32)
    return pl.pallas_call(
        functools.partial(late_kernel, ncore, naux),
        out_shape=(shape, shape),
        in_specs=[pl.BlockSpec(memory_space=pltpu.SMEM)] + [whole] * 3 + [pl.BlockSpec(memory_space=pl.ANY)] * len(late),
        out_specs=[whole] * 2,
        scratch_shapes=scratch(len(late)) + [pltpu.VMEM((rows, rows), jnp.float32)],
        compiler_params=params,
        cost_estimate=cost(len(late)),
        name="late",
    )(core, own, other, total, *late)


def ring(chunks, axis, size, beside, when):
    up = [(i, (i + 1) % size) for i in range(size)]
    down = [(i, (i - 1) % size) for i in range(size)]
    rights, lefts, got = list(chunks), list(chunks), []
    for step in range(1, size // 2 + 1):
        last = step == size // 2
        if step == when:
            rights, lefts, beside = lax.optimization_barrier((rights, lefts, beside))
        for n in range(len(chunks)):
            if not last or n % 2 == 0:
                rights[n] = lax.ppermute(rights[n], axis, up)
                got.append(rights[n])
            if not last or n % 2 == 1:
                lefts[n] = lax.ppermute(lefts[n], axis, down)
                got.append(lefts[n])
    return got, beside


def finish_kernel(scale_diagonal, scale_tiles, per, place_ref, got_ref, tiles_ref, diagonal_ref):
    messages = got_ref.shape[0] // per
    hc = per - 1
    cols, height = tiles_ref.shape
    total = got_ref[0:per, :]
    for n in range(1, messages):
        total = total + got_ref[n * per : (n + 1) * per, :]
    top = total[:hc]
    flat = jnp.concatenate([top, pltpu.roll(top, height, 1)], axis=0)[:, :height]
    n = place_ref[1] * cols + lax.broadcasted_iota(jnp.int32, flat.shape, 0)
    m = place_ref[0] * height + lax.broadcasted_iota(jnp.int32, flat.shape, 1)
    tiles_ref[...] = jnp.where(m == n, 0.0, flat) / scale_tiles
    diagonal_ref[...] = total[hc:per, :height] / scale_diagonal


def finish(got, place, height, cols, count):
    per = cols // 2 + 1
    return pl.pallas_call(
        functools.partial(finish_kernel, float(count), float(count) ** 0.5, per),
        out_shape=(
            jax.ShapeDtypeStruct((cols, height), jnp.float32),
            jax.ShapeDtypeStruct((1, height), jnp.float32),
        ),
        in_specs=[pl.BlockSpec(memory_space=pltpu.SMEM), pl.BlockSpec(memory_space=pltpu.VMEM)],
        out_specs=[pl.BlockSpec(memory_space=pltpu.VMEM)] * 2,
        name="finish",
    )(place, got)


def local(three_center, coefficients, col_tiles, tile_count):
    nq, _, height, width = three_center.shape
    nz, nxl, ncore = (lax.axis_size(a) for a in AUX)
    nrow = lax.axis_size("y") * lax.axis_size("xh")
    naux = nz * nxl * ncore
    norb = coefficients.shape[0]
    rows = nrow * height
    cols = rows // naux
    core = lax.axis_index("c")

    picks = pick(coefficients, col_tiles.reshape(-1), tile_count, nrow * nxl, height)
    integrals = three_center.reshape(nq, height, width)
    picks = lax.all_to_all(picks, ("xl",) + ROW, 0, 0, tiled=True)
    chunks = [picks[n * nrow : (n + 1) * nrow] for n in range(nxl)]
    own = lax.all_to_all(integrals, ROW, 0, 0, tiled=True)
    arrived, own = ring(chunks, "z", nz, own, 4)
    blocks = chunks + arrived
    own = own.reshape(nrow, nq // nrow, height, width)
    other = lax.ppermute(own, "c", [(0, 1), (1, 0)])

    early = len(blocks) // 2
    blocks = [pltpu.with_memory_space_constraint(b, pltpu.HBM) for b in blocks]
    keep, send = exchange(core.reshape(1), own, other, blocks[:early], blocks[early:], ncore, naux)
    mine = keep + lax.ppermute(send, "c", [(0, 1), (1, 0)])
    mine = mine.reshape(mine.shape[0], 1, mine.shape[1])
    got = lax.all_to_all(mine, ("z", "xl") + ROW, 0, 0, tiled=True)
    got = pltpu.with_memory_space_constraint(got.reshape(got.shape[0], got.shape[2]), pltpu.VMEM)

    row = lax.axis_index(ROW)
    place = jnp.stack([row, lax.axis_index(AUX)]).astype(jnp.int32)
    tiles, diagonal = finish(got, place, height, cols, nq * naux * norb * naux)
    return tiles.T, diagonal.reshape(height)


def solution(mesh):
    fine = Mesh(mesh.devices.reshape(8, 2, 2, 4, 2), AUX + ROW)
    in_specs = (P(AUX, ROW, None, None), P(AUX, None), P(ROW, None), P(ROW))
    out_specs = (P(ROW, AUX), P(ROW))
    return jax.shard_map(local, mesh=fine, in_specs=in_specs, out_specs=out_specs, check_vma=False)
```

time: 153 us -> 128 us (0.84)
  blocking collectives: 59.9 us -> 17.3 us
  starting transfers between devices: 11.1 us -> 39.6 us
  between operations: 14.7 us -> 1.51 us
  Pallas kernels: 17.3 us -> 20.2 us
    all_to_all x2 -> x1, blocking collectives: 59.9 us -> 17.3 us  [local(): picks = lax.all_to_all(picks, ('xl',) + ROW, 0, 0, tiled=True)]
    ppermute x0 -> x14, starting transfers between devices: none -> 24.3 us  [the longest x7 24.2 us: ring(): lefts[n] = lax.ppermute(lefts[n], axis, down)]
    ppermute x0 -> x14, waiting for transfers between devices: none -> 20.3 us  [the longest x7 16.8 us: ring(): rights[n] = lax.ppermute(rights[n], axis, up)]
    all_to_all x1, waiting for transfers between devices: 30.3 us -> 20.6 us  [local(): got = lax.all_to_all(mine, ('z', 'xl') + ROW, 0, 0, tiled=True)]
    all_gather x1 -> x0, waiting for transfers between devices: 7.01 us -> none  [local(): picked = lax.all_gather(picks, 'z', axis=0, tiled=True)]
    all_to_all x0 -> x1, starting transfers between devices: none -> 3.7 us  [local(): own = lax.all_to_all(integrals, ROW, 0, 0, tiled=True)]
    pallas_call x1 -> x2, Pallas kernels: 13.4 us -> 16.7 us  [the longest x1 8.56 us: exchange(): pl.pallas_call(functools.partial(late_kernel, ncore, naux), out_shape=(sh...]
    ppermute x1, waiting for transfers between devices: 5.79 us -> 2.46 us  [local(): other = lax.ppermute(own, 'c', [(0, 1), (1, 0)])]
  transfers between devices with their start and end apart: 4 -> 18, of which waited for: 4 -> 9; matrix products, arithmetic and copies ran while one was open for 0% -> 1% of each run, Pallas kernels for 0% -> 6%
where the time goes in v2:
time: 128 us
  waiting for transfers between devices  45.2 us (35%)
  starting transfers between devices  39.6 us (31%)
  Pallas kernels  20.2 us (16%)
  blocking collectives  17.3 us (14%)
  local copies, waits for them, and re-layouts  2.6 us (2%)
  between operations  1.51 us (1%)
  other arithmetic  1.48 us (1%)
    ppermute x7, starting transfers between devices, ring(): lefts[n] = lax.ppermute(lefts[n], axis, down)  24.2 us
    all_to_all x1, waiting for transfers between devices, local(): got = lax.all_to_all(mine, ('z', 'xl') + ROW, 0, 0, tiled=True)  20.6 us
    all_to_all x1, blocking collectives, local(): picks = lax.all_to_all(picks, ('xl',) + ROW, 0, 0, tiled=True)  17.3 us
    ppermute x7, waiting for transfers between devices, ring(): rights[n] = lax.ppermute(rights[n], axis, up)  16.8 us
    all_to_all x1, starting transfers between devices, local(): got = lax.all_to_all(mine, ('z', 'xl') + ROW, 0, 0, tiled=True)  11.4 us
    pallas_call x1, Pallas kernels, exchange(): pl.pallas_call(functools.partial(late_kernel, ncore, naux), out_shape=(sh...  8.56 us
    pallas_call x1, Pallas kernels, exchange(): pl.pallas_call(early_kernel, out_shape=jax.ShapeDtypeStruct((rows, rows),...  8.12 us
    all_to_all x1, starting transfers between devices, local(): own = lax.all_to_all(integrals, ROW, 0, 0, tiled=True)  3.7 us
  transfers between devices with their start and end apart: 18, of which 9 were waited for; matrix products, arithmetic and copies ran while one was open for 1% of the time, Pallas kernels for 6%

profile of v2, /device:TPU:2, one launch (start us, length us, event | category | flops | bytes accessed | tf_op | source)
XLA Modules:
  0.0 127.9 jit_solution(4365312596786312926)
XLA Ops:
  1.3 2.1 %pick.1 = bf16[16,32,512]{2,1,0:T(8,128)(2,1)} custom-call(s32[8]{0:T(128)} %bitcast.17, s32[1]{0:T(128)S(6)} %copy.7.count_ref, bf16[32,10240]{1,0:T(8,128)(2,1)} %coef_ref.1), custom_call_target="tpu_custom_call" | custom-call | tf_op jit(solution)/shard_map/pick/pallas_call | solution.py:36
  3.3 17.3 %all_to_all.15 = bf16[16,32,512]{2,1,0:T(8,128)(2,1)} all-to-all(bf16[16,32,512]{2,1,0:T(8,128)(2,1)} %pick.1), channel_id=1, replica_groups=mesh['z'=8,'xl'=2,'c'=2,'y'=4,'xh'=2] {'xl','y','xh'}, dimensions={0} | all-to-all | bytes 1048576 | tf_op jit(solution)/shard_map/all_to_all | solution.py:237
  20.6 3.7 %all-to-all-start.1 = ((bf16[48,64,512]{2,1,0:T(8,128)(2,1)}), bf16[48,64,512]{2,1,0:T(8,128)(2,1)S(1)}, u32[]{:S(2)}, u32[]{:S(2)}) async-start(bf16[48,64,512]{2,1,0:T(8,128)(2,1)} %bitcast.16), calls=%async_computation.1 | async-start | bytes 6291456 | tf_op jit(solution)/shard_map/all_to_all | solution.py:239
  24.3 1.1 fusion
  25.4 5.9 %collective-permute-start.9 = (bf16[8,32,512]{2,1,0:T(8,128)(2,1)S(1)}, bf16[8,32,512]{2,1,0:T(8,128)(2,1)S(1)}, u32[]{:S(2)}, u32[]{:S(2)}) collective-permute-start(bf16[8,32,512]{2,1,0:T(8,128)(2,1)S(1)} %get-tuple-element.16.refs_1_), channel_id=1, source_target_pairs={{0,224},{32,0},{64,32},{96,64},{128,96},{160,128},{192,160},{224,1... | collective-permute-start | bytes 786440 | tf_op jit(solution)/shard_map/ppermute | solution.py:191
  31.3 0.0 collective-permute-start
  31.4 3.3 %collective-permute-start.6 = (bf16[8,32,512]{2,1,0:T(8,128)(2,1)S(1)}, bf16[8,32,512]{2,1,0:T(8,128)(2,1)S(1)}, u32[]{:S(2)}, u32[]{:S(2)}) collective-permute-start(bf16[8,32,512]{2,1,0:T(8,128)(2,1)S(1)} %get-tuple-element.17.refs_0_), channel_id=1, source_target_pairs={{0,224},{32,0},{64,32},{96,64},{128,96},{160,128},{192,160},{224,1... | collective-permute-start | bytes 786440 | tf_op jit(solution)/shard_map/ppermute | solution.py:191
  34.6 3.5 %collective-permute-done.9.refs_5_ = bf16[8,32,512]{2,1,0:T(8,128)(2,1)S(1)} collective-permute-done((bf16[8,32,512]{2,1,0:T(8,128)(2,1)S(1)}, bf16[8,32,512]{2,1,0:T(8,128)(2,1)S(1)}, u32[]{:S(2)}, u32[]{:S(2)}) %collective-permute-start.9) | collective-permute-done | bytes 262176 | tf_op jit(solution)/shard_map/ppermute | solution.py:191
  38.1 3.7 %collective-permute-start.10 = (bf16[8,32,512]{2,1,0:T(8,128)(2,1)S(1)}, bf16[8,32,512]{2,1,0:T(8,128)(2,1)S(1)}, u32[]{:S(2)}, u32[]{:S(2)}) collective-permute-start(bf16[8,32,512]{2,1,0:T(8,128)(2,1)S(1)} %collective-permute-done.9.refs_5_), channel_id=1, source_target_pairs={{0,224},{32,0},{64,32},{96,64},{128,96},{160,128},{192,160},{224,1... | collective-permute-start | bytes 786440 | tf_op jit(solution)/shard_map/ppermute | solution.py:191
  41.8 5.6 %collective-permute-done.3.refs_4_ = bf16[8,32,512]{2,1,0:T(8,128)(2,1)S(1)} collective-permute-done((bf16[8,32,512]{2,1,0:T(8,128)(2,1)S(1)}, bf16[8,32,512]{2,1,0:T(8,128)(2,1)S(1)}, u32[]{:S(2)}, u32[]{:S(2)}) %collective-permute-start.3) | collective-permute-done | bytes 262176 | tf_op jit(solution)/shard_map/ppermute | solution.py:188
  47.4 3.2 %collective-permute-start.7 = (bf16[8,32,512]{2,1,0:T(8,128)(2,1)S(1)}, bf16[8,32,512]{2,1,0:T(8,128)(2,1)S(1)}, u32[]{:S(2)}, u32[]{:S(2)}) collective-permute-start(bf16[8,32,512]{2,1,0:T(8,128)(2,1)S(1)} %collective-permute-done.6.refs_3_), channel_id=1, source_target_pairs={{0,224},{32,0},{64,32},{96,64},{128,96},{160,128},{192,160},{224,1... | collective-permute-start | bytes 786440 | tf_op jit(solution)/shard_map/ppermute | solution.py:191
  50.7 1.6 %collective-permute-start.11 = (bf16[8,32,512]{2,1,0:T(8,128)(2,1)S(1)}, bf16[8,32,512]{2,1,0:T(8,128)(2,1)S(1)}, u32[]{:S(2)}, u32[]{:S(2)}) collective-permute-start(bf16[8,32,512]{2,1,0:T(8,128)(2,1)S(1)} %collective-permute-done.10.refs_1_), channel_id=1, source_target_pairs={{0,224},{32,0},{64,32},{96,64},{128,96},{160,128},{192,160},{224,1... | collective-permute-start | bytes 786440 | tf_op jit(solution)/shard_map/ppermute | solution.py:191
  52.3 0.8 collective-permute-done.1.refs_6_
  53.0 5.6 %collective-permute-done.4.refs_0_ = bf16[8,32,512]{2,1,0:T(8,128)(2,1)S(1)} collective-permute-done((bf16[8,32,512]{2,1,0:T(8,128)(2,1)S(1)}, bf16[8,32,512]{2,1,0:T(8,128)(2,1)S(1)}, u32[]{:S(2)}, u32[]{:S(2)}) %collective-permute-start.4) | collective-permute-done | bytes 262176 | tf_op jit(solution)/shard_map/ppermute | solution.py:188
  58.7 3.2 %collective-permute-start.8 = (bf16[8,32,512]{2,1,0:T(8,128)(2,1)S(1)}, bf16[8,32,512]{2,1,0:T(8,128)(2,1)}, u32[]{:S(2)}, u32[]{:S(2)}) collective-permute-start(bf16[8,32,512]{2,1,0:T(8,128)(2,1)S(1)} %collective-permute-done.7.refs_7_), channel_id=1, source_target_pairs={{0,224},{32,0},{64,32},{96,64},{128,96},{160,128},{192,160},{224,1... | collective-permute-start | bytes 786440 | tf_op jit(solution)/shard_map/ppermute | solution.py:191
  61.9 2.0 %collective-permute-done.2.refs_2_ = bf16[8,32,512]{2,1,0:T(8,128)(2,1)S(1)} collective-permute-done((bf16[8,32,512]{2,1,0:T(8,128)(2,1)S(1)}, bf16[8,32,512]{2,1,0:T(8,128)(2,1)S(1)}, u32[]{:S(2)}, u32[]{:S(2)}) %collective-permute-start.2) | collective-permute-done | bytes 262176 | tf_op jit(solution)/shard_map/ppermute | solution.py:188
  63.9 2.8 %collective-permute-done.5.refs_4_ = bf16[8,32,512]{2,1,0:T(8,128)(2,1)S(1)} collective-permute-done((bf16[8,32,512]{2,1,0:T(8,128)(2,1)S(1)}, bf16[8,32,512]{2,1,0:T(8,128)(2,1)S(1)}, u32[]{:S(2)}, u32[]{:S(2)}) %collective-permute-start.5) | collective-permute-done | bytes 262176 | tf_op jit(solution)/shard_map/ppermute | solution.py:188
  66.8 0.7 copy-done.12
  67.5 0.1 collective-permute-start.13
  67.6 3.2 %collective-permute-start.14 = (bf16[8,32,512]{2,1,0:T(8,128)(2,1)}, bf16[8,32,512]{2,1,0:T(8,128)(2,1)S(1)}, u32[]{:S(2)}, u32[]{:S(2)}) collective-permute-start(bf16[8,32,512]{2,1,0:T(8,128)(2,1)} %copy-done.9), channel_id=1, source_target_pairs={{0,224},{32,0},{64,32},{96,64},{128,96},{160,128},{192,160},{224,1... | collective-permute-start | bytes 786440 | tf_op jit(solution)/shard_map/ppermute | solution.py:191
  70.9 2.5 %collective-permute-done.12.other_ref = bf16[8,6,64,512]{3,2,1,0:T(8,128)(2,1)} collective-permute-done((bf16[8,6,64,512]{3,2,1,0:T(8,128)(2,1)S(1)}, bf16[8,6,64,512]{3,2,1,0:T(8,128)(2,1)}, u32[]{:S(2)}, u32[]{:S(2)}) %collective-permute-start.12) | collective-permute-done | bytes 3145760 | tf_op jit(solution)/shard_map/ppermute | solution.py:243
  73.3 8.1 %early.1.early_ref = f32[512,512]{1,0:T(8,128)S(1)} custom-call(bf16[8,6,64,512]{3,2,1,0:T(8,128)(2,1)S(1)} %bitcast.13, bf16[8,6,64,512]{3,2,1,0:T(8,128)(2,1)} %collective-permute-done.12.other_ref, bf16[8,32,512]{2,1,0:T(8,128)(2,1)} %copy-done.1, bf16[8,32,512]{2,1,0:T(8,128)(2,1)} %copy-done, bf16[8,32,512]{2,1,0:T(8,128)(2,1)} %copy-done.3, ...), custom_call_target="tpu_custom_call" | custom-call | flops 3221225472 | bytes 1048576 | tf_op jit(solution)/shard_map/early/pallas_call | solution.py:155
  81.5 0.7 copy-done.13
  82.2 0.1 copy-done.14
  82.3 8.6 %late.1 = (f32[1152,128]{1,0:T(8,128)S(1)}, f32[1152,128]{1,0:T(8,128)S(1)}) custom-call(s32[1]{0:T(128)} %bitcast.2.core_ref, bf16[8,6,64,512]{3,2,1,0:T(8,128)(2,1)S(1)} %bitcast.14, bf16[8,6,64,512]{3,2,1,0:T(8,128)(2,1)} %collective-permute-done.12.other_ref, f32[512,512]{1,0:T(8,128)S(1)} %early.1.early_ref, bf16[8,32,512]{2,1,0:T(8,128)(2,1)} %copy-done.7, ...), custom_call_target="tpu_custom_call" | custom-call | flops 3221225472 | bytes 1048576 | tf_op jit(solution)/shard_map/late/pallas_call | solution.py:166
  90.8 0.2 collective-permute-start.15
  91.1 1.9 %collective-permute-done.15 = f32[1152,128]{1,0:T(8,128)S(1)} collective-permute-done((f32[1152,128]{1,0:T(8,128)S(1)}, f32[1152,128]{1,0:T(8,128)S(1)}, u32[]{:S(2)}, u32[]{:S(2)}) %collective-permute-start.15) | collective-permute-done | bytes 589856 | tf_op jit(solution)/shard_map/ppermute | solution.py:248
  92.9 0.9 add.15
  93.8 11.4 %all-to-all-start.2 = ((f32[1152,1,128]{2,1,0:T(1,128)}), f32[1152,1,128]{2,1,0:T(1,128)S(1)}, u32[]{:S(2)}, u32[]{:S(2)}) async-start(f32[1152,1,128]{2,1,0:T(1,128)} %bitcast.7), calls=%async_computation.2 | async-start | bytes 1179648 | tf_op jit(solution)/shard_map/all_to_all | solution.py:250
  105.2 0.6 pad_add_fusion.place_ref
  105.8 20.6 %all-to-all-done.2 = f32[1152,1,128]{2,1,0:T(1,128)S(1)} async-done(((f32[1152,1,128]{2,1,0:T(1,128)}), f32[1152,1,128]{2,1,0:T(1,128)S(1)}, u32[]{:S(2)}, u32[]{:S(2)}) %all-to-all-start.2) | async-done | bytes 589856 | tf_op jit(solution)/shard_map/all_to_all | solution.py:250
  126.4 1.5 %finish.1 = (f32[16,64]{1,0:T(8,128)}, f32[1,64]{1,0:T(1,128)}) custom-call(s32[2]{0:T(128)} %pad_add_fusion.place_ref, f32[1152,128]{1,0:T(8,128)S(1)} %bitcast.15), custom_call_target="tpu_custom_call" | custom-call | tf_op jit(solution)/shard_map/finish/pallas_call | solution.py:213
  (42 shorter events, 0.1 us)
Async XLA Ops:
  20.6 46.9 %all-to-all-start.1 = ((bf16[48,64,512]{2,1,0:T(8,128)(2,1)}), bf16[48,64,512]{2,1,0:T(8,128)(2,1)S(1)}, u32[]{:S(2)}, u32[]{:S(2)}) async-start(bf16[48,64,512]{2,1,0:T(8,128)(2,1)} %bitcast.16), calls=%async_computation.1 | async-start | bytes 6291456 | tf_op jit(solution)/shard_map/all_to_all | solution.py:239
  25.4 41.3 %copy-start.1 = (bf16[8,32,512]{2,1,0:T(8,128)(2,1)}, bf16[8,32,512]{2,1,0:T(8,128)(2,1)S(1)}, u32[]{:S(2)}) copy-start(bf16[8,32,512]{2,1,0:T(8,128)(2,1)S(1)} %get-tuple-element.17.refs_0_) | copy-start | bytes 786436
  25.4 47.9 %copy-start = (bf16[8,32,512]{2,1,0:T(8,128)(2,1)}, bf16[8,32,512]{2,1,0:T(8,128)(2,1)S(1)}, u32[]{:S(2)}) copy-start(bf16[8,32,512]{2,1,0:T(8,128)(2,1)S(1)} %get-tuple-element.16.refs_1_) | copy-start | bytes 786436
  25.4 12.7 %collective-permute-start.9 = (bf16[8,32,512]{2,1,0:T(8,128)(2,1)S(1)}, bf16[8,32,512]{2,1,0:T(8,128)(2,1)S(1)}, u32[]{:S(2)}, u32[]{:S(2)}) collective-permute-start(bf16[8,32,512]{2,1,0:T(8,128)(2,1)S(1)} %get-tuple-element.16.refs_1_), channel_id=1, source_target_pairs={{0,224},{32,0},{64,32},{96,64},{128,96},{160,128},{192,160},{224,1... | collective-permute-start | bytes 786440 | tf_op jit(solution)/shard_map/ppermute | solution.py:191
  31.3 10.5 %collective-permute-start = (bf16[8,32,512]{2,1,0:T(8,128)(2,1)S(1)}, bf16[8,32,512]{2,1,0:T(8,128)(2,1)S(1)}, u32[]{:S(2)}, u32[]{:S(2)}) collective-permute-start(bf16[8,32,512]{2,1,0:T(8,128)(2,1)S(1)} %get-tuple-element.17.refs_0_), channel_id=1, source_target_pairs={{0,32},{32,64},{64,96},{96,128},{128,160},{160,192},{192,224},{224... | collective-permute-start | bytes 786440 | tf_op jit(solution)/shard_map/ppermute | solution.py:188
  31.3 16.1 %collective-permute-start.3 = (bf16[8,32,512]{2,1,0:T(8,128)(2,1)S(1)}, bf16[8,32,512]{2,1,0:T(8,128)(2,1)S(1)}, u32[]{:S(2)}, u32[]{:S(2)}) collective-permute-start(bf16[8,32,512]{2,1,0:T(8,128)(2,1)S(1)} %get-tuple-element.16.refs_1_), channel_id=1, source_target_pairs={{0,32},{32,64},{64,96},{96,128},{128,160},{160,192},{192,224},{224... | collective-permute-start | bytes 786440 | tf_op jit(solution)/shard_map/ppermute | solution.py:188
  31.4 16.1 %collective-permute-start.6 = (bf16[8,32,512]{2,1,0:T(8,128)(2,1)S(1)}, bf16[8,32,512]{2,1,0:T(8,128)(2,1)S(1)}, u32[]{:S(2)}, u32[]{:S(2)}) collective-permute-start(bf16[8,32,512]{2,1,0:T(8,128)(2,1)S(1)} %get-tuple-element.17.refs_0_), channel_id=1, source_target_pairs={{0,224},{32,0},{64,32},{96,64},{128,96},{160,128},{192,160},{224,1... | collective-permute-start | bytes 786440 | tf_op jit(solution)/shard_map/ppermute | solution.py:191
  38.1 28.6 %copy-start.2 = (bf16[8,32,512]{2,1,0:T(8,128)(2,1)}, bf16[8,32,512]{2,1,0:T(8,128)(2,1)S(1)}, u32[]{:S(2)}) copy-start(bf16[8,32,512]{2,1,0:T(8,128)(2,1)S(1)} %collective-permute-done.9.refs_5_) | copy-start | bytes 786436
  38.1 12.6 %collective-permute-start.10 = (bf16[8,32,512]{2,1,0:T(8,128)(2,1)S(1)}, bf16[8,32,512]{2,1,0:T(8,128)(2,1)S(1)}, u32[]{:S(2)}, u32[]{:S(2)}) collective-permute-start(bf16[8,32,512]{2,1,0:T(8,128)(2,1)S(1)} %collective-permute-done.9.refs_5_), channel_id=1, source_target_pairs={{0,224},{32,0},{64,32},{96,64},{128,96},{160,128},{192,160},{224,1... | collective-permute-start | bytes 786440 | tf_op jit(solution)/shard_map/ppermute | solution.py:191
  41.8 24.9 %copy-start.3 = (bf16[8,32,512]{2,1,0:T(8,128)(2,1)}, bf16[8,32,512]{2,1,0:T(8,128)(2,1)S(1)}, u32[]{:S(2)}) copy-start(bf16[8,32,512]{2,1,0:T(8,128)(2,1)S(1)} %collective-permute-done.refs_2_) | copy-start | bytes 786436
  41.8 11.2 %collective-permute-start.1 = (bf16[8,32,512]{2,1,0:T(8,128)(2,1)S(1)}, bf16[8,32,512]{2,1,0:T(8,128)(2,1)S(1)}, u32[]{:S(2)}, u32[]{:S(2)}) collective-permute-start(bf16[8,32,512]{2,1,0:T(8,128)(2,1)S(1)} %collective-permute-done.refs_2_), channel_id=1, source_target_pairs={{0,32},{32,64},{64,96},{96,128},{128,160},{160,192},{192,224},{224... | collective-permute-start | bytes 786440 | tf_op jit(solution)/shard_map/ppermute | solution.py:188
  47.4 19.3 %copy-start.5 = (bf16[8,32,512]{2,1,0:T(8,128)(2,1)}, bf16[8,32,512]{2,1,0:T(8,128)(2,1)S(1)}, u32[]{:S(2)}) copy-start(bf16[8,32,512]{2,1,0:T(8,128)(2,1)S(1)} %collective-permute-done.3.refs_4_) | copy-start | bytes 786436
  47.4 11.2 %collective-permute-start.4 = (bf16[8,32,512]{2,1,0:T(8,128)(2,1)S(1)}, bf16[8,32,512]{2,1,0:T(8,128)(2,1)S(1)}, u32[]{:S(2)}, u32[]{:S(2)}) collective-permute-start(bf16[8,32,512]{2,1,0:T(8,128)(2,1)S(1)} %collective-permute-done.3.refs_4_), channel_id=1, source_target_pairs={{0,32},{32,64},{64,96},{96,128},{128,160},{160,192},{192,224},{224... | collective-permute-start | bytes 786440 | tf_op jit(solution)/shard_map/ppermute | solution.py:188
  47.4 19.3 %copy-start.6 = (bf16[8,32,512]{2,1,0:T(8,128)(2,1)}, bf16[8,32,512]{2,1,0:T(8,128)(2,1)S(1)}, u32[]{:S(2)}) copy-start(bf16[8,32,512]{2,1,0:T(8,128)(2,1)S(1)} %collective-permute-done.6.refs_3_) | copy-start | bytes 786436
  47.4 11.2 %collective-permute-start.7 = (bf16[8,32,512]{2,1,0:T(8,128)(2,1)S(1)}, bf16[8,32,512]{2,1,0:T(8,128)(2,1)S(1)}, u32[]{:S(2)}, u32[]{:S(2)}) collective-permute-start(bf16[8,32,512]{2,1,0:T(8,128)(2,1)S(1)} %collective-permute-done.6.refs_3_), channel_id=1, source_target_pairs={{0,224},{32,0},{64,32},{96,64},{128,96},{160,128},{192,160},{224,1... | collective-permute-start | bytes 786440 | tf_op jit(solution)/shard_map/ppermute | solution.py:191
  50.7 16.1 %copy-start.4 = (bf16[8,32,512]{2,1,0:T(8,128)(2,1)}, bf16[8,32,512]{2,1,0:T(8,128)(2,1)S(1)}, u32[]{:S(2)}) copy-start(bf16[8,32,512]{2,1,0:T(8,128)(2,1)S(1)} %collective-permute-done.10.refs_1_) | copy-start | bytes 786436
  50.7 11.2 %collective-permute-start.11 = (bf16[8,32,512]{2,1,0:T(8,128)(2,1)S(1)}, bf16[8,32,512]{2,1,0:T(8,128)(2,1)S(1)}, u32[]{:S(2)}, u32[]{:S(2)}) collective-permute-start(bf16[8,32,512]{2,1,0:T(8,128)(2,1)S(1)} %collective-permute-done.10.refs_1_), channel_id=1, source_target_pairs={{0,224},{32,0},{64,32},{96,64},{128,96},{160,128},{192,160},{224,1... | collective-permute-start | bytes 786440 | tf_op jit(solution)/shard_map/ppermute | solution.py:191
  53.0 13.7 %copy-start.8 = (bf16[8,32,512]{2,1,0:T(8,128)(2,1)}, bf16[8,32,512]{2,1,0:T(8,128)(2,1)S(1)}, u32[]{:S(2)}) copy-start(bf16[8,32,512]{2,1,0:T(8,128)(2,1)S(1)} %collective-permute-done.1.refs_6_) | copy-start | bytes 786436
  53.0 10.9 %collective-permute-start.2 = (bf16[8,32,512]{2,1,0:T(8,128)(2,1)S(1)}, bf16[8,32,512]{2,1,0:T(8,128)(2,1)S(1)}, u32[]{:S(2)}, u32[]{:S(2)}) collective-permute-start(bf16[8,32,512]{2,1,0:T(8,128)(2,1)S(1)} %collective-permute-done.1.refs_6_), channel_id=1, source_target_pairs={{0,32},{32,64},{64,96},{96,128},{128,160},{160,192},{192,224},{224... | collective-permute-start | bytes 786440 | tf_op jit(solution)/shard_map/ppermute | solution.py:188
  58.7 8.1 %copy-start.7 = (bf16[8,32,512]{2,1,0:T(8,128)(2,1)}, bf16[8,32,512]{2,1,0:T(8,128)(2,1)S(1)}, u32[]{:S(2)}) copy-start(bf16[8,32,512]{2,1,0:T(8,128)(2,1)S(1)} %collective-permute-done.4.refs_0_) | copy-start | bytes 786436
  58.7 8.1 %collective-permute-start.5 = (bf16[8,32,512]{2,1,0:T(8,128)(2,1)S(1)}, bf16[8,32,512]{2,1,0:T(8,128)(2,1)S(1)}, u32[]{:S(2)}, u32[]{:S(2)}) collective-permute-start(bf16[8,32,512]{2,1,0:T(8,128)(2,1)S(1)} %collective-permute-done.4.refs_0_), channel_id=1, source_target_pairs={{0,32},{32,64},{64,96},{96,128},{128,160},{160,192},{192,224},{224... | collective-permute-start | bytes 786440 | tf_op jit(solution)/shard_map/ppermute | solution.py:188
  58.7 8.1 %copy-start.10 = (bf16[8,32,512]{2,1,0:T(8,128)(2,1)}, bf16[8,32,512]{2,1,0:T(8,128)(2,1)S(1)}, u32[]{:S(2)}) copy-start(bf16[8,32,512]{2,1,0:T(8,128)(2,1)S(1)} %collective-permute-done.7.refs_7_) | copy-start | bytes 786436
  58.7 8.9 %collective-permute-start.8 = (bf16[8,32,512]{2,1,0:T(8,128)(2,1)S(1)}, bf16[8,32,512]{2,1,0:T(8,128)(2,1)}, u32[]{:S(2)}, u32[]{:S(2)}) collective-permute-start(bf16[8,32,512]{2,1,0:T(8,128)(2,1)S(1)} %collective-permute-done.7.refs_7_), channel_id=1, source_target_pairs={{0,224},{32,0},{64,32},{96,64},{128,96},{160,128},{192,160},{224,1... | collective-permute-start | bytes 786440 | tf_op jit(solution)/shard_map/ppermute | solution.py:191
  61.9 4.9 %copy-start.9 = (bf16[8,32,512]{2,1,0:T(8,128)(2,1)}, bf16[8,32,512]{2,1,0:T(8,128)(2,1)S(1)}, u32[]{:S(2)}) copy-start(bf16[8,32,512]{2,1,0:T(8,128)(2,1)S(1)} %collective-permute-done.11.refs_5_) | copy-start | bytes 786436
  63.9 2.9 %copy-start.11 = (bf16[8,32,512]{2,1,0:T(8,128)(2,1)}, bf16[8,32,512]{2,1,0:T(8,128)(2,1)S(1)}, u32[]{:S(2)}) copy-start(bf16[8,32,512]{2,1,0:T(8,128)(2,1)S(1)} %collective-permute-done.2.refs_2_) | copy-start | bytes 786436
  66.8 0.7 copy-start.12
  67.5 5.8 %collective-permute-start.12 = (bf16[8,6,64,512]{3,2,1,0:T(8,128)(2,1)S(1)}, bf16[8,6,64,512]{3,2,1,0:T(8,128)(2,1)}, u32[]{:S(2)}, u32[]{:S(2)}) collective-permute-start(bf16[8,6,64,512]{3,2,1,0:T(8,128)(2,1)S(1)} %bitcast.12), channel_id=1, source_target_pairs={{0,8},{8,0},{1,9},{9,1},{2,10},{10,2},{3,11},{11,3},{4,12},{12,4},... | collective-permute-start | bytes 9437192 | tf_op jit(solution)/shard_map/ppermute | solution.py:243
  67.5 13.9 %collective-permute-start.13 = (bf16[8,32,512]{2,1,0:T(8,128)(2,1)}, bf16[8,32,512]{2,1,0:T(8,128)(2,1)S(1)}, u32[]{:S(2)}, u32[]{:S(2)}) collective-permute-start(bf16[8,32,512]{2,1,0:T(8,128)(2,1)} %copy-done.11), channel_id=1, source_target_pairs={{0,32},{32,64},{64,96},{96,128},{128,160},{160,192},{192,224},{224... | collective-permute-start | bytes 786440 | tf_op jit(solution)/shard_map/ppermute | solution.py:188
  67.6 13.8 %collective-permute-start.14 = (bf16[8,32,512]{2,1,0:T(8,128)(2,1)}, bf16[8,32,512]{2,1,0:T(8,128)(2,1)S(1)}, u32[]{:S(2)}, u32[]{:S(2)}) collective-permute-start(bf16[8,32,512]{2,1,0:T(8,128)(2,1)} %copy-done.9), channel_id=1, source_target_pairs={{0,224},{32,0},{64,32},{96,64},{128,96},{160,128},{192,160},{224,1... | collective-permute-start | bytes 786440 | tf_op jit(solution)/shard_map/ppermute | solution.py:191
  81.5 0.8 copy-start.14
  90.8 2.1 %collective-permute-start.15 = (f32[1152,128]{1,0:T(8,128)S(1)}, f32[1152,128]{1,0:T(8,128)S(1)}, u32[]{:S(2)}, u32[]{:S(2)}) collective-permute-start(f32[1152,128]{1,0:T(8,128)S(1)} %get-tuple-element.13), channel_id=1, source_target_pairs={{0,8},{8,0},{1,9},{9,1},{2,10},{10,2},{3,11},{11,3},{4,12},{12,4},... | collective-permute-start | bytes 1769480 | tf_op jit(solution)/shard_map/ppermute | solution.py:248
  93.8 32.6 %all-to-all-start.2 = ((f32[1152,1,128]{2,1,0:T(1,128)}), f32[1152,1,128]{2,1,0:T(1,128)S(1)}, u32[]{:S(2)}, u32[]{:S(2)}) async-start(f32[1152,1,128]{2,1,0:T(1,128)} %bitcast.7), calls=%async_computation.2 | async-start | bytes 1179648 | tf_op jit(solution)/shard_map/all_to_all | solution.py:250
  (1 other events, 0.7 us)

commit v3 on v2

v3 whole, which is shorter than its diff:
```python
import functools

import jax
import jax.numpy as jnp
from jax import lax
from jax.experimental import pallas as pl
from jax.experimental.pallas import tpu as pltpu
from jax.sharding import Mesh, PartitionSpec as P

ROW = ("y", "xh")
AUX = ("z", "xl", "c")
A_PASS = 8
UNROLL = 4


def pick_kernel(copies, width, col_ref, count_ref, coef_ref, out_ref):
    slots = col_ref.shape[0]
    for pair in range(slots // 2):
        halves = []
        for s in (2 * pair, 2 * pair + 1):
            tile = col_ref[s]
            start = pl.multiple_of((tile // 2) * (2 * width), 2 * width)
            both = coef_ref[:, pl.ds(start, 2 * width)].astype(jnp.float32)
            want = s % 2
            swapped = pltpu.roll(both, width, 1)
            keep = jnp.full(both.shape, tile % 2, jnp.int32) == want
            live = jnp.full(both.shape, s, jnp.int32) < count_ref[0]
            halves.append(jnp.where(live, jnp.where(keep, both, swapped), 0.0))
        lane = lax.broadcasted_iota(jnp.int32, halves[0].shape, 1)
        merged = jnp.where(lane < width, halves[0], halves[1]).astype(out_ref.dtype)
        for n in range(copies):
            out_ref[n, :, pair * 2 * width : (pair + 1) * 2 * width] = merged


def pick(coefficients, cols, count, copies, width):
    norb = coefficients.shape[0]
    slots = cols.shape[0]
    return pl.pallas_call(
        functools.partial(pick_kernel, copies, width),
        out_shape=jax.ShapeDtypeStruct((copies, norb, slots * width), coefficients.dtype),
        in_specs=[
            pl.BlockSpec(memory_space=pltpu.SMEM),
            pl.BlockSpec(memory_space=pltpu.SMEM),
            pl.BlockSpec(memory_space=pltpu.VMEM),
        ],
        out_specs=pl.BlockSpec(memory_space=pltpu.VMEM),
        name="pick",
    )(cols, count, coefficients)


def half_rows(part, pieces, base, half, tiles):
    _, nq, height, width = part.shape
    orbitals = sum(piece.shape[0] * piece.shape[2] for piece in pieces)

    def tile(t, _):
        start = pl.multiple_of(t * height, height)
        picked = [piece[:, t].reshape(-1, width) for piece in pieces]
        result = lax.dot_general(
            part[t].reshape(nq * height, width),
            picked[0] if len(picked) == 1 else jnp.concatenate(picked, axis=0),
            (((1,), (1,)), ((), ())),
            preferred_element_type=jnp.float32,
        ).astype(jnp.bfloat16)
        for q in range(nq):
            col = base + q * orbitals
            half[pl.ds(start, height), col : col + orbitals] = result[q * height : (q + 1) * height]
        return 0

    lax.fori_loop(tiles[0], tiles[1], tile, 0, unroll=UNROLL)
    return base + nq * orbitals


def copies_of(blocks, held, sem):
    copies = [pltpu.make_async_copy(ref, held.at[n], sem.at[n]) for n, ref in enumerate(blocks)]
    for copy in copies:
        copy.start()
    return copies


def lower_products(half, add):
    step = half.shape[0] // 2
    for i, j in ((0, 0), (1, 1), (1, 0)):
        rows, cols = slice(i * step, (i + 1) * step), slice(j * step, (j + 1) * step)
        add(
            rows,
            cols,
            lax.dot_general(
                half[rows, :], half[cols, :], (((1,), (1,)), ((), ())), preferred_element_type=jnp.float32
            ),
        )


def early_kernel(own_ref, *refs):
    *blocks, total_ref, held, sem, half = refs
    copies = copies_of(blocks, held, sem)
    base = 0
    for low in range(0, len(blocks), A_PASS):
        high = min(low + A_PASS, len(blocks))
        for copy in copies[low:high]:
            copy.wait()
        base = half_rows(own_ref, [held.at[low:high]], base, half, (0, own_ref.shape[0]))

    def add(rows, cols, block):
        total_ref[rows, cols] = block

    lower_products(half, add)


def late_kernel(nz, nxl, ncore, core_ref, own_ref, early_ref, held, other_ref, *refs):
    *blocks, keep_ref, send_ref, other, other_sem, last, sem, half, total = refs
    rows = total.shape[0]
    ntiles, nq, height, _ = own_ref.shape
    copies = copies_of(blocks, last, sem)
    parts = [pltpu.make_async_copy(other_ref.at[t], other.at[t], other_sem.at[t]) for t in range(ntiles)]
    for copy in parts:
        copy.start()
    for copy in copies:
        copy.wait()
    base = half_rows(own_ref, [last], 0, half, (0, ntiles))
    for low in range(0, ntiles, UNROLL):
        tiles = (low, low + UNROLL)
        for copy in parts[low : low + UNROLL]:
            copy.wait()
        middle = half_rows(other, [held.at[:A_PASS]], base, half, tiles)
        half_rows(other, [held.at[A_PASS : held.shape[0]], last], middle, half, tiles)

    def add(rows, cols, block):
        block = block + early_ref[rows, cols]
        total[rows, cols] = block
        if rows != cols:
            total[cols, rows] = block.T

    lower_products(half, add)
    whole = total[...]
    on_diagonal = lax.broadcasted_iota(jnp.int32, whole.shape, 0) == lax.broadcasted_iota(
        jnp.int32, whole.shape, 1
    )
    diagonal = jnp.sum(jnp.where(on_diagonal, whole, 0.0), axis=0, keepdims=True)
    cols = rows // (nz * nxl * ncore)
    nrow = rows // height
    hc = cols // 2
    low = lax.broadcasted_iota(jnp.int32, (hc, 2 * height), 1) < height
    low1 = lax.broadcasted_iota(jnp.int32, (1, 2 * height), 1) < height
    per = hc + 1
    for which, out_ref in ((0, keep_ref), (1, send_ref)):
        core = core_ref[0] if which == 0 else 1 - core_ref[0]
        for z in range(nz):
            for x in range(nxl):
                first = pl.multiple_of(((z * nxl + x) * ncore + core) * cols, cols)
                for pair in range(nrow // 2):
                    lanes = slice(pair * 2 * height, (pair + 1) * 2 * height)
                    top = total[pl.ds(first, hc), lanes]
                    bottom = total[pl.ds(pl.multiple_of(first + hc, hc), hc), lanes]
                    d = diagonal[:, lanes]
                    even = jnp.where(low, top, pltpu.roll(bottom, height, 1))
                    odd = jnp.where(low, pltpu.roll(top, height, 1), bottom)
                    base = ((x * nrow + 2 * pair) * nz + z) * per
                    out_ref[base : base + hc, :] = even
                    out_ref[base + hc : base + per, :] = jnp.where(low1, d, 0.0)
                    base += nz * per
                    out_ref[base : base + hc, :] = odd
                    out_ref[base + hc : base + per, :] = jnp.where(low1, pltpu.roll(d, height, 1), 0.0)


def exchange(core, own, other, blocks, rest, sizes):
    ntiles, nq, height, width = own.shape
    norb = blocks[0].shape[1]
    rows = ntiles * height
    nz, nxl, ncore = sizes
    cols = rows // (nz * nxl * ncore)
    messages = nz * nxl * ntiles
    count = len(blocks)
    whole = pl.BlockSpec(memory_space=pltpu.VMEM)
    blocks = [pltpu.with_memory_space_constraint(b, pltpu.HBM) for b in blocks[:rest]] + blocks[rest:]
    other = pltpu.with_memory_space_constraint(other, pltpu.HBM)
    own = pltpu.with_memory_space_constraint(own, pltpu.VMEM)

    def anywhere(n):
        return [pl.BlockSpec(memory_space=pl.ANY)] * n

    def settings(terms):
        return dict(
            compiler_params=pltpu.CompilerParams(vmem_limit_bytes=32 * 1024 * 1024),
            cost_estimate=pl.CostEstimate(
                flops=2 * nq * rows * terms * norb * (width + rows), bytes_accessed=1 << 20, transcendentals=0
            ),
        )

    total, held = pl.pallas_call(
        early_kernel,
        out_shape=(
            jax.ShapeDtypeStruct((rows, rows), jnp.float32),
            jax.ShapeDtypeStruct((rest, ntiles, norb, width), jnp.bfloat16),
        ),
        in_specs=[whole] + anywhere(rest),
        out_specs=[whole] * 2,
        scratch_shapes=[
            pltpu.SemaphoreType.DMA((rest,)),
            pltpu.VMEM((rows, nq * rest * norb), jnp.bfloat16),
        ],
        name="early",
        **settings(rest),
    )(own, *blocks[:rest])
    total = pltpu.with_memory_space_constraint(total, pltpu.VMEM)
    held = pltpu.with_memory_space_constraint(held, pltpu.VMEM)
    shape = jax.ShapeDtypeStruct((messages * (cols // 2 + 1), 2 * height), jnp.float32)
    terms = 2 * count - rest
    return pl.pallas_call(
        functools.partial(late_kernel, *sizes),
        out_shape=(shape, shape),
        in_specs=[pl.BlockSpec(memory_space=pltpu.SMEM)] + [whole] * 3 + anywhere(1 + count - rest),
        out_specs=[whole] * 2,
        scratch_shapes=[
            pltpu.VMEM(other.shape, other.dtype),
            pltpu.SemaphoreType.DMA((ntiles,)),
            pltpu.VMEM((count - rest, ntiles, norb, width), jnp.bfloat16),
            pltpu.SemaphoreType.DMA((count - rest,)),
            pltpu.VMEM((rows, nq * terms * norb), jnp.bfloat16),
            pltpu.VMEM((rows, rows), jnp.float32),
        ],
        name="late",
        **settings(terms),
    )(core, own, total, held, other, *blocks[rest:])


def ring(chunks, axis, size, beside, when):
    up = [(i, (i + 1) % size) for i in range(size)]
    down = [(i, (i - 1) % size) for i in range(size)]
    rights, lefts, got = list(chunks), list(chunks), []
    for step in range(1, size // 2 + 1):
        last = step == size // 2
        if step == when:
            rights, lefts, beside = lax.optimization_barrier((rights, lefts, beside))
        for n in range(len(chunks)):
            if not last or n % 2 == 0:
                rights[n] = lax.ppermute(rights[n], axis, up)
                got.append(rights[n])
            if not last or n % 2 == 1:
                lefts[n] = lax.ppermute(lefts[n], axis, down)
                got.append(lefts[n])
    return got, beside


def add_up(got_ref, per):
    total = got_ref[0:per, :]
    for n in range(1, got_ref.shape[0] // per):
        total = total + got_ref[n * per : (n + 1) * per, :]
    return total


def sum_kernel(got_ref, out_ref):
    out_ref[...] = add_up(got_ref, out_ref.shape[0])


def summed(got, parts):
    return pl.pallas_call(
        sum_kernel,
        out_shape=jax.ShapeDtypeStruct((got.shape[0] // parts, got.shape[1]), got.dtype),
        in_specs=[pl.BlockSpec(memory_space=pltpu.VMEM)],
        out_specs=pl.BlockSpec(memory_space=pltpu.VMEM),
        name="summed",
    )(pltpu.with_memory_space_constraint(got, pltpu.VMEM))


def finish_kernel(scale_diagonal, scale_tiles, per, place_ref, got_ref, tiles_ref, diagonal_ref):
    hc = per - 1
    cols, height = tiles_ref.shape
    total = add_up(got_ref, per)
    top = total[:hc]
    flat = jnp.concatenate([top, pltpu.roll(top, height, 1)], axis=0)[:, :height]
    n = place_ref[1] * cols + lax.broadcasted_iota(jnp.int32, flat.shape, 0)
    m = place_ref[0] * height + lax.broadcasted_iota(jnp.int32, flat.shape, 1)
    tiles_ref[...] = jnp.where(m == n, 0.0, flat) / scale_tiles
    diagonal_ref[...] = total[hc:per, :height] / scale_diagonal


def finish(got, place, height, cols, count):
    per = cols // 2 + 1
    return pl.pallas_call(
        functools.partial(finish_kernel, float(count), float(count) ** 0.5, per),
        out_shape=(
            jax.ShapeDtypeStruct((cols, height), jnp.float32),
            jax.ShapeDtypeStruct((1, height), jnp.float32),
        ),
        in_specs=[pl.BlockSpec(memory_space=pltpu.SMEM), pl.BlockSpec(memory_space=pltpu.VMEM)],
        out_specs=[pl.BlockSpec(memory_space=pltpu.VMEM)] * 2,
        name="finish",
    )(place, pltpu.with_memory_space_constraint(got, pltpu.VMEM))


def turn(rows, axes):
    rows = rows.reshape(rows.shape[0], 1, rows.shape[1])
    rows = lax.all_to_all(rows, axes, 0, 0, tiled=True)
    return rows.reshape(rows.shape[0], rows.shape[2])


def local(three_center, coefficients, col_tiles, tile_count):
    nq, _, height, width = three_center.shape
    nz, nxl, ncore = (lax.axis_size(a) for a in AUX)
    nrow = lax.axis_size("y") * lax.axis_size("xh")
    naux = nz * nxl * ncore
    norb = coefficients.shape[0]
    rows = nrow * height
    cols = rows // naux
    core = lax.axis_index("c")

    picks = pick(coefficients, col_tiles.reshape(-1), tile_count, nrow * nxl, height)
    integrals = three_center.reshape(nq, height, width)
    picks = lax.all_to_all(picks, ("xl",) + ROW, 0, 0, tiled=True)
    chunks = [picks[n * nrow : (n + 1) * nrow] for n in range(nxl)]
    own = lax.all_to_all(integrals, ROW, 0, 0, tiled=True)
    arrived, own = ring(chunks, "z", nz, own, 4)
    blocks = chunks + arrived
    own = own.reshape(nrow, nq // nrow, height, width)
    other = lax.ppermute(own, "c", [(0, 1), (1, 0)])

    keep, send = exchange(core.reshape(1), own, other, blocks, len(blocks) - nxl, (nz, nxl, ncore))
    mine = keep + lax.ppermute(send, "c", [(0, 1), (1, 0)])
    got = summed(turn(mine, ("xl",) + ROW), nrow * nxl)
    got = turn(got, "z")

    row = lax.axis_index(ROW)
    place = jnp.stack([row, lax.axis_index(AUX)]).astype(jnp.int32)
    tiles, diagonal = finish(got, place, height, cols, nq * naux * norb * naux)
    return tiles.T, diagonal.reshape(height)


def solution(mesh):
    fine = Mesh(mesh.devices.reshape(8, 2, 2, 4, 2), AUX + ROW)
    in_specs = (P(AUX, ROW, None, None), P(AUX, None), P(ROW, None), P(ROW))
    out_specs = (P(ROW, AUX), P(ROW))
    return jax.shard_map(local, mesh=fine, in_specs=in_specs, out_specs=out_specs, check_vma=False)
```

time: 128 us -> 120 us (0.938)
  waiting for transfers between devices: 45.2 us -> 37.4 us
  Pallas kernels: 20.2 us -> 15.7 us
  starting transfers between devices: 39.6 us -> 43.5 us
    ppermute x7, waiting for transfers between devices: 16.8 us -> 6.25 us  [ring(): rights[n] = lax.ppermute(rights[n], axis, up)]
    ppermute x7, waiting for transfers between devices: 3.51 us -> 11.1 us  [ring(): lefts[n] = lax.ppermute(lefts[n], axis, down)]
    pallas_call x2 -> x3, Pallas kernels: 16.7 us -> 12.3 us  [the longest x1 6.13 us: exchange(): pl.pallas_call(functools.partial(late_kernel, *sizes), out_shape=(shape,...]
    ppermute x7, starting transfers between devices: 24.2 us -> 27.2 us  [ring(): lefts[n] = lax.ppermute(lefts[n], axis, down)]
    all_to_all x1 -> x2, waiting for transfers between devices: 20.6 us -> 18.1 us  [turn(): rows = lax.all_to_all(rows, axes, 0, 0, tiled=True)]
    ppermute x1, waiting for transfers between devices: 2.46 us -> 0.01 us  [local(): other = lax.ppermute(own, 'c', [(0, 1), (1, 0)])]
    all_to_all x1 -> x2, starting transfers between devices: 11.4 us -> 12.6 us  [turn(): rows = lax.all_to_all(rows, axes, 0, 0, tiled=True)]
  transfers between devices with their start and end apart: 18 -> 19, of which waited for: 9 -> 11; matrix products, arithmetic and copies ran while one was open for 1% -> 1% of each run, Pallas kernels for 6% -> 5%
where the time goes in v3:
time: 120 us; the launch traced here: 119 us
  starting transfers between devices  43.5 us (36%)
  waiting for transfers between devices  37.4 us (31%)
  blocking collectives  17.3 us (14%)
  Pallas kernels  15.7 us (13%)
  local copies, waits for them, and re-layouts  2.42 us (2%)
  other arithmetic  1.48 us (1%)
  between operations  1.44 us (1%)
    ppermute x7, starting transfers between devices, ring(): lefts[n] = lax.ppermute(lefts[n], axis, down)  27.2 us
    all_to_all x2, waiting for transfers between devices, turn(): rows = lax.all_to_all(rows, axes, 0, 0, tiled=True)  18.1 us
    all_to_all x1, blocking collectives, local(): picks = lax.all_to_all(picks, ('xl',) + ROW, 0, 0, tiled=True)  17.3 us
    all_to_all x2, starting transfers between devices, turn(): rows = lax.all_to_all(rows, axes, 0, 0, tiled=True)  12.6 us
    ppermute x7, waiting for transfers between devices, ring(): lefts[n] = lax.ppermute(lefts[n], axis, down)  11.1 us
    ppermute x7, waiting for transfers between devices, ring(): rights[n] = lax.ppermute(rights[n], axis, up)  6.25 us
    pallas_call x1, Pallas kernels, exchange(): pl.pallas_call(functools.partial(late_kernel, *sizes), out_shape=(shape,...  6.13 us
    pallas_call x1, Pallas kernels, exchange(): pl.pallas_call(early_kernel, out_shape=(jax.ShapeDtypeStruct((rows, rows)...  5.56 us
  transfers between devices with their start and end apart: 19, of which 11 were waited for; matrix products, arithmetic and copies ran while one was open for 1% of the time, Pallas kernels for 5%

profile of v3, /device:TPU:2, one launch (start us, length us, event | category | flops | bytes accessed | tf_op | source)
XLA Modules:
  0.0 119.3 jit_solution(12810695965382920868)
XLA Ops:
  1.3 2.1 %pick.1 = bf16[16,32,512]{2,1,0:T(8,128)(2,1)} custom-call(s32[8]{0:T(128)} %bitcast.23, s32[1]{0:T(128)S(6)} %copy.8.count_ref, bf16[32,10240]{1,0:T(8,128)(2,1)} %coef_ref.1), custom_call_target="tpu_custom_call" | custom-call | tf_op jit(solution)/shard_map/pick/pallas_call | solution.py:38
  3.3 17.3 %all_to_all.20 = bf16[16,32,512]{2,1,0:T(8,128)(2,1)} all-to-all(bf16[16,32,512]{2,1,0:T(8,128)(2,1)} %pick.1), channel_id=1, replica_groups=mesh['z'=8,'xl'=2,'c'=2,'y'=4,'xh'=2] {'xl','y','xh'}, dimensions={0} | all-to-all | bytes 1048576 | tf_op jit(solution)/shard_map/all_to_all | solution.py:309
  20.6 3.7 %all-to-all-start.1 = ((bf16[48,64,512]{2,1,0:T(8,128)(2,1)}), bf16[48,64,512]{2,1,0:T(8,128)(2,1)S(1)}, u32[]{:S(2)}, u32[]{:S(2)}) async-start(bf16[48,64,512]{2,1,0:T(8,128)(2,1)} %bitcast.21), calls=%async_computation.1 | async-start | bytes 6291456 | tf_op jit(solution)/shard_map/all_to_all | solution.py:311
  24.3 1.1 fusion
  25.4 5.9 %collective-permute-start.9 = (bf16[8,32,512]{2,1,0:T(8,128)(2,1)S(1)}, bf16[8,32,512]{2,1,0:T(8,128)(2,1)S(1)}, u32[]{:S(2)}, u32[]{:S(2)}) collective-permute-start(bf16[8,32,512]{2,1,0:T(8,128)(2,1)S(1)} %get-tuple-element.20.refs_1_), channel_id=1, source_target_pairs={{0,224},{32,0},{64,32},{96,64},{128,96},{160,128},{192,160},{224,1... | collective-permute-start | bytes 786440 | tf_op jit(solution)/shard_map/ppermute | solution.py:239
  31.4 3.2 %collective-permute-start.6 = (bf16[8,32,512]{2,1,0:T(8,128)(2,1)S(1)}, bf16[8,32,512]{2,1,0:T(8,128)(2,1)S(1)}, u32[]{:S(2)}, u32[]{:S(2)}) collective-permute-start(bf16[8,32,512]{2,1,0:T(8,128)(2,1)S(1)} %get-tuple-element.21.refs_0_), channel_id=1, source_target_pairs={{0,224},{32,0},{64,32},{96,64},{128,96},{160,128},{192,160},{224,1... | collective-permute-start | bytes 786440 | tf_op jit(solution)/shard_map/ppermute | solution.py:239
  34.6 3.5 %collective-permute-done.9.refs_5_ = bf16[8,32,512]{2,1,0:T(8,128)(2,1)S(1)} collective-permute-done((bf16[8,32,512]{2,1,0:T(8,128)(2,1)S(1)}, bf16[8,32,512]{2,1,0:T(8,128)(2,1)S(1)}, u32[]{:S(2)}, u32[]{:S(2)}) %collective-permute-start.9) | collective-permute-done | bytes 262176 | tf_op jit(solution)/shard_map/ppermute | solution.py:239
  38.1 3.7 %collective-permute-start.10 = (bf16[8,32,512]{2,1,0:T(8,128)(2,1)S(1)}, bf16[8,32,512]{2,1,0:T(8,128)(2,1)S(1)}, u32[]{:S(2)}, u32[]{:S(2)}) collective-permute-start(bf16[8,32,512]{2,1,0:T(8,128)(2,1)S(1)} %collective-permute-done.9.refs_5_), channel_id=1, source_target_pairs={{0,224},{32,0},{64,32},{96,64},{128,96},{160,128},{192,160},{224,1... | collective-permute-start | bytes 786440 | tf_op jit(solution)/shard_map/ppermute | solution.py:239
  41.8 1.9 %collective-permute-done.6.refs_3_ = bf16[8,32,512]{2,1,0:T(8,128)(2,1)S(1)} collective-permute-done((bf16[8,32,512]{2,1,0:T(8,128)(2,1)S(1)}, bf16[8,32,512]{2,1,0:T(8,128)(2,1)S(1)}, u32[]{:S(2)}, u32[]{:S(2)}) %collective-permute-start.6) | collective-permute-done | bytes 262176 | tf_op jit(solution)/shard_map/ppermute | solution.py:239
  43.7 3.7 %collective-permute-start.7 = (bf16[8,32,512]{2,1,0:T(8,128)(2,1)S(1)}, bf16[8,32,512]{2,1,0:T(8,128)(2,1)S(1)}, u32[]{:S(2)}, u32[]{:S(2)}) collective-permute-start(bf16[8,32,512]{2,1,0:T(8,128)(2,1)S(1)} %collective-permute-done.6.refs_3_), channel_id=1, source_target_pairs={{0,224},{32,0},{64,32},{96,64},{128,96},{160,128},{192,160},{224,1... | collective-permute-start | bytes 786440 | tf_op jit(solution)/shard_map/ppermute | solution.py:239
  47.4 1.9 %collective-permute-done.10.refs_9_ = bf16[8,32,512]{2,1,0:T(8,128)(2,1)S(1)} collective-permute-done((bf16[8,32,512]{2,1,0:T(8,128)(2,1)S(1)}, bf16[8,32,512]{2,1,0:T(8,128)(2,1)S(1)}, u32[]{:S(2)}, u32[]{:S(2)}) %collective-permute-start.10) | collective-permute-done | bytes 262176 | tf_op jit(solution)/shard_map/ppermute | solution.py:239
  49.4 3.7 %collective-permute-start.11 = (bf16[8,32,512]{2,1,0:T(8,128)(2,1)S(1)}, bf16[8,32,512]{2,1,0:T(8,128)(2,1)S(1)}, u32[]{:S(2)}, u32[]{:S(2)}) collective-permute-start(bf16[8,32,512]{2,1,0:T(8,128)(2,1)S(1)} %collective-permute-done.10.refs_9_), channel_id=1, source_target_pairs={{0,224},{32,0},{64,32},{96,64},{128,96},{160,128},{192,160},{224,1... | collective-permute-start | bytes 786440 | tf_op jit(solution)/shard_map/ppermute | solution.py:239
  53.1 1.9 %collective-permute-done.7.refs_7_ = bf16[8,32,512]{2,1,0:T(8,128)(2,1)S(1)} collective-permute-done((bf16[8,32,512]{2,1,0:T(8,128)(2,1)S(1)}, bf16[8,32,512]{2,1,0:T(8,128)(2,1)S(1)}, u32[]{:S(2)}, u32[]{:S(2)}) %collective-permute-start.7) | collective-permute-done | bytes 262176 | tf_op jit(solution)/shard_map/ppermute | solution.py:239
  55.0 3.7 %collective-permute-start.8 = (bf16[8,32,512]{2,1,0:T(8,128)(2,1)S(1)}, bf16[8,32,512]{2,1,0:T(8,128)(2,1)S(1)}, u32[]{:S(2)}, u32[]{:S(2)}) collective-permute-start(bf16[8,32,512]{2,1,0:T(8,128)(2,1)S(1)} %collective-permute-done.7.refs_7_), channel_id=1, source_target_pairs={{0,224},{32,0},{64,32},{96,64},{128,96},{160,128},{192,160},{224,1... | collective-permute-start | bytes 786440 | tf_op jit(solution)/shard_map/ppermute | solution.py:239
  58.7 1.8 %collective-permute-done.11.refs_13_ = bf16[8,32,512]{2,1,0:T(8,128)(2,1)S(1)} collective-permute-done((bf16[8,32,512]{2,1,0:T(8,128)(2,1)S(1)}, bf16[8,32,512]{2,1,0:T(8,128)(2,1)S(1)}, u32[]{:S(2)}, u32[]{:S(2)}) %collective-permute-start.11) | collective-permute-done | bytes 262176 | tf_op jit(solution)/shard_map/ppermute | solution.py:239
  60.5 3.4 %collective-permute-done.5.refs_12_ = bf16[8,32,512]{2,1,0:T(8,128)(2,1)S(1)} collective-permute-done((bf16[8,32,512]{2,1,0:T(8,128)(2,1)S(1)}, bf16[8,32,512]{2,1,0:T(8,128)(2,1)S(1)}, u32[]{:S(2)}, u32[]{:S(2)}) %collective-permute-start.5) | collective-permute-done | bytes 262176 | tf_op jit(solution)/shard_map/ppermute | solution.py:236
  64.0 0.6 copy-done.11
  64.6 0.7 copy-done.12
  65.3 1.5 %collective-permute-done.2.refs_10_ = bf16[8,32,512]{2,1,0:T(8,128)(2,1)} collective-permute-done((bf16[8,32,512]{2,1,0:T(8,128)(2,1)S(1)}, bf16[8,32,512]{2,1,0:T(8,128)(2,1)}, u32[]{:S(2)}, u32[]{:S(2)}) %collective-permute-start.2) | collective-permute-done | bytes 262176 | tf_op jit(solution)/shard_map/ppermute | solution.py:236
  66.8 3.2 %collective-permute-start.14 = (bf16[8,32,512]{2,1,0:T(8,128)(2,1)}, bf16[8,32,512]{2,1,0:T(8,128)(2,1)S(1)}, u32[]{:S(2)}, u32[]{:S(2)}) collective-permute-start(bf16[8,32,512]{2,1,0:T(8,128)(2,1)} %copy-done.10), channel_id=1, source_target_pairs={{0,224},{32,0},{64,32},{96,64},{128,96},{160,128},{192,160},{224,1... | collective-permute-start | bytes 786440 | tf_op jit(solution)/shard_map/ppermute | solution.py:239
  70.1 5.6 %early.1 = (f32[512,512]{1,0:T(8,128)S(1)}, bf16[14,8,32,512]{3,2,1,0:T(8,128)(2,1)S(1)}) custom-call(bf16[8,6,64,512]{3,2,1,0:T(8,128)(2,1)S(1)} %bitcast.17, bf16[8,32,512]{2,1,0:T(8,128)(2,1)} %copy-done.1, bf16[8,32,512]{2,1,0:T(8,128)(2,1)} %copy-done, bf16[8,32,512]{2,1,0:T(8,128)(2,1)} %copy-done.5, bf16[8,32,512]{2,1,0:T(8,128)(2,1)} %copy-done.4, ...), custom_call_target="tpu_custom_call" | custom-call | flops 2818572288 | bytes 1048576 | tf_op jit(solution)/shard_map/early/pallas_call | solution.py:189
  75.6 1.3 %collective-permute-done.13.refs_0_ = bf16[8,32,512]{2,1,0:T(8,128)(2,1)S(1)} collective-permute-done((bf16[8,32,512]{2,1,0:T(8,128)(2,1)}, bf16[8,32,512]{2,1,0:T(8,128)(2,1)S(1)}, u32[]{:S(2)}, u32[]{:S(2)}) %collective-permute-start.13) | collective-permute-done | bytes 262176 | tf_op jit(solution)/shard_map/ppermute | solution.py:236
  77.0 6.1 %late.1 = (f32[1152,128]{1,0:T(8,128)S(1)}, f32[1152,128]{1,0:T(8,128)S(1)}) custom-call(s32[1]{0:T(128)} %bitcast.2.core_ref, bf16[8,6,64,512]{3,2,1,0:T(8,128)(2,1)S(1)} %bitcast.18, f32[512,512]{1,0:T(8,128)S(1)} %get-tuple-element.12.early_ref, bf16[14,8,32,512]{3,2,1,0:T(8,128)(2,1)S(1)} %get-tuple-element.13.held, ...), custom_call_target="tpu_custom_call" | custom-call | flops 3623878656 | bytes 1048576 | tf_op jit(solution)/shard_map/late/pallas_call | solution.py:208
  83.2 2.0 %collective-permute-done.15 = f32[1152,128]{1,0:T(8,128)S(1)} collective-permute-done((f32[1152,128]{1,0:T(8,128)S(1)}, f32[1152,128]{1,0:T(8,128)S(1)}, u32[]{:S(2)}, u32[]{:S(2)}) %collective-permute-start.15) | collective-permute-done | bytes 589856 | tf_op jit(solution)/shard_map/ppermute | solution.py:318
  85.2 0.9 add.15
  86.1 8.3 %all-to-all-start.2 = ((f32[1152,1,128]{2,1,0:T(1,128)}), f32[1152,1,128]{2,1,0:T(1,128)S(1)}, u32[]{:S(2)}, u32[]{:S(2)}) async-start(f32[1152,1,128]{2,1,0:T(1,128)} %bitcast.7), calls=%async_computation.2 | async-start | bytes 1179648 | tf_op jit(solution)/shard_map/all_to_all | solution.py:293
  94.4 10.6 %all-to-all-done.2 = f32[1152,1,128]{2,1,0:T(1,128)S(1)} async-done(((f32[1152,1,128]{2,1,0:T(1,128)}), f32[1152,1,128]{2,1,0:T(1,128)S(1)}, u32[]{:S(2)}, u32[]{:S(2)}) %all-to-all-start.2) | async-done | bytes 589856 | tf_op jit(solution)/shard_map/all_to_all | solution.py:293
  105.0 0.6 summed.1
  105.7 4.2 %all-to-all-start.3 = ((f32[72,1,128]{2,1,0:T(1,128)}), f32[72,1,128]{2,1,0:T(1,128)S(1)}, u32[]{:S(2)}, u32[]{:S(2)}) async-start(f32[72,1,128]{2,1,0:T(1,128)} %bitcast.22), calls=%async_computation.3 | async-start | bytes 73728 | tf_op jit(solution)/shard_map/all_to_all | solution.py:293
  109.9 0.6 pad_add_fusion.place_ref
  110.5 7.5 %all-to-all-done.3 = f32[72,1,128]{2,1,0:T(1,128)S(1)} async-done(((f32[72,1,128]{2,1,0:T(1,128)}), f32[72,1,128]{2,1,0:T(1,128)S(1)}, u32[]{:S(2)}, u32[]{:S(2)}) %all-to-all-start.3) | async-done | bytes 36896 | tf_op jit(solution)/shard_map/all_to_all | solution.py:293
  118.0 1.3 %finish.1 = (f32[16,64]{1,0:T(8,128)}, f32[1,64]{1,0:T(1,128)}) custom-call(s32[2]{0:T(128)} %pad_add_fusion.place_ref, f32[72,128]{1,0:T(8,128)S(1)} %bitcast.20), custom_call_target="tpu_custom_call" | custom-call | tf_op jit(solution)/shard_map/finish/pallas_call | solution.py:279
  (41 shorter events, 0.2 us)
Async XLA Ops:
  20.6 46.2 %all-to-all-start.1 = ((bf16[48,64,512]{2,1,0:T(8,128)(2,1)}), bf16[48,64,512]{2,1,0:T(8,128)(2,1)S(1)}, u32[]{:S(2)}, u32[]{:S(2)}) async-start(bf16[48,64,512]{2,1,0:T(8,128)(2,1)} %bitcast.21), calls=%async_computation.1 | async-start | bytes 6291456 | tf_op jit(solution)/shard_map/all_to_all | solution.py:311
  25.4 38.5 %copy-start.1 = (bf16[8,32,512]{2,1,0:T(8,128)(2,1)}, bf16[8,32,512]{2,1,0:T(8,128)(2,1)S(1)}, u32[]{:S(2)}) copy-start(bf16[8,32,512]{2,1,0:T(8,128)(2,1)S(1)} %get-tuple-element.21.refs_0_) | copy-start | bytes 786436
  25.4 44.7 %copy-start = (bf16[8,32,512]{2,1,0:T(8,128)(2,1)}, bf16[8,32,512]{2,1,0:T(8,128)(2,1)S(1)}, u32[]{:S(2)}) copy-start(bf16[8,32,512]{2,1,0:T(8,128)(2,1)S(1)} %get-tuple-element.20.refs_1_) | copy-start | bytes 786436
  25.4 12.7 %collective-permute-start.9 = (bf16[8,32,512]{2,1,0:T(8,128)(2,1)S(1)}, bf16[8,32,512]{2,1,0:T(8,128)(2,1)S(1)}, u32[]{:S(2)}, u32[]{:S(2)}) collective-permute-start(bf16[8,32,512]{2,1,0:T(8,128)(2,1)S(1)} %get-tuple-element.20.refs_1_), channel_id=1, source_target_pairs={{0,224},{32,0},{64,32},{96,64},{128,96},{160,128},{192,160},{224,1... | collective-permute-start | bytes 786440 | tf_op jit(solution)/shard_map/ppermute | solution.py:239
  31.3 10.5 %collective-permute-start.3 = (bf16[8,32,512]{2,1,0:T(8,128)(2,1)S(1)}, bf16[8,32,512]{2,1,0:T(8,128)(2,1)S(1)}, u32[]{:S(2)}, u32[]{:S(2)}) collective-permute-start(bf16[8,32,512]{2,1,0:T(8,128)(2,1)S(1)} %get-tuple-element.20.refs_1_), channel_id=1, source_target_pairs={{0,32},{32,64},{64,96},{96,128},{128,160},{160,192},{192,224},{224... | collective-permute-start | bytes 786440 | tf_op jit(solution)/shard_map/ppermute | solution.py:236
  31.4 12.4 %collective-permute-start.6 = (bf16[8,32,512]{2,1,0:T(8,128)(2,1)S(1)}, bf16[8,32,512]{2,1,0:T(8,128)(2,1)S(1)}, u32[]{:S(2)}, u32[]{:S(2)}) collective-permute-start(bf16[8,32,512]{2,1,0:T(8,128)(2,1)S(1)} %get-tuple-element.21.refs_0_), channel_id=1, source_target_pairs={{0,224},{32,0},{64,32},{96,64},{128,96},{160,128},{192,160},{224,1... | collective-permute-start | bytes 786440 | tf_op jit(solution)/shard_map/ppermute | solution.py:239
  34.6 12.8 %collective-permute-start = (bf16[8,32,512]{2,1,0:T(8,128)(2,1)S(1)}, bf16[8,32,512]{2,1,0:T(8,128)(2,1)S(1)}, u32[]{:S(2)}, u32[]{:S(2)}) collective-permute-start(bf16[8,32,512]{2,1,0:T(8,128)(2,1)S(1)} %get-tuple-element.21.refs_0_), channel_id=1, source_target_pairs={{0,32},{32,64},{64,96},{96,128},{128,160},{160,192},{192,224},{224... | collective-permute-start | bytes 786440 | tf_op jit(solution)/shard_map/ppermute | solution.py:236
  38.1 25.8 %copy-start.2 = (bf16[8,32,512]{2,1,0:T(8,128)(2,1)}, bf16[8,32,512]{2,1,0:T(8,128)(2,1)S(1)}, u32[]{:S(2)}) copy-start(bf16[8,32,512]{2,1,0:T(8,128)(2,1)S(1)} %collective-permute-done.9.refs_5_) | copy-start | bytes 786436
  38.1 11.2 %collective-permute-start.10 = (bf16[8,32,512]{2,1,0:T(8,128)(2,1)S(1)}, bf16[8,32,512]{2,1,0:T(8,128)(2,1)S(1)}, u32[]{:S(2)}, u32[]{:S(2)}) collective-permute-start(bf16[8,32,512]{2,1,0:T(8,128)(2,1)S(1)} %collective-permute-done.9.refs_5_), channel_id=1, source_target_pairs={{0,224},{32,0},{64,32},{96,64},{128,96},{160,128},{192,160},{224,1... | collective-permute-start | bytes 786440 | tf_op jit(solution)/shard_map/ppermute | solution.py:239
  41.8 22.1 %copy-start.3 = (bf16[8,32,512]{2,1,0:T(8,128)(2,1)}, bf16[8,32,512]{2,1,0:T(8,128)(2,1)S(1)}, u32[]{:S(2)}) copy-start(bf16[8,32,512]{2,1,0:T(8,128)(2,1)S(1)} %collective-permute-done.3.refs_4_) | copy-start | bytes 786436
  41.8 11.2 %collective-permute-start.4 = (bf16[8,32,512]{2,1,0:T(8,128)(2,1)S(1)}, bf16[8,32,512]{2,1,0:T(8,128)(2,1)S(1)}, u32[]{:S(2)}, u32[]{:S(2)}) collective-permute-start(bf16[8,32,512]{2,1,0:T(8,128)(2,1)S(1)} %collective-permute-done.3.refs_4_), channel_id=1, source_target_pairs={{0,32},{32,64},{64,96},{96,128},{128,160},{160,192},{192,224},{224... | collective-permute-start | bytes 786440 | tf_op jit(solution)/shard_map/ppermute | solution.py:236
  43.7 20.2 %copy-start.4 = (bf16[8,32,512]{2,1,0:T(8,128)(2,1)}, bf16[8,32,512]{2,1,0:T(8,128)(2,1)S(1)}, u32[]{:S(2)}) copy-start(bf16[8,32,512]{2,1,0:T(8,128)(2,1)S(1)} %collective-permute-done.6.refs_3_) | copy-start | bytes 786436
  43.7 11.2 %collective-permute-start.7 = (bf16[8,32,512]{2,1,0:T(8,128)(2,1)S(1)}, bf16[8,32,512]{2,1,0:T(8,128)(2,1)S(1)}, u32[]{:S(2)}, u32[]{:S(2)}) collective-permute-start(bf16[8,32,512]{2,1,0:T(8,128)(2,1)S(1)} %collective-permute-done.6.refs_3_), channel_id=1, source_target_pairs={{0,224},{32,0},{64,32},{96,64},{128,96},{160,128},{192,160},{224,1... | collective-permute-start | bytes 786440 | tf_op jit(solution)/shard_map/ppermute | solution.py:239
  47.4 16.5 %copy-start.5 = (bf16[8,32,512]{2,1,0:T(8,128)(2,1)}, bf16[8,32,512]{2,1,0:T(8,128)(2,1)S(1)}, u32[]{:S(2)}) copy-start(bf16[8,32,512]{2,1,0:T(8,128)(2,1)S(1)} %collective-permute-done.refs_2_) | copy-start | bytes 786436
  47.4 11.2 %collective-permute-start.1 = (bf16[8,32,512]{2,1,0:T(8,128)(2,1)S(1)}, bf16[8,32,512]{2,1,0:T(8,128)(2,1)S(1)}, u32[]{:S(2)}, u32[]{:S(2)}) collective-permute-start(bf16[8,32,512]{2,1,0:T(8,128)(2,1)S(1)} %collective-permute-done.refs_2_), channel_id=1, source_target_pairs={{0,32},{32,64},{64,96},{96,128},{128,160},{160,192},{192,224},{224... | collective-permute-start | bytes 786440 | tf_op jit(solution)/shard_map/ppermute | solution.py:236
  49.3 14.6 %copy-start.6 = (bf16[8,32,512]{2,1,0:T(8,128)(2,1)}, bf16[8,32,512]{2,1,0:T(8,128)(2,1)S(1)}, u32[]{:S(2)}) copy-start(bf16[8,32,512]{2,1,0:T(8,128)(2,1)S(1)} %collective-permute-done.10.refs_9_) | copy-start | bytes 786436
  49.4 11.2 %collective-permute-start.11 = (bf16[8,32,512]{2,1,0:T(8,128)(2,1)S(1)}, bf16[8,32,512]{2,1,0:T(8,128)(2,1)S(1)}, u32[]{:S(2)}, u32[]{:S(2)}) collective-permute-start(bf16[8,32,512]{2,1,0:T(8,128)(2,1)S(1)} %collective-permute-done.10.refs_9_), channel_id=1, source_target_pairs={{0,224},{32,0},{64,32},{96,64},{128,96},{160,128},{192,160},{224,1... | collective-permute-start | bytes 786440 | tf_op jit(solution)/shard_map/ppermute | solution.py:239
  53.0 10.9 %copy-start.7 = (bf16[8,32,512]{2,1,0:T(8,128)(2,1)}, bf16[8,32,512]{2,1,0:T(8,128)(2,1)S(1)}, u32[]{:S(2)}) copy-start(bf16[8,32,512]{2,1,0:T(8,128)(2,1)S(1)} %collective-permute-done.4.refs_8_) | copy-start | bytes 786436
  53.0 10.9 %collective-permute-start.5 = (bf16[8,32,512]{2,1,0:T(8,128)(2,1)S(1)}, bf16[8,32,512]{2,1,0:T(8,128)(2,1)S(1)}, u32[]{:S(2)}, u32[]{:S(2)}) collective-permute-start(bf16[8,32,512]{2,1,0:T(8,128)(2,1)S(1)} %collective-permute-done.4.refs_8_), channel_id=1, source_target_pairs={{0,32},{32,64},{64,96},{96,128},{128,160},{160,192},{192,224},{224... | collective-permute-start | bytes 786440 | tf_op jit(solution)/shard_map/ppermute | solution.py:236
  55.0 9.0 %copy-start.8 = (bf16[8,32,512]{2,1,0:T(8,128)(2,1)}, bf16[8,32,512]{2,1,0:T(8,128)(2,1)S(1)}, u32[]{:S(2)}) copy-start(bf16[8,32,512]{2,1,0:T(8,128)(2,1)S(1)} %collective-permute-done.7.refs_7_) | copy-start | bytes 786436
  55.0 8.9 %collective-permute-start.8 = (bf16[8,32,512]{2,1,0:T(8,128)(2,1)S(1)}, bf16[8,32,512]{2,1,0:T(8,128)(2,1)S(1)}, u32[]{:S(2)}, u32[]{:S(2)}) collective-permute-start(bf16[8,32,512]{2,1,0:T(8,128)(2,1)S(1)} %collective-permute-done.7.refs_7_), channel_id=1, source_target_pairs={{0,224},{32,0},{64,32},{96,64},{128,96},{160,128},{192,160},{224,1... | collective-permute-start | bytes 786440 | tf_op jit(solution)/shard_map/ppermute | solution.py:239
  58.7 5.3 %copy-start.9 = (bf16[8,32,512]{2,1,0:T(8,128)(2,1)}, bf16[8,32,512]{2,1,0:T(8,128)(2,1)S(1)}, u32[]{:S(2)}) copy-start(bf16[8,32,512]{2,1,0:T(8,128)(2,1)S(1)} %collective-permute-done.1.refs_6_) | copy-start | bytes 786436
  58.7 8.2 %collective-permute-start.2 = (bf16[8,32,512]{2,1,0:T(8,128)(2,1)S(1)}, bf16[8,32,512]{2,1,0:T(8,128)(2,1)}, u32[]{:S(2)}, u32[]{:S(2)}) collective-permute-start(bf16[8,32,512]{2,1,0:T(8,128)(2,1)S(1)} %collective-permute-done.1.refs_6_), channel_id=1, source_target_pairs={{0,32},{32,64},{64,96},{96,128},{128,160},{160,192},{192,224},{224... | collective-permute-start | bytes 786440 | tf_op jit(solution)/shard_map/ppermute | solution.py:236
  60.5 3.5 %copy-start.10 = (bf16[8,32,512]{2,1,0:T(8,128)(2,1)}, bf16[8,32,512]{2,1,0:T(8,128)(2,1)S(1)}, u32[]{:S(2)}) copy-start(bf16[8,32,512]{2,1,0:T(8,128)(2,1)S(1)} %collective-permute-done.11.refs_13_) | copy-start | bytes 786436
  63.9 0.7 copy-start.11
  64.6 0.7 copy-start.12
  66.8 10.2 %collective-permute-start.12 = (bf16[8,6,64,512]{3,2,1,0:T(8,128)(2,1)S(1)}, bf16[8,6,64,512]{3,2,1,0:T(8,128)(2,1)}, u32[]{:S(2)}, u32[]{:S(2)}) collective-permute-start(bf16[8,6,64,512]{3,2,1,0:T(8,128)(2,1)S(1)} %bitcast.16), channel_id=1, source_target_pairs={{0,8},{8,0},{1,9},{9,1},{2,10},{10,2},{3,11},{11,3},{4,12},{12,4},... | collective-permute-start | bytes 9437192 | tf_op jit(solution)/shard_map/ppermute | solution.py:315
  66.8 10.1 %collective-permute-start.13 = (bf16[8,32,512]{2,1,0:T(8,128)(2,1)}, bf16[8,32,512]{2,1,0:T(8,128)(2,1)S(1)}, u32[]{:S(2)}, u32[]{:S(2)}) collective-permute-start(bf16[8,32,512]{2,1,0:T(8,128)(2,1)} %collective-permute-done.2.refs_10_), channel_id=1, source_target_pairs={{0,32},{32,64},{64,96},{96,128},{128,160},{160,192},{192,224},{224... | collective-permute-start | bytes 786440 | tf_op jit(solution)/shard_map/ppermute | solution.py:236
  66.8 10.1 %collective-permute-start.14 = (bf16[8,32,512]{2,1,0:T(8,128)(2,1)}, bf16[8,32,512]{2,1,0:T(8,128)(2,1)S(1)}, u32[]{:S(2)}, u32[]{:S(2)}) collective-permute-start(bf16[8,32,512]{2,1,0:T(8,128)(2,1)} %copy-done.10), channel_id=1, source_target_pairs={{0,224},{32,0},{64,32},{96,64},{128,96},{160,128},{192,160},{224,1... | collective-permute-start | bytes 786440 | tf_op jit(solution)/shard_map/ppermute | solution.py:239
  83.1 2.1 %collective-permute-start.15 = (f32[1152,128]{1,0:T(8,128)S(1)}, f32[1152,128]{1,0:T(8,128)S(1)}, u32[]{:S(2)}, u32[]{:S(2)}) collective-permute-start(f32[1152,128]{1,0:T(8,128)S(1)} %get-tuple-element.17), channel_id=1, source_target_pairs={{0,8},{8,0},{1,9},{9,1},{2,10},{10,2},{3,11},{11,3},{4,12},{12,4},... | collective-permute-start | bytes 1769480 | tf_op jit(solution)/shard_map/ppermute | solution.py:318
  86.1 19.0 %all-to-all-start.2 = ((f32[1152,1,128]{2,1,0:T(1,128)}), f32[1152,1,128]{2,1,0:T(1,128)S(1)}, u32[]{:S(2)}, u32[]{:S(2)}) async-start(f32[1152,1,128]{2,1,0:T(1,128)} %bitcast.7), calls=%async_computation.2 | async-start | bytes 1179648 | tf_op jit(solution)/shard_map/all_to_all | solution.py:293
  105.7 12.3 %all-to-all-start.3 = ((f32[72,1,128]{2,1,0:T(1,128)}), f32[72,1,128]{2,1,0:T(1,128)S(1)}, u32[]{:S(2)}, u32[]{:S(2)}) async-start(f32[72,1,128]{2,1,0:T(1,128)} %bitcast.22), calls=%async_computation.3 | async-start | bytes 73728 | tf_op jit(solution)/shard_map/all_to_all | solution.py:293

commit v4 on v3

--- a/solution.py
+++ b/solution.py
@@ -10,7 +10,7 @@
 ROW = ("y", "xh")
 AUX = ("z", "xl", "c")
 A_PASS = 8
-UNROLL = 4
+UNROLL = 8
 
 
 def pick_kernel(copies, width, col_ref, count_ref, coef_ref, out_ref):
@@ -308,6 +308,7 @@
     integrals = three_center.reshape(nq, height, width)
     picks = lax.all_to_all(picks, ("xl",) + ROW, 0, 0, tiled=True)
     chunks = [picks[n * nrow : (n + 1) * nrow] for n in range(nxl)]
+    integrals, chunks = lax.optimization_barrier((integrals, chunks))
     own = lax.all_to_all(integrals, ROW, 0, 0, tiled=True)
     arrived, own = ring(chunks, "z", nz, own, 4)
     blocks = chunks + arrived

time: 120 us -> 119 us (level)
  no operation moved by 1% of the time
where the time goes in v4:
time: 119 us
  starting transfers between devices  43.4 us (36%)
  waiting for transfers between devices  37.9 us (32%)
  blocking collectives  17.2 us (14%)
  Pallas kernels  15.5 us (13%)
  local copies, waits for them, and re-layouts  2.08 us (2%)
  other arithmetic  1.51 us (1%)
  between operations  1.41 us (1%)
    ppermute x7, starting transfers between devices, ring(): lefts[n] = lax.ppermute(lefts[n], axis, down)  27 us
    all_to_all x2, waiting for transfers between devices, turn(): rows = lax.all_to_all(rows, axes, 0, 0, tiled=True)  18.1 us
    all_to_all x1, blocking collectives, local(): picks = lax.all_to_all(picks, ('xl',) + ROW, 0, 0, tiled=True)  17.2 us
    all_to_all x2, starting transfers between devices, turn(): rows = lax.all_to_all(rows, axes, 0, 0, tiled=True)  12.6 us
    ppermute x7, waiting for transfers between devices, ring(): lefts[n] = lax.ppermute(lefts[n], axis, down)  11.4 us
    ppermute x7, waiting for transfers between devices, ring(): rights[n] = lax.ppermute(rights[n], axis, up)  6.47 us
    pallas_call x1, Pallas kernels, exchange(): pl.pallas_call(functools.partial(late_kernel, *sizes), out_shape=(shape,...  6.09 us
    pallas_call x1, Pallas kernels, exchange(): pl.pallas_call(early_kernel, out_shape=(jax.ShapeDtypeStruct((rows, rows)...  5.35 us
  transfers between devices with their start and end apart: 19, of which 11 were waited for; matrix products, arithmetic and copies ran while one was open for 1% of the time, Pallas kernels for 5%

profile of v4, /device:TPU:2, one launch (start us, length us, event | category | flops | bytes accessed | tf_op | source)
XLA Modules:
  0.0 118.9 jit_solution(1039026272334627109)
XLA Ops:
  1.3 2.1 %pick.1 = bf16[16,32,512]{2,1,0:T(8,128)(2,1)} custom-call(s32[8]{0:T(128)} %bitcast.23, s32[1]{0:T(128)S(6)} %copy.8.count_ref, bf16[32,10240]{1,0:T(8,128)(2,1)} %coef_ref.1), custom_call_target="tpu_custom_call" | custom-call | tf_op jit(solution)/shard_map/pick/pallas_call | solution.py:38
  3.3 17.2 %all_to_all.20 = bf16[16,32,512]{2,1,0:T(8,128)(2,1)S(1)} all-to-all(bf16[16,32,512]{2,1,0:T(8,128)(2,1)} %pick.1), channel_id=1, replica_groups=mesh['z'=8,'xl'=2,'c'=2,'y'=4,'xh'=2] {'xl','y','xh'}, dimensions={0} | all-to-all | bytes 1048576 | tf_op jit(solution)/shard_map/all_to_all | solution.py:309
  20.5 0.7 fusion
  21.2 3.7 %all-to-all-start.1 = ((bf16[48,64,512]{2,1,0:T(8,128)(2,1)}), bf16[48,64,512]{2,1,0:T(8,128)(2,1)S(1)}, u32[]{:S(2)}, u32[]{:S(2)}) async-start(bf16[48,64,512]{2,1,0:T(8,128)(2,1)} %bitcast.21), calls=%async_computation.1 | async-start | bytes 6291456 | tf_op jit(solution)/shard_map/all_to_all | solution.py:312
  24.9 5.9 %collective-permute-start.6 = (bf16[8,32,512]{2,1,0:T(8,128)(2,1)}, bf16[8,32,512]{2,1,0:T(8,128)(2,1)S(1)}, u32[]{:S(2)}, u32[]{:S(2)}) collective-permute-start(bf16[8,32,512]{2,1,0:T(8,128)(2,1)} %get-tuple-element.14.refs_0_), channel_id=1, source_target_pairs={{0,224},{32,0},{64,32},{96,64},{128,96},{160,128},{192,160},{224,1... | collective-permute-start | bytes 786440 | tf_op jit(solution)/shard_map/ppermute | solution.py:239
  30.9 3.2 %collective-permute-start.9 = (bf16[8,32,512]{2,1,0:T(8,128)(2,1)S(1)}, bf16[8,32,512]{2,1,0:T(8,128)(2,1)S(1)}, u32[]{:S(2)}, u32[]{:S(2)}) collective-permute-start(bf16[8,32,512]{2,1,0:T(8,128)(2,1)S(1)} %get-tuple-element.15.refs_1_), channel_id=1, source_target_pairs={{0,224},{32,0},{64,32},{96,64},{128,96},{160,128},{192,160},{224,1... | collective-permute-start | bytes 786440 | tf_op jit(solution)/shard_map/ppermute | solution.py:239
  34.1 3.8 %collective-permute-done.6.refs_3_ = bf16[8,32,512]{2,1,0:T(8,128)(2,1)S(1)} collective-permute-done((bf16[8,32,512]{2,1,0:T(8,128)(2,1)}, bf16[8,32,512]{2,1,0:T(8,128)(2,1)S(1)}, u32[]{:S(2)}, u32[]{:S(2)}) %collective-permute-start.6) | collective-permute-done | bytes 262176 | tf_op jit(solution)/shard_map/ppermute | solution.py:239
  37.9 3.6 %collective-permute-start.7 = (bf16[8,32,512]{2,1,0:T(8,128)(2,1)S(1)}, bf16[8,32,512]{2,1,0:T(8,128)(2,1)S(1)}, u32[]{:S(2)}, u32[]{:S(2)}) collective-permute-start(bf16[8,32,512]{2,1,0:T(8,128)(2,1)S(1)} %collective-permute-done.6.refs_3_), channel_id=1, source_target_pairs={{0,224},{32,0},{64,32},{96,64},{128,96},{160,128},{192,160},{224,1... | collective-permute-start | bytes 786440 | tf_op jit(solution)/shard_map/ppermute | solution.py:239
  41.5 1.9 %collective-permute-done.9.refs_5_ = bf16[8,32,512]{2,1,0:T(8,128)(2,1)S(1)} collective-permute-done((bf16[8,32,512]{2,1,0:T(8,128)(2,1)S(1)}, bf16[8,32,512]{2,1,0:T(8,128)(2,1)S(1)}, u32[]{:S(2)}, u32[]{:S(2)}) %collective-permute-start.9) | collective-permute-done | bytes 262176 | tf_op jit(solution)/shard_map/ppermute | solution.py:239
  43.4 3.7 %collective-permute-start.10 = (bf16[8,32,512]{2,1,0:T(8,128)(2,1)S(1)}, bf16[8,32,512]{2,1,0:T(8,128)(2,1)S(1)}, u32[]{:S(2)}, u32[]{:S(2)}) collective-permute-start(bf16[8,32,512]{2,1,0:T(8,128)(2,1)S(1)} %collective-permute-done.9.refs_5_), channel_id=1, source_target_pairs={{0,224},{32,0},{64,32},{96,64},{128,96},{160,128},{192,160},{224,1... | collective-permute-start | bytes 786440 | tf_op jit(solution)/shard_map/ppermute | solution.py:239
  47.1 1.9 %collective-permute-done.7.refs_7_ = bf16[8,32,512]{2,1,0:T(8,128)(2,1)S(1)} collective-permute-done((bf16[8,32,512]{2,1,0:T(8,128)(2,1)S(1)}, bf16[8,32,512]{2,1,0:T(8,128)(2,1)S(1)}, u32[]{:S(2)}, u32[]{:S(2)}) %collective-permute-start.7) | collective-permute-done | bytes 262176 | tf_op jit(solution)/shard_map/ppermute | solution.py:239
  49.1 3.7 %collective-permute-start.8 = (bf16[8,32,512]{2,1,0:T(8,128)(2,1)S(1)}, bf16[8,32,512]{2,1,0:T(8,128)(2,1)S(1)}, u32[]{:S(2)}, u32[]{:S(2)}) collective-permute-start(bf16[8,32,512]{2,1,0:T(8,128)(2,1)S(1)} %collective-permute-done.7.refs_7_), channel_id=1, source_target_pairs={{0,224},{32,0},{64,32},{96,64},{128,96},{160,128},{192,160},{224,1... | collective-permute-start | bytes 786440 | tf_op jit(solution)/shard_map/ppermute | solution.py:239
  52.8 1.9 %collective-permute-done.10.refs_9_ = bf16[8,32,512]{2,1,0:T(8,128)(2,1)S(1)} collective-permute-done((bf16[8,32,512]{2,1,0:T(8,128)(2,1)S(1)}, bf16[8,32,512]{2,1,0:T(8,128)(2,1)S(1)}, u32[]{:S(2)}, u32[]{:S(2)}) %collective-permute-start.10) | collective-permute-done | bytes 262176 | tf_op jit(solution)/shard_map/ppermute | solution.py:239
  54.7 3.7 %collective-permute-start.11 = (bf16[8,32,512]{2,1,0:T(8,128)(2,1)S(1)}, bf16[8,32,512]{2,1,0:T(8,128)(2,1)S(1)}, u32[]{:S(2)}, u32[]{:S(2)}) collective-permute-start(bf16[8,32,512]{2,1,0:T(8,128)(2,1)S(1)} %collective-permute-done.10.refs_9_), channel_id=1, source_target_pairs={{0,224},{32,0},{64,32},{96,64},{128,96},{160,128},{192,160},{224,1... | collective-permute-start | bytes 786440 | tf_op jit(solution)/shard_map/ppermute | solution.py:239
  58.4 1.8 %collective-permute-done.8.refs_11_ = bf16[8,32,512]{2,1,0:T(8,128)(2,1)S(1)} collective-permute-done((bf16[8,32,512]{2,1,0:T(8,128)(2,1)S(1)}, bf16[8,32,512]{2,1,0:T(8,128)(2,1)S(1)}, u32[]{:S(2)}, u32[]{:S(2)}) %collective-permute-start.8) | collective-permute-done | bytes 262176 | tf_op jit(solution)/shard_map/ppermute | solution.py:239
  60.2 3.4 %collective-permute-done.2.refs_10_ = bf16[8,32,512]{2,1,0:T(8,128)(2,1)S(1)} collective-permute-done((bf16[8,32,512]{2,1,0:T(8,128)(2,1)S(1)}, bf16[8,32,512]{2,1,0:T(8,128)(2,1)S(1)}, u32[]{:S(2)}, u32[]{:S(2)}) %collective-permute-start.2) | collective-permute-done | bytes 262176 | tf_op jit(solution)/shard_map/ppermute | solution.py:236
  63.7 0.6 copy-done.10
  64.3 0.7 copy-done.11
  65.0 1.5 %collective-permute-done.5.refs_12_ = bf16[8,32,512]{2,1,0:T(8,128)(2,1)} collective-permute-done((bf16[8,32,512]{2,1,0:T(8,128)(2,1)S(1)}, bf16[8,32,512]{2,1,0:T(8,128)(2,1)}, u32[]{:S(2)}, u32[]{:S(2)}) %collective-permute-start.5) | collective-permute-done | bytes 262176 | tf_op jit(solution)/shard_map/ppermute | solution.py:236
  66.5 3.2 %collective-permute-start.14 = (bf16[8,32,512]{2,1,0:T(8,128)(2,1)}, bf16[8,32,512]{2,1,0:T(8,128)(2,1)S(1)}, u32[]{:S(2)}, u32[]{:S(2)}) collective-permute-start(bf16[8,32,512]{2,1,0:T(8,128)(2,1)} %copy-done.11), channel_id=1, source_target_pairs={{0,224},{32,0},{64,32},{96,64},{128,96},{160,128},{192,160},{224,1... | collective-permute-start | bytes 786440 | tf_op jit(solution)/shard_map/ppermute | solution.py:239
  69.7 5.4 %early.1 = (f32[512,512]{1,0:T(8,128)S(1)}, bf16[14,8,32,512]{3,2,1,0:T(8,128)(2,1)S(1)}) custom-call(bf16[8,6,64,512]{3,2,1,0:T(8,128)(2,1)S(1)} %bitcast.17, bf16[8,32,512]{2,1,0:T(8,128)(2,1)} %get-tuple-element.14.refs_0_, bf16[8,32,512]{2,1,0:T(8,128)(2,1)} %copy-done, bf16[8,32,512]{2,1,0:T(8,128)(2,1)} %copy-done.2, bf16[8,32,512]{2,1,0:T(8,128)(2,1)} %copy-done.1, ...), custom_call_target="tpu_custom_call" | custom-call | flops 2818572288 | bytes 1048576 | tf_op jit(solution)/shard_map/early/pallas_call | solution.py:189
  75.1 1.5 %collective-permute-done.13.refs_0_ = bf16[8,32,512]{2,1,0:T(8,128)(2,1)S(1)} collective-permute-done((bf16[8,32,512]{2,1,0:T(8,128)(2,1)}, bf16[8,32,512]{2,1,0:T(8,128)(2,1)S(1)}, u32[]{:S(2)}, u32[]{:S(2)}) %collective-permute-start.13) | collective-permute-done | bytes 262176 | tf_op jit(solution)/shard_map/ppermute | solution.py:236
  76.6 6.1 %late.1 = (f32[1152,128]{1,0:T(8,128)S(1)}, f32[1152,128]{1,0:T(8,128)S(1)}) custom-call(s32[1]{0:T(128)} %bitcast.2.core_ref, bf16[8,6,64,512]{3,2,1,0:T(8,128)(2,1)S(1)} %bitcast.18, f32[512,512]{1,0:T(8,128)S(1)} %get-tuple-element.18.early_ref, bf16[14,8,32,512]{3,2,1,0:T(8,128)(2,1)S(1)} %get-tuple-element.19.held, ...), custom_call_target="tpu_custom_call" | custom-call | flops 3623878656 | bytes 1048576 | tf_op jit(solution)/shard_map/late/pallas_call | solution.py:208
  82.8 2.0 %collective-permute-done.15 = f32[1152,128]{1,0:T(8,128)S(1)} collective-permute-done((f32[1152,128]{1,0:T(8,128)S(1)}, f32[1152,128]{1,0:T(8,128)S(1)}, u32[]{:S(2)}, u32[]{:S(2)}) %collective-permute-start.15) | collective-permute-done | bytes 589856 | tf_op jit(solution)/shard_map/ppermute | solution.py:319
  84.8 0.9 add.15
  85.7 8.3 %all-to-all-start.2 = ((f32[1152,1,128]{2,1,0:T(1,128)}), f32[1152,1,128]{2,1,0:T(1,128)S(1)}, u32[]{:S(2)}, u32[]{:S(2)}) async-start(f32[1152,1,128]{2,1,0:T(1,128)} %bitcast.7), calls=%async_computation.2 | async-start | bytes 1179648 | tf_op jit(solution)/shard_map/all_to_all | solution.py:293
  94.0 10.6 %all-to-all-done.2 = f32[1152,1,128]{2,1,0:T(1,128)S(1)} async-done(((f32[1152,1,128]{2,1,0:T(1,128)}), f32[1152,1,128]{2,1,0:T(1,128)S(1)}, u32[]{:S(2)}, u32[]{:S(2)}) %all-to-all-start.2) | async-done | bytes 589856 | tf_op jit(solution)/shard_map/all_to_all | solution.py:293
  104.7 0.6 summed.1
  105.3 4.2 %all-to-all-start.3 = ((f32[72,1,128]{2,1,0:T(1,128)}), f32[72,1,128]{2,1,0:T(1,128)S(1)}, u32[]{:S(2)}, u32[]{:S(2)}) async-start(f32[72,1,128]{2,1,0:T(1,128)} %bitcast.22), calls=%async_computation.3 | async-start | bytes 73728 | tf_op jit(solution)/shard_map/all_to_all | solution.py:293
  109.5 0.6 pad_add_fusion.place_ref
  110.2 7.4 %all-to-all-done.3 = f32[72,1,128]{2,1,0:T(1,128)S(1)} async-done(((f32[72,1,128]{2,1,0:T(1,128)}), f32[72,1,128]{2,1,0:T(1,128)S(1)}, u32[]{:S(2)}, u32[]{:S(2)}) %all-to-all-start.3) | async-done | bytes 36896 | tf_op jit(solution)/shard_map/all_to_all | solution.py:293
  117.6 1.3 %finish.1 = (f32[16,64]{1,0:T(8,128)}, f32[1,64]{1,0:T(1,128)}) custom-call(s32[2]{0:T(128)} %pad_add_fusion.place_ref, f32[72,128]{1,0:T(8,128)S(1)} %bitcast.20), custom_call_target="tpu_custom_call" | custom-call | tf_op jit(solution)/shard_map/finish/pallas_call | solution.py:279
  (39 shorter events, 0.2 us)
Async XLA Ops:
  21.2 12.8 %copy-start = (bf16[8,32,512]{2,1,0:T(8,128)(2,1)}, bf16[8,32,512]{2,1,0:T(8,128)(2,1)S(1)}, u32[]{:S(2)}) copy-start(bf16[8,32,512]{2,1,0:T(8,128)(2,1)S(1)} %get-tuple-element.15.refs_1_) | copy-start | bytes 786436
  21.2 45.2 %all-to-all-start.1 = ((bf16[48,64,512]{2,1,0:T(8,128)(2,1)}), bf16[48,64,512]{2,1,0:T(8,128)(2,1)S(1)}, u32[]{:S(2)}, u32[]{:S(2)}) async-start(bf16[48,64,512]{2,1,0:T(8,128)(2,1)} %bitcast.21), calls=%async_computation.1 | async-start | bytes 6291456 | tf_op jit(solution)/shard_map/all_to_all | solution.py:312
  24.9 13.0 %collective-permute-start.6 = (bf16[8,32,512]{2,1,0:T(8,128)(2,1)}, bf16[8,32,512]{2,1,0:T(8,128)(2,1)S(1)}, u32[]{:S(2)}, u32[]{:S(2)}) collective-permute-start(bf16[8,32,512]{2,1,0:T(8,128)(2,1)} %get-tuple-element.14.refs_0_), channel_id=1, source_target_pairs={{0,224},{32,0},{64,32},{96,64},{128,96},{160,128},{192,160},{224,1... | collective-permute-start | bytes 786440 | tf_op jit(solution)/shard_map/ppermute | solution.py:239
  30.9 10.7 %collective-permute-start = (bf16[8,32,512]{2,1,0:T(8,128)(2,1)}, bf16[8,32,512]{2,1,0:T(8,128)(2,1)S(1)}, u32[]{:S(2)}, u32[]{:S(2)}) collective-permute-start(bf16[8,32,512]{2,1,0:T(8,128)(2,1)} %get-tuple-element.14.refs_0_), channel_id=1, source_target_pairs={{0,32},{32,64},{64,96},{96,128},{128,160},{160,192},{192,224},{224... | collective-permute-start | bytes 786440 | tf_op jit(solution)/shard_map/ppermute | solution.py:236
  30.9 12.6 %collective-permute-start.9 = (bf16[8,32,512]{2,1,0:T(8,128)(2,1)S(1)}, bf16[8,32,512]{2,1,0:T(8,128)(2,1)S(1)}, u32[]{:S(2)}, u32[]{:S(2)}) collective-permute-start(bf16[8,32,512]{2,1,0:T(8,128)(2,1)S(1)} %get-tuple-element.15.refs_1_), channel_id=1, source_target_pairs={{0,224},{32,0},{64,32},{96,64},{128,96},{160,128},{192,160},{224,1... | collective-permute-start | bytes 786440 | tf_op jit(solution)/shard_map/ppermute | solution.py:239
  34.1 13.0 %collective-permute-start.3 = (bf16[8,32,512]{2,1,0:T(8,128)(2,1)S(1)}, bf16[8,32,512]{2,1,0:T(8,128)(2,1)S(1)}, u32[]{:S(2)}, u32[]{:S(2)}) collective-permute-start(bf16[8,32,512]{2,1,0:T(8,128)(2,1)S(1)} %get-tuple-element.15.refs_1_), channel_id=1, source_target_pairs={{0,32},{32,64},{64,96},{96,128},{128,160},{160,192},{192,224},{224... | collective-permute-start | bytes 786440 | tf_op jit(solution)/shard_map/ppermute | solution.py:236
  37.9 25.7 %copy-start.1 = (bf16[8,32,512]{2,1,0:T(8,128)(2,1)}, bf16[8,32,512]{2,1,0:T(8,128)(2,1)S(1)}, u32[]{:S(2)}) copy-start(bf16[8,32,512]{2,1,0:T(8,128)(2,1)S(1)} %collective-permute-done.6.refs_3_) | copy-start | bytes 786436
  37.9 11.1 %collective-permute-start.7 = (bf16[8,32,512]{2,1,0:T(8,128)(2,1)S(1)}, bf16[8,32,512]{2,1,0:T(8,128)(2,1)S(1)}, u32[]{:S(2)}, u32[]{:S(2)}) collective-permute-start(bf16[8,32,512]{2,1,0:T(8,128)(2,1)S(1)} %collective-permute-done.6.refs_3_), channel_id=1, source_target_pairs={{0,224},{32,0},{64,32},{96,64},{128,96},{160,128},{192,160},{224,1... | collective-permute-start | bytes 786440 | tf_op jit(solution)/shard_map/ppermute | solution.py:239
  41.5 22.1 %copy-start.2 = (bf16[8,32,512]{2,1,0:T(8,128)(2,1)}, bf16[8,32,512]{2,1,0:T(8,128)(2,1)S(1)}, u32[]{:S(2)}) copy-start(bf16[8,32,512]{2,1,0:T(8,128)(2,1)S(1)} %collective-permute-done.refs_2_) | copy-start | bytes 786436
  41.5 11.2 %collective-permute-start.1 = (bf16[8,32,512]{2,1,0:T(8,128)(2,1)S(1)}, bf16[8,32,512]{2,1,0:T(8,128)(2,1)S(1)}, u32[]{:S(2)}, u32[]{:S(2)}) collective-permute-start(bf16[8,32,512]{2,1,0:T(8,128)(2,1)S(1)} %collective-permute-done.refs_2_), channel_id=1, source_target_pairs={{0,32},{32,64},{64,96},{96,128},{128,160},{160,192},{192,224},{224... | collective-permute-start | bytes 786440 | tf_op jit(solution)/shard_map/ppermute | solution.py:236
  43.4 20.2 %copy-start.3 = (bf16[8,32,512]{2,1,0:T(8,128)(2,1)}, bf16[8,32,512]{2,1,0:T(8,128)(2,1)S(1)}, u32[]{:S(2)}) copy-start(bf16[8,32,512]{2,1,0:T(8,128)(2,1)S(1)} %collective-permute-done.9.refs_5_) | copy-start | bytes 786436
  43.4 11.2 %collective-permute-start.10 = (bf16[8,32,512]{2,1,0:T(8,128)(2,1)S(1)}, bf16[8,32,512]{2,1,0:T(8,128)(2,1)S(1)}, u32[]{:S(2)}, u32[]{:S(2)}) collective-permute-start(bf16[8,32,512]{2,1,0:T(8,128)(2,1)S(1)} %collective-permute-done.9.refs_5_), channel_id=1, source_target_pairs={{0,224},{32,0},{64,32},{96,64},{128,96},{160,128},{192,160},{224,1... | collective-permute-start | bytes 786440 | tf_op jit(solution)/shard_map/ppermute | solution.py:239
  47.1 16.5 %copy-start.4 = (bf16[8,32,512]{2,1,0:T(8,128)(2,1)}, bf16[8,32,512]{2,1,0:T(8,128)(2,1)S(1)}, u32[]{:S(2)}) copy-start(bf16[8,32,512]{2,1,0:T(8,128)(2,1)S(1)} %collective-permute-done.3.refs_4_) | copy-start | bytes 786436
  47.1 11.2 %collective-permute-start.4 = (bf16[8,32,512]{2,1,0:T(8,128)(2,1)S(1)}, bf16[8,32,512]{2,1,0:T(8,128)(2,1)S(1)}, u32[]{:S(2)}, u32[]{:S(2)}) collective-permute-start(bf16[8,32,512]{2,1,0:T(8,128)(2,1)S(1)} %collective-permute-done.3.refs_4_), channel_id=1, source_target_pairs={{0,32},{32,64},{64,96},{96,128},{128,160},{160,192},{192,224},{224... | collective-permute-start | bytes 786440 | tf_op jit(solution)/shard_map/ppermute | solution.py:236
  49.1 14.6 %copy-start.5 = (bf16[8,32,512]{2,1,0:T(8,128)(2,1)}, bf16[8,32,512]{2,1,0:T(8,128)(2,1)S(1)}, u32[]{:S(2)}) copy-start(bf16[8,32,512]{2,1,0:T(8,128)(2,1)S(1)} %collective-permute-done.7.refs_7_) | copy-start | bytes 786436
  49.1 11.1 %collective-permute-start.8 = (bf16[8,32,512]{2,1,0:T(8,128)(2,1)S(1)}, bf16[8,32,512]{2,1,0:T(8,128)(2,1)S(1)}, u32[]{:S(2)}, u32[]{:S(2)}) collective-permute-start(bf16[8,32,512]{2,1,0:T(8,128)(2,1)S(1)} %collective-permute-done.7.refs_7_), channel_id=1, source_target_pairs={{0,224},{32,0},{64,32},{96,64},{128,96},{160,128},{192,160},{224,1... | collective-permute-start | bytes 786440 | tf_op jit(solution)/shard_map/ppermute | solution.py:239
  52.8 10.9 %copy-start.6 = (bf16[8,32,512]{2,1,0:T(8,128)(2,1)}, bf16[8,32,512]{2,1,0:T(8,128)(2,1)S(1)}, u32[]{:S(2)}) copy-start(bf16[8,32,512]{2,1,0:T(8,128)(2,1)S(1)} %collective-permute-done.1.refs_6_) | copy-start | bytes 786436
  52.8 10.8 %collective-permute-start.2 = (bf16[8,32,512]{2,1,0:T(8,128)(2,1)S(1)}, bf16[8,32,512]{2,1,0:T(8,128)(2,1)S(1)}, u32[]{:S(2)}, u32[]{:S(2)}) collective-permute-start(bf16[8,32,512]{2,1,0:T(8,128)(2,1)S(1)} %collective-permute-done.1.refs_6_), channel_id=1, source_target_pairs={{0,32},{32,64},{64,96},{96,128},{128,160},{160,192},{192,224},{224... | collective-permute-start | bytes 786440 | tf_op jit(solution)/shard_map/ppermute | solution.py:236
  54.7 9.0 %copy-start.7 = (bf16[8,32,512]{2,1,0:T(8,128)(2,1)}, bf16[8,32,512]{2,1,0:T(8,128)(2,1)S(1)}, u32[]{:S(2)}) copy-start(bf16[8,32,512]{2,1,0:T(8,128)(2,1)S(1)} %collective-permute-done.10.refs_9_) | copy-start | bytes 786436
  54.7 8.9 %collective-permute-start.11 = (bf16[8,32,512]{2,1,0:T(8,128)(2,1)S(1)}, bf16[8,32,512]{2,1,0:T(8,128)(2,1)S(1)}, u32[]{:S(2)}, u32[]{:S(2)}) collective-permute-start(bf16[8,32,512]{2,1,0:T(8,128)(2,1)S(1)} %collective-permute-done.10.refs_9_), channel_id=1, source_target_pairs={{0,224},{32,0},{64,32},{96,64},{128,96},{160,128},{192,160},{224,1... | collective-permute-start | bytes 786440 | tf_op jit(solution)/shard_map/ppermute | solution.py:239
  58.4 11.4 %copy-start.8 = (bf16[8,32,512]{2,1,0:T(8,128)(2,1)}, bf16[8,32,512]{2,1,0:T(8,128)(2,1)S(1)}, u32[]{:S(2)}) copy-start(bf16[8,32,512]{2,1,0:T(8,128)(2,1)S(1)} %collective-permute-done.4.refs_8_) | copy-start | bytes 786436
  58.4 8.1 %collective-permute-start.5 = (bf16[8,32,512]{2,1,0:T(8,128)(2,1)S(1)}, bf16[8,32,512]{2,1,0:T(8,128)(2,1)}, u32[]{:S(2)}, u32[]{:S(2)}) collective-permute-start(bf16[8,32,512]{2,1,0:T(8,128)(2,1)S(1)} %collective-permute-done.4.refs_8_), channel_id=1, source_target_pairs={{0,32},{32,64},{64,96},{96,128},{128,160},{160,192},{192,224},{224... | collective-permute-start | bytes 786440 | tf_op jit(solution)/shard_map/ppermute | solution.py:236
  60.2 3.5 %copy-start.9 = (bf16[8,32,512]{2,1,0:T(8,128)(2,1)}, bf16[8,32,512]{2,1,0:T(8,128)(2,1)S(1)}, u32[]{:S(2)}) copy-start(bf16[8,32,512]{2,1,0:T(8,128)(2,1)S(1)} %collective-permute-done.8.refs_11_) | copy-start | bytes 786436
  63.6 0.7 copy-start.10
  64.3 0.7 copy-start.11
  66.5 10.2 %collective-permute-start.12 = (bf16[8,6,64,512]{3,2,1,0:T(8,128)(2,1)S(1)}, bf16[8,6,64,512]{3,2,1,0:T(8,128)(2,1)}, u32[]{:S(2)}, u32[]{:S(2)}) collective-permute-start(bf16[8,6,64,512]{3,2,1,0:T(8,128)(2,1)S(1)} %bitcast.16), channel_id=1, source_target_pairs={{0,8},{8,0},{1,9},{9,1},{2,10},{10,2},{3,11},{11,3},{4,12},{12,4},... | collective-permute-start | bytes 9437192 | tf_op jit(solution)/shard_map/ppermute | solution.py:316
  66.5 10.1 %collective-permute-start.13 = (bf16[8,32,512]{2,1,0:T(8,128)(2,1)}, bf16[8,32,512]{2,1,0:T(8,128)(2,1)S(1)}, u32[]{:S(2)}, u32[]{:S(2)}) collective-permute-start(bf16[8,32,512]{2,1,0:T(8,128)(2,1)} %copy-done.10), channel_id=1, source_target_pairs={{0,32},{32,64},{64,96},{96,128},{128,160},{160,192},{192,224},{224... | collective-permute-start | bytes 786440 | tf_op jit(solution)/shard_map/ppermute | solution.py:236
  66.5 10.1 %collective-permute-start.14 = (bf16[8,32,512]{2,1,0:T(8,128)(2,1)}, bf16[8,32,512]{2,1,0:T(8,128)(2,1)S(1)}, u32[]{:S(2)}, u32[]{:S(2)}) collective-permute-start(bf16[8,32,512]{2,1,0:T(8,128)(2,1)} %copy-done.11), channel_id=1, source_target_pairs={{0,224},{32,0},{64,32},{96,64},{128,96},{160,128},{192,160},{224,1... | collective-permute-start | bytes 786440 | tf_op jit(solution)/shard_map/ppermute | solution.py:239
  82.7 2.1 %collective-permute-start.15 = (f32[1152,128]{1,0:T(8,128)S(1)}, f32[1152,128]{1,0:T(8,128)S(1)}, u32[]{:S(2)}, u32[]{:S(2)}) collective-permute-start(f32[1152,128]{1,0:T(8,128)S(1)} %get-tuple-element.23), channel_id=1, source_target_pairs={{0,8},{8,0},{1,9},{9,1},{2,10},{10,2},{3,11},{11,3},{4,12},{12,4},... | collective-permute-start | bytes 1769480 | tf_op jit(solution)/shard_map/ppermute | solution.py:319
  85.7 19.0 %all-to-all-start.2 = ((f32[1152,1,128]{2,1,0:T(1,128)}), f32[1152,1,128]{2,1,0:T(1,128)S(1)}, u32[]{:S(2)}, u32[]{:S(2)}) async-start(f32[1152,1,128]{2,1,0:T(1,128)} %bitcast.7), calls=%async_computation.2 | async-start | bytes 1179648 | tf_op jit(solution)/shard_map/all_to_all | solution.py:293
  105.3 12.3 %all-to-all-start.3 = ((f32[72,1,128]{2,1,0:T(1,128)}), f32[72,1,128]{2,1,0:T(1,128)S(1)}, u32[]{:S(2)}, u32[]{:S(2)}) async-start(f32[72,1,128]{2,1,0:T(1,128)} %bitcast.22), calls=%async_computation.3 | async-start | bytes 73728 | tf_op jit(solution)/shard_map/all_to_all | solution.py:293

commit v5 on v4

--- a/solution.py
+++ b/solution.py
@@ -106,23 +106,32 @@
     lower_products(half, add)
 
 
-def late_kernel(nz, nxl, ncore, core_ref, own_ref, early_ref, held, other_ref, *refs):
-    *blocks, keep_ref, send_ref, other, other_sem, last, sem, half, total = refs
-    rows = total.shape[0]
-    ntiles, nq, height, _ = own_ref.shape
-    copies = copies_of(blocks, last, sem)
-    parts = [pltpu.make_async_copy(other_ref.at[t], other.at[t], other_sem.at[t]) for t in range(ntiles)]
+def middle_kernel(early_ref, held, other_ref, total_ref, other, sem, half):
+    ntiles = other.shape[0]
+    parts = [pltpu.make_async_copy(other_ref.at[t], other.at[t], sem.at[t]) for t in range(ntiles)]
     for copy in parts:
         copy.start()
+    for low in range(0, ntiles, ntiles // 2):
+        for copy in parts[low : low + ntiles // 2]:
+            copy.wait()
+        half_rows(other, [held.at[:A_PASS]], 0, half, (low, low + ntiles // 2))
+
+    def add(rows, cols, block):
+        total_ref[rows, cols] = block + early_ref[rows, cols]
+
+    lower_products(half, add)
+
+
+def late_kernel(nz, nxl, ncore, core_ref, own_ref, early_ref, held, other_ref, *refs):
+    *blocks, keep_ref, send_ref, last, sem, half, total = refs
+    rows = total.shape[0]
+    ntiles, _, height, _ = own_ref.shape
+    copies = copies_of(blocks, last, sem)
+    everything = (0, ntiles)
     for copy in copies:
         copy.wait()
-    base = half_rows(own_ref, [last], 0, half, (0, ntiles))
-    for low in range(0, ntiles, UNROLL):
-        tiles = (low, low + UNROLL)
-        for copy in parts[low : low + UNROLL]:
-            copy.wait()
-        middle = half_rows(other, [held.at[:A_PASS]], base, half, tiles)
-        half_rows(other, [held.at[A_PASS : held.shape[0]], last], middle, half, tiles)
+    base = half_rows(own_ref, [last], 0, half, everything)
+    half_rows(other_ref, [held.at[A_PASS : held.shape[0]], last], base, half, everything)
 
     def add(rows, cols, block):
         block = block + early_ref[rows, cols]
@@ -203,16 +212,28 @@
     )(own, *blocks[:rest])
     total = pltpu.with_memory_space_constraint(total, pltpu.VMEM)
     held = pltpu.with_memory_space_constraint(held, pltpu.VMEM)
+    total, other = pl.pallas_call(
+        middle_kernel,
+        out_shape=(jax.ShapeDtypeStruct(total.shape, total.dtype), jax.ShapeDtypeStruct(other.shape, other.dtype)),
+        in_specs=[whole] * 2 + anywhere(1),
+        out_specs=[whole] * 2,
+        scratch_shapes=[
+            pltpu.SemaphoreType.DMA((ntiles,)),
+            pltpu.VMEM((rows, nq * A_PASS * norb), jnp.bfloat16),
+        ],
+        name="middle",
+        **settings(A_PASS),
+    )(total, held, other)
+    total = pltpu.with_memory_space_constraint(total, pltpu.VMEM)
+    other = pltpu.with_memory_space_constraint(other, pltpu.VMEM)
     shape = jax.ShapeDtypeStruct((messages * (cols // 2 + 1), 2 * height), jnp.float32)
-    terms = 2 * count - rest
+    terms = 2 * count - rest - A_PASS
     return pl.pallas_call(
         functools.partial(late_kernel, *sizes),
         out_shape=(shape, shape),
-        in_specs=[pl.BlockSpec(memory_space=pltpu.SMEM)] + [whole] * 3 + anywhere(1 + count - rest),
+        in_specs=[pl.BlockSpec(memory_space=pltpu.SMEM)] + [whole] * 4 + anywhere(count - rest),
         out_specs=[whole] * 2,
         scratch_shapes=[
-            pltpu.VMEM(other.shape, other.dtype),
-            pltpu.SemaphoreType.DMA((ntiles,)),
             pltpu.VMEM((count - rest, ntiles, norb, width), jnp.bfloat16),
             pltpu.SemaphoreType.DMA((count - rest,)),
             pltpu.VMEM((rows, nq * terms * norb), jnp.bfloat16),
@@ -229,8 +250,6 @@
     rights, lefts, got = list(chunks), list(chunks), []
     for step in range(1, size // 2 + 1):
         last = step == size // 2
-        if step == when:
-            rights, lefts, beside = lax.optimization_barrier((rights, lefts, beside))
         for n in range(len(chunks)):
             if not last or n % 2 == 0:
                 rights[n] = lax.ppermute(rights[n], axis, up)
@@ -238,6 +257,8 @@
             if not last or n % 2 == 1:
                 lefts[n] = lax.ppermute(lefts[n], axis, down)
                 got.append(lefts[n])
+        if step == when:
+            *got, beside = lax.optimization_barrier((*got, beside))
     return got, beside
 
 
@@ -310,7 +331,7 @@
     chunks = [picks[n * nrow : (n + 1) * nrow] for n in range(nxl)]
     integrals, chunks = lax.optimization_barrier((integrals, chunks))
     own = lax.all_to_all(integrals, ROW, 0, 0, tiled=True)
-    arrived, own = ring(chunks, "z", nz, own, 4)
+    arrived, own = ring(chunks, "z", nz, own, nz // 2 - 1)
     blocks = chunks + arrived
     own = own.reshape(nrow, nq // nrow, height, width)
     other = lax.ppermute(own, "c", [(0, 1), (1, 0)])

time: 119 us -> 120 us (level)
  starting transfers between devices: 43.4 us -> 39.4 us
  waiting for transfers between devices: 37.9 us -> 40.7 us
  Pallas kernels: 15.5 us -> 17.2 us
    ppermute x7, waiting for transfers between devices: 6.47 us -> 17.3 us  [ring(): rights[n] = lax.ppermute(rights[n], axis, up)]
    ppermute x7, waiting for transfers between devices: 11.4 us -> 3.4 us  [ring(): lefts[n] = lax.ppermute(lefts[n], axis, down)]
    pallas_call x0 -> x1, Pallas kernels: none -> 4.62 us  [exchange(): pl.pallas_call(middle_kernel, out_shape=(jax.ShapeDtypeStruct(total.shape...]
    ppermute x7, starting transfers between devices: 27 us -> 23.8 us  [ring(): lefts[n] = lax.ppermute(lefts[n], axis, down)]
    pallas_call x1, Pallas kernels: 6.09 us -> 3.19 us  [exchange(): pl.pallas_call(functools.partial(late_kernel, *sizes), out_shape=(shape,...]
  transfers between devices with their start and end apart: 19 -> 19, of which waited for: 11 -> 10; matrix products, arithmetic and copies ran while one was open for 1% -> 1% of each run, Pallas kernels for 5% -> 8%
where the time goes in v5:
time: 120 us; the launch traced here: 119 us
  waiting for transfers between devices  40.7 us (34%)
  starting transfers between devices  39.4 us (33%)
  Pallas kernels  17.2 us (14%)
  blocking collectives  17.2 us (14%)
  local copies, waits for them, and re-layouts  1.48 us (1%)
  other arithmetic  1.48 us (1%)
  between operations  1.47 us (1%)
    ppermute x7, starting transfers between devices, ring(): lefts[n] = lax.ppermute(lefts[n], axis, down)  23.8 us
    all_to_all x2, waiting for transfers between devices, turn(): rows = lax.all_to_all(rows, axes, 0, 0, tiled=True)  18 us
    ppermute x7, waiting for transfers between devices, ring(): rights[n] = lax.ppermute(rights[n], axis, up)  17.3 us
    all_to_all x1, blocking collectives, local(): picks = lax.all_to_all(picks, ('xl',) + ROW, 0, 0, tiled=True)  17.2 us
    all_to_all x2, starting transfers between devices, turn(): rows = lax.all_to_all(rows, axes, 0, 0, tiled=True)  11.7 us
    pallas_call x1, Pallas kernels, exchange(): pl.pallas_call(early_kernel, out_shape=(jax.ShapeDtypeStruct((rows, rows)...  5.35 us
    pallas_call x1, Pallas kernels, exchange(): pl.pallas_call(middle_kernel, out_shape=(jax.ShapeDtypeStruct(total.shape...  4.62 us
    all_to_all x1, starting transfers between devices, local(): own = lax.all_to_all(integrals, ROW, 0, 0, tiled=True)  3.7 us
  transfers between devices with their start and end apart: 19, of which 10 were waited for; matrix products, arithmetic and copies ran while one was open for 1% of the time, Pallas kernels for 8%

profile of v5, /device:TPU:2, one launch (start us, length us, event | category | flops | bytes accessed | tf_op | source)
XLA Modules:
  0.0 119.0 jit_solution(2483416426138398274)
XLA Ops:
  1.3 2.1 %pick.1 = bf16[16,32,512]{2,1,0:T(8,128)(2,1)} custom-call(s32[8]{0:T(128)} %bitcast.23, s32[1]{0:T(128)S(6)} %copy.8.count_ref, bf16[32,10240]{1,0:T(8,128)(2,1)} %coef_ref.1), custom_call_target="tpu_custom_call" | custom-call | tf_op jit(solution)/shard_map/pick/pallas_call | solution.py:38
  3.3 17.2 %all_to_all.20 = bf16[16,32,512]{2,1,0:T(8,128)(2,1)S(1)} all-to-all(bf16[16,32,512]{2,1,0:T(8,128)(2,1)} %pick.1), channel_id=1, replica_groups=mesh['z'=8,'xl'=2,'c'=2,'y'=4,'xh'=2] {'xl','y','xh'}, dimensions={0} | all-to-all | bytes 1048576 | tf_op jit(solution)/shard_map/all_to_all | solution.py:330
  20.5 0.7 fusion
  21.3 3.7 %all-to-all-start.1 = ((bf16[48,64,512]{2,1,0:T(8,128)(2,1)}), bf16[48,64,512]{2,1,0:T(8,128)(2,1)S(1)}, u32[]{:S(2)}, u32[]{:S(2)}) async-start(bf16[48,64,512]{2,1,0:T(8,128)(2,1)} %bitcast.21), calls=%async_computation.1 | async-start | bytes 6291456 | tf_op jit(solution)/shard_map/all_to_all | solution.py:333
  24.9 5.9 %collective-permute-start.3 = (bf16[8,32,512]{2,1,0:T(8,128)(2,1)S(1)}, bf16[8,32,512]{2,1,0:T(8,128)(2,1)S(1)}, u32[]{:S(2)}, u32[]{:S(2)}) collective-permute-start(bf16[8,32,512]{2,1,0:T(8,128)(2,1)S(1)} %get-tuple-element.27.refs_1_), channel_id=1, source_target_pairs={{0,224},{32,0},{64,32},{96,64},{128,96},{160,128},{192,160},{224,1... | collective-permute-start | bytes 786440 | tf_op jit(solution)/shard_map/ppermute | solution.py:258
  30.9 3.3 %collective-permute-start.1 = (bf16[8,32,512]{2,1,0:T(8,128)(2,1)}, bf16[8,32,512]{2,1,0:T(8,128)(2,1)S(1)}, u32[]{:S(2)}, u32[]{:S(2)}) collective-permute-start(bf16[8,32,512]{2,1,0:T(8,128)(2,1)} %get-tuple-element.26.refs_0_), channel_id=1, source_target_pairs={{0,224},{32,0},{64,32},{96,64},{128,96},{160,128},{192,160},{224,1... | collective-permute-start | bytes 786440 | tf_op jit(solution)/shard_map/ppermute | solution.py:258
  34.1 3.4 %collective-permute-done.3.refs_5_ = bf16[8,32,512]{2,1,0:T(8,128)(2,1)S(1)} collective-permute-done((bf16[8,32,512]{2,1,0:T(8,128)(2,1)S(1)}, bf16[8,32,512]{2,1,0:T(8,128)(2,1)S(1)}, u32[]{:S(2)}, u32[]{:S(2)}) %collective-permute-start.3) | collective-permute-done | bytes 262176 | tf_op jit(solution)/shard_map/ppermute | solution.py:258
  37.5 3.7 %collective-permute-start.7 = (bf16[8,32,512]{2,1,0:T(8,128)(2,1)S(1)}, bf16[8,32,512]{2,1,0:T(8,128)(2,1)S(1)}, u32[]{:S(2)}, u32[]{:S(2)}) collective-permute-start(bf16[8,32,512]{2,1,0:T(8,128)(2,1)S(1)} %collective-permute-done.3.refs_5_), channel_id=1, source_target_pairs={{0,224},{32,0},{64,32},{96,64},{128,96},{160,128},{192,160},{224,1... | collective-permute-start | bytes 786440 | tf_op jit(solution)/shard_map/ppermute | solution.py:258
  41.2 0.3 collective-permute-done.refs_2_
  41.5 5.6 %collective-permute-done.2.refs_4_ = bf16[8,32,512]{2,1,0:T(8,128)(2,1)S(1)} collective-permute-done((bf16[8,32,512]{2,1,0:T(8,128)(2,1)S(1)}, bf16[8,32,512]{2,1,0:T(8,128)(2,1)S(1)}, u32[]{:S(2)}, u32[]{:S(2)}) %collective-permute-start.2) | collective-permute-done | bytes 262176 | tf_op jit(solution)/shard_map/ppermute | solution.py:255
  47.2 3.2 %collective-permute-start.5 = (bf16[8,32,512]{2,1,0:T(8,128)(2,1)S(1)}, bf16[8,32,512]{2,1,0:T(8,128)(2,1)S(1)}, u32[]{:S(2)}, u32[]{:S(2)}) collective-permute-start(bf16[8,32,512]{2,1,0:T(8,128)(2,1)S(1)} %collective-permute-done.1.refs_3_), channel_id=1, source_target_pairs={{0,224},{32,0},{64,32},{96,64},{128,96},{160,128},{192,160},{224,1... | collective-permute-start | bytes 786440 | tf_op jit(solution)/shard_map/ppermute | solution.py:258
  50.4 1.3 %collective-permute-start.11 = (bf16[8,32,512]{2,1,0:T(8,128)(2,1)S(1)}, bf16[8,32,512]{2,1,0:T(8,128)(2,1)S(1)}, u32[]{:S(2)}, u32[]{:S(2)}) collective-permute-start(bf16[8,32,512]{2,1,0:T(8,128)(2,1)S(1)} %collective-permute-done.7.refs_9_), channel_id=1, source_target_pairs={{0,224},{32,0},{64,32},{96,64},{128,96},{160,128},{192,160},{224,1... | collective-permute-start | bytes 786440 | tf_op jit(solution)/shard_map/ppermute | solution.py:258
  51.7 1.0 collective-permute-done.4.refs_6_
  52.8 5.6 %collective-permute-done.6.refs_8_ = bf16[8,32,512]{2,1,0:T(8,128)(2,1)S(1)} collective-permute-done((bf16[8,32,512]{2,1,0:T(8,128)(2,1)S(1)}, bf16[8,32,512]{2,1,0:T(8,128)(2,1)S(1)}, u32[]{:S(2)}, u32[]{:S(2)}) %collective-permute-start.6) | collective-permute-done | bytes 262176 | tf_op jit(solution)/shard_map/ppermute | solution.py:255
  58.4 3.2 %collective-permute-start.9 = (bf16[8,32,512]{2,1,0:T(8,128)(2,1)S(1)}, bf16[8,32,512]{2,1,0:T(8,128)(2,1)}, u32[]{:S(2)}, u32[]{:S(2)}) collective-permute-start(bf16[8,32,512]{2,1,0:T(8,128)(2,1)S(1)} %collective-permute-done.5.refs_7_), channel_id=1, source_target_pairs={{0,224},{32,0},{64,32},{96,64},{128,96},{160,128},{192,160},{224,1... | collective-permute-start | bytes 786440 | tf_op jit(solution)/shard_map/ppermute | solution.py:258
  61.6 2.0 %collective-permute-done.8.refs_10_ = bf16[8,32,512]{2,1,0:T(8,128)(2,1)S(1)} collective-permute-done((bf16[8,32,512]{2,1,0:T(8,128)(2,1)S(1)}, bf16[8,32,512]{2,1,0:T(8,128)(2,1)S(1)}, u32[]{:S(2)}, u32[]{:S(2)}) %collective-permute-start.8) | collective-permute-done | bytes 262176 | tf_op jit(solution)/shard_map/ppermute | solution.py:255
  63.6 2.8 %collective-permute-done.10.refs_12_ = bf16[8,32,512]{2,1,0:T(8,128)(2,1)S(1)} collective-permute-done((bf16[8,32,512]{2,1,0:T(8,128)(2,1)S(1)}, bf16[8,32,512]{2,1,0:T(8,128)(2,1)S(1)}, u32[]{:S(2)}, u32[]{:S(2)}) %collective-permute-start.10) | collective-permute-done | bytes 262176 | tf_op jit(solution)/shard_map/ppermute | solution.py:255
  66.5 0.7 copy-done.11
  67.3 3.2 %collective-permute-start.14 = (bf16[8,32,512]{2,1,0:T(8,128)(2,1)S(1)}, bf16[8,32,512]{2,1,0:T(8,128)(2,1)S(1)}, u32[]{:S(2)}, u32[]{:S(2)}) collective-permute-start(bf16[8,32,512]{2,1,0:T(8,128)(2,1)S(1)} %collective-permute-done.11.refs_13_), channel_id=1, source_target_pairs={{0,224},{32,0},{64,32},{96,64},{128,96},{160,128},{192,160},{224,1... | collective-permute-start | bytes 786440 | tf_op jit(solution)/shard_map/ppermute | solution.py:258
  70.5 5.4 %early.1 = (f32[512,512]{1,0:T(8,128)S(1)}, bf16[14,8,32,512]{3,2,1,0:T(8,128)(2,1)S(1)}) custom-call(bf16[8,6,64,512]{3,2,1,0:T(8,128)(2,1)S(1)} %bitcast.17, bf16[8,32,512]{2,1,0:T(8,128)(2,1)} %get-tuple-element.26.refs_0_, bf16[8,32,512]{2,1,0:T(8,128)(2,1)} %copy-done, bf16[8,32,512]{2,1,0:T(8,128)(2,1)} %copy-done.2, bf16[8,32,512]{2,1,0:T(8,128)(2,1)} %copy-done.4, ...), custom_call_target="tpu_custom_call" | custom-call | flops 2818572288 | bytes 1048576 | tf_op jit(solution)/shard_map/early/pallas_call | solution.py:198
  75.9 4.6 %middle.1 = (f32[512,512]{1,0:T(8,128)S(1)}, bf16[8,6,64,512]{3,2,1,0:T(8,128)(2,1)S(1)}) custom-call(f32[512,512]{1,0:T(8,128)S(1)} %get-tuple-element.42.early_ref, bf16[14,8,32,512]{3,2,1,0:T(8,128)(2,1)S(1)} %get-tuple-element.43.held, bf16[8,6,64,512]{3,2,1,0:T(8,128)(2,1)} %collective-permute-done.12.other_ref), custom_call_target="tpu_custom_call" | custom-call | flops 1610612736 | bytes 1048576 | tf_op jit(solution)/shard_map/middle/pallas_call | solution.py:215
  80.5 3.2 %late.1 = (f32[1152,128]{1,0:T(8,128)S(1)}, f32[1152,128]{1,0:T(8,128)S(1)}) custom-call(s32[1]{0:T(128)} %bitcast.2.core_ref, bf16[8,6,64,512]{3,2,1,0:T(8,128)(2,1)S(1)} %bitcast.18, f32[512,512]{1,0:T(8,128)S(1)} %get-tuple-element.44.early_ref, bf16[14,8,32,512]{3,2,1,0:T(8,128)(2,1)S(1)} %get-tuple-element.43.held, ...), custom_call_target="tpu_custom_call" | custom-call | flops 2013265920 | bytes 1048576 | tf_op jit(solution)/shard_map/late/pallas_call | solution.py:231
  83.7 0.1 collective-permute-start.15
  83.8 2.0 %collective-permute-done.15 = f32[1152,128]{1,0:T(8,128)S(1)} collective-permute-done((f32[1152,128]{1,0:T(8,128)S(1)}, f32[1152,128]{1,0:T(8,128)S(1)}, u32[]{:S(2)}, u32[]{:S(2)}) %collective-permute-start.15) | collective-permute-done | bytes 589856 | tf_op jit(solution)/shard_map/ppermute | solution.py:340
  85.8 0.9 add.15
  86.7 8.4 %all-to-all-start.2 = ((f32[1152,1,128]{2,1,0:T(1,128)}), f32[1152,1,128]{2,1,0:T(1,128)S(1)}, u32[]{:S(2)}, u32[]{:S(2)}) async-start(f32[1152,1,128]{2,1,0:T(1,128)} %bitcast.7), calls=%async_computation.2 | async-start | bytes 1179648 | tf_op jit(solution)/shard_map/all_to_all | solution.py:314
  95.1 10.6 %all-to-all-done.2 = f32[1152,1,128]{2,1,0:T(1,128)S(1)} async-done(((f32[1152,1,128]{2,1,0:T(1,128)}), f32[1152,1,128]{2,1,0:T(1,128)S(1)}, u32[]{:S(2)}, u32[]{:S(2)}) %all-to-all-start.2) | async-done | bytes 589856 | tf_op jit(solution)/shard_map/all_to_all | solution.py:314
  105.7 0.6 summed.1
  106.3 3.3 %all-to-all-start.3 = ((f32[72,1,128]{2,1,0:T(1,128)}), f32[72,1,128]{2,1,0:T(1,128)S(1)}, u32[]{:S(2)}, u32[]{:S(2)}) async-start(f32[72,1,128]{2,1,0:T(1,128)} %bitcast.22), calls=%async_computation.3 | async-start | bytes 73728 | tf_op jit(solution)/shard_map/all_to_all | solution.py:314
  109.7 0.6 pad_add_fusion.place_ref
  110.3 7.4 %all-to-all-done.3 = f32[72,1,128]{2,1,0:T(1,128)S(1)} async-done(((f32[72,1,128]{2,1,0:T(1,128)}), f32[72,1,128]{2,1,0:T(1,128)S(1)}, u32[]{:S(2)}, u32[]{:S(2)}) %all-to-all-start.3) | async-done | bytes 36896 | tf_op jit(solution)/shard_map/all_to_all | solution.py:314
  117.7 1.3 %finish.1 = (f32[16,64]{1,0:T(8,128)}, f32[1,64]{1,0:T(1,128)}) custom-call(s32[2]{0:T(128)} %pad_add_fusion.place_ref, f32[72,128]{1,0:T(8,128)S(1)} %bitcast.20), custom_call_target="tpu_custom_call" | custom-call | tf_op jit(solution)/shard_map/finish/pallas_call | solution.py:300
  (40 shorter events, 0.2 us)
Async XLA Ops:
  21.3 9.6 %copy-start = (bf16[8,32,512]{2,1,0:T(8,128)(2,1)}, bf16[8,32,512]{2,1,0:T(8,128)(2,1)S(1)}, u32[]{:S(2)}) copy-start(bf16[8,32,512]{2,1,0:T(8,128)(2,1)S(1)} %get-tuple-element.27.refs_1_) | copy-start | bytes 786436
  21.3 45.9 %all-to-all-start.1 = ((bf16[48,64,512]{2,1,0:T(8,128)(2,1)}), bf16[48,64,512]{2,1,0:T(8,128)(2,1)S(1)}, u32[]{:S(2)}, u32[]{:S(2)}) async-start(bf16[48,64,512]{2,1,0:T(8,128)(2,1)} %bitcast.21), calls=%async_computation.1 | async-start | bytes 6291456 | tf_op jit(solution)/shard_map/all_to_all | solution.py:333
  24.9 12.6 %collective-permute-start.3 = (bf16[8,32,512]{2,1,0:T(8,128)(2,1)S(1)}, bf16[8,32,512]{2,1,0:T(8,128)(2,1)S(1)}, u32[]{:S(2)}, u32[]{:S(2)}) collective-permute-start(bf16[8,32,512]{2,1,0:T(8,128)(2,1)S(1)} %get-tuple-element.27.refs_1_), channel_id=1, source_target_pairs={{0,224},{32,0},{64,32},{96,64},{128,96},{160,128},{192,160},{224,1... | collective-permute-start | bytes 786440 | tf_op jit(solution)/shard_map/ppermute | solution.py:258
  30.9 10.7 %collective-permute-start = (bf16[8,32,512]{2,1,0:T(8,128)(2,1)}, bf16[8,32,512]{2,1,0:T(8,128)(2,1)S(1)}, u32[]{:S(2)}, u32[]{:S(2)}) collective-permute-start(bf16[8,32,512]{2,1,0:T(8,128)(2,1)} %get-tuple-element.26.refs_0_), channel_id=1, source_target_pairs={{0,32},{32,64},{64,96},{96,128},{128,160},{160,192},{192,224},{224... | collective-permute-start | bytes 786440 | tf_op jit(solution)/shard_map/ppermute | solution.py:255
  30.9 16.3 %collective-permute-start.2 = (bf16[8,32,512]{2,1,0:T(8,128)(2,1)S(1)}, bf16[8,32,512]{2,1,0:T(8,128)(2,1)S(1)}, u32[]{:S(2)}, u32[]{:S(2)}) collective-permute-start(bf16[8,32,512]{2,1,0:T(8,128)(2,1)S(1)} %get-tuple-element.27.refs_1_), channel_id=1, source_target_pairs={{0,32},{32,64},{64,96},{96,128},{128,160},{160,192},{192,224},{224... | collective-permute-start | bytes 786440 | tf_op jit(solution)/shard_map/ppermute | solution.py:255
  30.9 16.3 %collective-permute-start.1 = (bf16[8,32,512]{2,1,0:T(8,128)(2,1)}, bf16[8,32,512]{2,1,0:T(8,128)(2,1)S(1)}, u32[]{:S(2)}, u32[]{:S(2)}) collective-permute-start(bf16[8,32,512]{2,1,0:T(8,128)(2,1)} %get-tuple-element.26.refs_0_), channel_id=1, source_target_pairs={{0,224},{32,0},{64,32},{96,64},{128,96},{160,128},{192,160},{224,1... | collective-permute-start | bytes 786440 | tf_op jit(solution)/shard_map/ppermute | solution.py:258
  37.5 28.9 %copy-start.1 = (bf16[8,32,512]{2,1,0:T(8,128)(2,1)}, bf16[8,32,512]{2,1,0:T(8,128)(2,1)S(1)}, u32[]{:S(2)}) copy-start(bf16[8,32,512]{2,1,0:T(8,128)(2,1)S(1)} %collective-permute-done.3.refs_5_) | copy-start | bytes 786436
  37.5 12.9 %collective-permute-start.7 = (bf16[8,32,512]{2,1,0:T(8,128)(2,1)S(1)}, bf16[8,32,512]{2,1,0:T(8,128)(2,1)S(1)}, u32[]{:S(2)}, u32[]{:S(2)}) collective-permute-start(bf16[8,32,512]{2,1,0:T(8,128)(2,1)S(1)} %collective-permute-done.3.refs_5_), channel_id=1, source_target_pairs={{0,224},{32,0},{64,32},{96,64},{128,96},{160,128},{192,160},{224,1... | collective-permute-start | bytes 786440 | tf_op jit(solution)/shard_map/ppermute | solution.py:258
  41.5 24.9 %copy-start.2 = (bf16[8,32,512]{2,1,0:T(8,128)(2,1)}, bf16[8,32,512]{2,1,0:T(8,128)(2,1)S(1)}, u32[]{:S(2)}) copy-start(bf16[8,32,512]{2,1,0:T(8,128)(2,1)S(1)} %collective-permute-done.refs_2_) | copy-start | bytes 786436
  41.5 11.2 %collective-permute-start.4 = (bf16[8,32,512]{2,1,0:T(8,128)(2,1)S(1)}, bf16[8,32,512]{2,1,0:T(8,128)(2,1)S(1)}, u32[]{:S(2)}, u32[]{:S(2)}) collective-permute-start(bf16[8,32,512]{2,1,0:T(8,128)(2,1)S(1)} %collective-permute-done.refs_2_), channel_id=1, source_target_pairs={{0,32},{32,64},{64,96},{96,128},{128,160},{160,192},{192,224},{224... | collective-permute-start | bytes 786440 | tf_op jit(solution)/shard_map/ppermute | solution.py:255
  47.1 19.3 %copy-start.3 = (bf16[8,32,512]{2,1,0:T(8,128)(2,1)}, bf16[8,32,512]{2,1,0:T(8,128)(2,1)S(1)}, u32[]{:S(2)}) copy-start(bf16[8,32,512]{2,1,0:T(8,128)(2,1)S(1)} %collective-permute-done.2.refs_4_) | copy-start | bytes 786436
  47.1 11.2 %collective-permute-start.6 = (bf16[8,32,512]{2,1,0:T(8,128)(2,1)S(1)}, bf16[8,32,512]{2,1,0:T(8,128)(2,1)S(1)}, u32[]{:S(2)}, u32[]{:S(2)}) collective-permute-start(bf16[8,32,512]{2,1,0:T(8,128)(2,1)S(1)} %collective-permute-done.2.refs_4_), channel_id=1, source_target_pairs={{0,32},{32,64},{64,96},{96,128},{128,160},{160,192},{192,224},{224... | collective-permute-start | bytes 786440 | tf_op jit(solution)/shard_map/ppermute | solution.py:255
  47.2 19.3 %copy-start.4 = (bf16[8,32,512]{2,1,0:T(8,128)(2,1)}, bf16[8,32,512]{2,1,0:T(8,128)(2,1)S(1)}, u32[]{:S(2)}) copy-start(bf16[8,32,512]{2,1,0:T(8,128)(2,1)S(1)} %collective-permute-done.1.refs_3_) | copy-start | bytes 786436
  47.2 11.2 %collective-permute-start.5 = (bf16[8,32,512]{2,1,0:T(8,128)(2,1)S(1)}, bf16[8,32,512]{2,1,0:T(8,128)(2,1)S(1)}, u32[]{:S(2)}, u32[]{:S(2)}) collective-permute-start(bf16[8,32,512]{2,1,0:T(8,128)(2,1)S(1)} %collective-permute-done.1.refs_3_), channel_id=1, source_target_pairs={{0,224},{32,0},{64,32},{96,64},{128,96},{160,128},{192,160},{224,1... | collective-permute-start | bytes 786440 | tf_op jit(solution)/shard_map/ppermute | solution.py:258
  50.4 16.0 %copy-start.5 = (bf16[8,32,512]{2,1,0:T(8,128)(2,1)}, bf16[8,32,512]{2,1,0:T(8,128)(2,1)S(1)}, u32[]{:S(2)}) copy-start(bf16[8,32,512]{2,1,0:T(8,128)(2,1)S(1)} %collective-permute-done.7.refs_9_) | copy-start | bytes 786436
  50.4 11.2 %collective-permute-start.11 = (bf16[8,32,512]{2,1,0:T(8,128)(2,1)S(1)}, bf16[8,32,512]{2,1,0:T(8,128)(2,1)S(1)}, u32[]{:S(2)}, u32[]{:S(2)}) collective-permute-start(bf16[8,32,512]{2,1,0:T(8,128)(2,1)S(1)} %collective-permute-done.7.refs_9_), channel_id=1, source_target_pairs={{0,224},{32,0},{64,32},{96,64},{128,96},{160,128},{192,160},{224,1... | collective-permute-start | bytes 786440 | tf_op jit(solution)/shard_map/ppermute | solution.py:258
  52.8 13.7 %copy-start.6 = (bf16[8,32,512]{2,1,0:T(8,128)(2,1)}, bf16[8,32,512]{2,1,0:T(8,128)(2,1)S(1)}, u32[]{:S(2)}) copy-start(bf16[8,32,512]{2,1,0:T(8,128)(2,1)S(1)} %collective-permute-done.4.refs_6_) | copy-start | bytes 786436
  52.8 10.8 %collective-permute-start.8 = (bf16[8,32,512]{2,1,0:T(8,128)(2,1)S(1)}, bf16[8,32,512]{2,1,0:T(8,128)(2,1)S(1)}, u32[]{:S(2)}, u32[]{:S(2)}) collective-permute-start(bf16[8,32,512]{2,1,0:T(8,128)(2,1)S(1)} %collective-permute-done.4.refs_6_), channel_id=1, source_target_pairs={{0,32},{32,64},{64,96},{96,128},{128,160},{160,192},{192,224},{224... | collective-permute-start | bytes 786440 | tf_op jit(solution)/shard_map/ppermute | solution.py:255
  58.4 8.1 %copy-start.8 = (bf16[8,32,512]{2,1,0:T(8,128)(2,1)}, bf16[8,32,512]{2,1,0:T(8,128)(2,1)S(1)}, u32[]{:S(2)}) copy-start(bf16[8,32,512]{2,1,0:T(8,128)(2,1)S(1)} %collective-permute-done.6.refs_8_) | copy-start | bytes 786436
  58.4 8.0 %collective-permute-start.10 = (bf16[8,32,512]{2,1,0:T(8,128)(2,1)S(1)}, bf16[8,32,512]{2,1,0:T(8,128)(2,1)S(1)}, u32[]{:S(2)}, u32[]{:S(2)}) collective-permute-start(bf16[8,32,512]{2,1,0:T(8,128)(2,1)S(1)} %collective-permute-done.6.refs_8_), channel_id=1, source_target_pairs={{0,32},{32,64},{64,96},{96,128},{128,160},{160,192},{192,224},{224... | collective-permute-start | bytes 786440 | tf_op jit(solution)/shard_map/ppermute | solution.py:255
  58.4 8.1 %copy-start.9 = (bf16[8,32,512]{2,1,0:T(8,128)(2,1)}, bf16[8,32,512]{2,1,0:T(8,128)(2,1)S(1)}, u32[]{:S(2)}) copy-start(bf16[8,32,512]{2,1,0:T(8,128)(2,1)S(1)} %collective-permute-done.5.refs_7_) | copy-start | bytes 786436
  58.4 8.8 %collective-permute-start.9 = (bf16[8,32,512]{2,1,0:T(8,128)(2,1)S(1)}, bf16[8,32,512]{2,1,0:T(8,128)(2,1)}, u32[]{:S(2)}, u32[]{:S(2)}) collective-permute-start(bf16[8,32,512]{2,1,0:T(8,128)(2,1)S(1)} %collective-permute-done.5.refs_7_), channel_id=1, source_target_pairs={{0,224},{32,0},{64,32},{96,64},{128,96},{160,128},{192,160},{224,1... | collective-permute-start | bytes 786440 | tf_op jit(solution)/shard_map/ppermute | solution.py:258
  61.6 8.9 %copy-start.7 = (bf16[8,32,512]{2,1,0:T(8,128)(2,1)}, bf16[8,32,512]{2,1,0:T(8,128)(2,1)S(1)}, u32[]{:S(2)}) copy-start(bf16[8,32,512]{2,1,0:T(8,128)(2,1)S(1)} %collective-permute-done.11.refs_13_) | copy-start | bytes 786436
  63.6 2.9 %copy-start.10 = (bf16[8,32,512]{2,1,0:T(8,128)(2,1)}, bf16[8,32,512]{2,1,0:T(8,128)(2,1)S(1)}, u32[]{:S(2)}) copy-start(bf16[8,32,512]{2,1,0:T(8,128)(2,1)S(1)} %collective-permute-done.8.refs_10_) | copy-start | bytes 786436
  66.5 0.7 copy-start.11
  67.2 8.7 %collective-permute-start.12 = (bf16[8,6,64,512]{3,2,1,0:T(8,128)(2,1)S(1)}, bf16[8,6,64,512]{3,2,1,0:T(8,128)(2,1)}, u32[]{:S(2)}, u32[]{:S(2)}) collective-permute-start(bf16[8,6,64,512]{3,2,1,0:T(8,128)(2,1)S(1)} %bitcast.16), channel_id=1, source_target_pairs={{0,8},{8,0},{1,9},{9,1},{2,10},{10,2},{3,11},{11,3},{4,12},{12,4},... | collective-permute-start | bytes 9437192 | tf_op jit(solution)/shard_map/ppermute | solution.py:337
  67.2 13.3 %collective-permute-start.13 = (bf16[8,32,512]{2,1,0:T(8,128)(2,1)}, bf16[8,32,512]{2,1,0:T(8,128)(2,1)S(1)}, u32[]{:S(2)}, u32[]{:S(2)}) collective-permute-start(bf16[8,32,512]{2,1,0:T(8,128)(2,1)} %copy-done.10), channel_id=1, source_target_pairs={{0,32},{32,64},{64,96},{96,128},{128,160},{160,192},{192,224},{224... | collective-permute-start | bytes 786440 | tf_op jit(solution)/shard_map/ppermute | solution.py:255
  67.3 13.2 %collective-permute-start.14 = (bf16[8,32,512]{2,1,0:T(8,128)(2,1)S(1)}, bf16[8,32,512]{2,1,0:T(8,128)(2,1)S(1)}, u32[]{:S(2)}, u32[]{:S(2)}) collective-permute-start(bf16[8,32,512]{2,1,0:T(8,128)(2,1)S(1)} %collective-permute-done.11.refs_13_), channel_id=1, source_target_pairs={{0,224},{32,0},{64,32},{96,64},{128,96},{160,128},{192,160},{224,1... | collective-permute-start | bytes 786440 | tf_op jit(solution)/shard_map/ppermute | solution.py:258
  83.7 2.1 %collective-permute-start.15 = (f32[1152,128]{1,0:T(8,128)S(1)}, f32[1152,128]{1,0:T(8,128)S(1)}, u32[]{:S(2)}, u32[]{:S(2)}) collective-permute-start(f32[1152,128]{1,0:T(8,128)S(1)} %get-tuple-element.47), channel_id=1, source_target_pairs={{0,8},{8,0},{1,9},{9,1},{2,10},{10,2},{3,11},{11,3},{4,12},{12,4},... | collective-permute-start | bytes 1769480 | tf_op jit(solution)/shard_map/ppermute | solution.py:340
  86.7 19.0 %all-to-all-start.2 = ((f32[1152,1,128]{2,1,0:T(1,128)}), f32[1152,1,128]{2,1,0:T(1,128)S(1)}, u32[]{:S(2)}, u32[]{:S(2)}) async-start(f32[1152,1,128]{2,1,0:T(1,128)} %bitcast.7), calls=%async_computation.2 | async-start | bytes 1179648 | tf_op jit(solution)/shard_map/all_to_all | solution.py:314
  106.3 11.3 %all-to-all-start.3 = ((f32[72,1,128]{2,1,0:T(1,128)}), f32[72,1,128]{2,1,0:T(1,128)S(1)}, u32[]{:S(2)}, u32[]{:S(2)}) async-start(f32[72,1,128]{2,1,0:T(1,128)} %bitcast.22), calls=%async_computation.3 | async-start | bytes 73728 | tf_op jit(solution)/shard_map/all_to_all | solution.py:314

commit v6 on v4

--- a/solution.py
+++ b/solution.py
@@ -37,7 +37,7 @@
     slots = cols.shape[0]
     return pl.pallas_call(
         functools.partial(pick_kernel, copies, width),
-        out_shape=jax.ShapeDtypeStruct((copies, norb, slots * width), coefficients.dtype),
+        out_shape=pltpu.VMEM((copies, norb, slots * width), coefficients.dtype),
         in_specs=[
             pl.BlockSpec(memory_space=pltpu.SMEM),
             pl.BlockSpec(memory_space=pltpu.SMEM),

time: 119 us -> 118 us (level)
  no operation moved by 1% of the time
where the time goes in v6:
time: 118 us
  starting transfers between devices  43.4 us (37%)
  waiting for transfers between devices  37.9 us (32%)
  blocking collectives  17 us (14%)
  Pallas kernels  14.7 us (12%)
  local copies, waits for them, and re-layouts  2.09 us (2%)
  other arithmetic  1.51 us (1%)
  between operations  1.41 us (1%)
    ppermute x7, starting transfers between devices, ring(): lefts[n] = lax.ppermute(lefts[n], axis, down)  27 us
    all_to_all x2, waiting for transfers between devices, turn(): rows = lax.all_to_all(rows, axes, 0, 0, tiled=True)  18.1 us
    all_to_all x1, blocking collectives, local(): picks = lax.all_to_all(picks, ('xl',) + ROW, 0, 0, tiled=True)  17 us
    all_to_all x2, starting transfers between devices, turn(): rows = lax.all_to_all(rows, axes, 0, 0, tiled=True)  12.6 us
    ppermute x7, waiting for transfers between devices, ring(): lefts[n] = lax.ppermute(lefts[n], axis, down)  11.4 us
    ppermute x7, waiting for transfers between devices, ring(): rights[n] = lax.ppermute(rights[n], axis, up)  6.47 us
    pallas_call x1, Pallas kernels, exchange(): pl.pallas_call(functools.partial(late_kernel, *sizes), out_shape=(shape,...  6.09 us
    pallas_call x1, Pallas kernels, exchange(): pl.pallas_call(early_kernel, out_shape=(jax.ShapeDtypeStruct((rows, rows)...  5.36 us
  transfers between devices with their start and end apart: 19, of which 11 were waited for; matrix products, arithmetic and copies ran while one was open for 1% of the time, Pallas kernels for 5%

profile of v6, /device:TPU:2, one launch (start us, length us, event | category | flops | bytes accessed | tf_op | source)
XLA Modules:
  0.0 118.0 jit_solution(10562240727458670772)
XLA Ops:
  1.3 1.3 %pick.1 = bf16[16,32,512]{2,1,0:T(8,128)(2,1)S(1)} custom-call(s32[8]{0:T(128)} %bitcast.23, s32[1]{0:T(128)S(6)} %copy.8.count_ref, bf16[32,10240]{1,0:T(8,128)(2,1)} %coef_ref.1), custom_call_target="tpu_custom_call" | custom-call | tf_op jit(solution)/shard_map/pick/pallas_call | solution.py:38
  2.5 17.0 %all_to_all.20 = bf16[16,32,512]{2,1,0:T(8,128)(2,1)S(1)} all-to-all(bf16[16,32,512]{2,1,0:T(8,128)(2,1)S(1)} %pick.1), channel_id=1, replica_groups=mesh['z'=8,'xl'=2,'c'=2,'y'=4,'xh'=2] {'xl','y','xh'}, dimensions={0} | all-to-all | bytes 1048576 | tf_op jit(solution)/shard_map/all_to_all | solution.py:309
  19.5 0.7 fusion
  20.3 3.7 %all-to-all-start.1 = ((bf16[48,64,512]{2,1,0:T(8,128)(2,1)}), bf16[48,64,512]{2,1,0:T(8,128)(2,1)S(1)}, u32[]{:S(2)}, u32[]{:S(2)}) async-start(bf16[48,64,512]{2,1,0:T(8,128)(2,1)} %bitcast.21), calls=%async_computation.1 | async-start | bytes 6291456 | tf_op jit(solution)/shard_map/all_to_all | solution.py:312
  24.0 5.9 %collective-permute-start.6 = (bf16[8,32,512]{2,1,0:T(8,128)(2,1)}, bf16[8,32,512]{2,1,0:T(8,128)(2,1)S(1)}, u32[]{:S(2)}, u32[]{:S(2)}) collective-permute-start(bf16[8,32,512]{2,1,0:T(8,128)(2,1)} %get-tuple-element.14.refs_0_), channel_id=1, source_target_pairs={{0,224},{32,0},{64,32},{96,64},{128,96},{160,128},{192,160},{224,1... | collective-permute-start | bytes 786440 | tf_op jit(solution)/shard_map/ppermute | solution.py:239
  29.9 3.2 %collective-permute-start.9 = (bf16[8,32,512]{2,1,0:T(8,128)(2,1)S(1)}, bf16[8,32,512]{2,1,0:T(8,128)(2,1)S(1)}, u32[]{:S(2)}, u32[]{:S(2)}) collective-permute-start(bf16[8,32,512]{2,1,0:T(8,128)(2,1)S(1)} %get-tuple-element.15.refs_1_), channel_id=1, source_target_pairs={{0,224},{32,0},{64,32},{96,64},{128,96},{160,128},{192,160},{224,1... | collective-permute-start | bytes 786440 | tf_op jit(solution)/shard_map/ppermute | solution.py:239
  33.1 3.8 %collective-permute-done.6.refs_3_ = bf16[8,32,512]{2,1,0:T(8,128)(2,1)S(1)} collective-permute-done((bf16[8,32,512]{2,1,0:T(8,128)(2,1)}, bf16[8,32,512]{2,1,0:T(8,128)(2,1)S(1)}, u32[]{:S(2)}, u32[]{:S(2)}) %collective-permute-start.6) | collective-permute-done | bytes 262176 | tf_op jit(solution)/shard_map/ppermute | solution.py:239
  37.0 3.6 %collective-permute-start.7 = (bf16[8,32,512]{2,1,0:T(8,128)(2,1)S(1)}, bf16[8,32,512]{2,1,0:T(8,128)(2,1)S(1)}, u32[]{:S(2)}, u32[]{:S(2)}) collective-permute-start(bf16[8,32,512]{2,1,0:T(8,128)(2,1)S(1)} %collective-permute-done.6.refs_3_), channel_id=1, source_target_pairs={{0,224},{32,0},{64,32},{96,64},{128,96},{160,128},{192,160},{224,1... | collective-permute-start | bytes 786440 | tf_op jit(solution)/shard_map/ppermute | solution.py:239
  40.6 1.9 %collective-permute-done.9.refs_5_ = bf16[8,32,512]{2,1,0:T(8,128)(2,1)S(1)} collective-permute-done((bf16[8,32,512]{2,1,0:T(8,128)(2,1)S(1)}, bf16[8,32,512]{2,1,0:T(8,128)(2,1)S(1)}, u32[]{:S(2)}, u32[]{:S(2)}) %collective-permute-start.9) | collective-permute-done | bytes 262176 | tf_op jit(solution)/shard_map/ppermute | solution.py:239
  42.5 3.7 %collective-permute-start.10 = (bf16[8,32,512]{2,1,0:T(8,128)(2,1)S(1)}, bf16[8,32,512]{2,1,0:T(8,128)(2,1)S(1)}, u32[]{:S(2)}, u32[]{:S(2)}) collective-permute-start(bf16[8,32,512]{2,1,0:T(8,128)(2,1)S(1)} %collective-permute-done.9.refs_5_), channel_id=1, source_target_pairs={{0,224},{32,0},{64,32},{96,64},{128,96},{160,128},{192,160},{224,1... | collective-permute-start | bytes 786440 | tf_op jit(solution)/shard_map/ppermute | solution.py:239
  46.2 1.9 %collective-permute-done.7.refs_7_ = bf16[8,32,512]{2,1,0:T(8,128)(2,1)S(1)} collective-permute-done((bf16[8,32,512]{2,1,0:T(8,128)(2,1)S(1)}, bf16[8,32,512]{2,1,0:T(8,128)(2,1)S(1)}, u32[]{:S(2)}, u32[]{:S(2)}) %collective-permute-start.7) | collective-permute-done | bytes 262176 | tf_op jit(solution)/shard_map/ppermute | solution.py:239
  48.1 3.7 %collective-permute-start.8 = (bf16[8,32,512]{2,1,0:T(8,128)(2,1)S(1)}, bf16[8,32,512]{2,1,0:T(8,128)(2,1)S(1)}, u32[]{:S(2)}, u32[]{:S(2)}) collective-permute-start(bf16[8,32,512]{2,1,0:T(8,128)(2,1)S(1)} %collective-permute-done.7.refs_7_), channel_id=1, source_target_pairs={{0,224},{32,0},{64,32},{96,64},{128,96},{160,128},{192,160},{224,1... | collective-permute-start | bytes 786440 | tf_op jit(solution)/shard_map/ppermute | solution.py:239
  51.8 1.9 %collective-permute-done.10.refs_9_ = bf16[8,32,512]{2,1,0:T(8,128)(2,1)S(1)} collective-permute-done((bf16[8,32,512]{2,1,0:T(8,128)(2,1)S(1)}, bf16[8,32,512]{2,1,0:T(8,128)(2,1)S(1)}, u32[]{:S(2)}, u32[]{:S(2)}) %collective-permute-start.10) | collective-permute-done | bytes 262176 | tf_op jit(solution)/shard_map/ppermute | solution.py:239
  53.7 3.7 %collective-permute-start.11 = (bf16[8,32,512]{2,1,0:T(8,128)(2,1)S(1)}, bf16[8,32,512]{2,1,0:T(8,128)(2,1)S(1)}, u32[]{:S(2)}, u32[]{:S(2)}) collective-permute-start(bf16[8,32,512]{2,1,0:T(8,128)(2,1)S(1)} %collective-permute-done.10.refs_9_), channel_id=1, source_target_pairs={{0,224},{32,0},{64,32},{96,64},{128,96},{160,128},{192,160},{224,1... | collective-permute-start | bytes 786440 | tf_op jit(solution)/shard_map/ppermute | solution.py:239
  57.4 1.8 %collective-permute-done.8.refs_11_ = bf16[8,32,512]{2,1,0:T(8,128)(2,1)S(1)} collective-permute-done((bf16[8,32,512]{2,1,0:T(8,128)(2,1)S(1)}, bf16[8,32,512]{2,1,0:T(8,128)(2,1)S(1)}, u32[]{:S(2)}, u32[]{:S(2)}) %collective-permute-start.8) | collective-permute-done | bytes 262176 | tf_op jit(solution)/shard_map/ppermute | solution.py:239
  59.2 3.4 %collective-permute-done.2.refs_10_ = bf16[8,32,512]{2,1,0:T(8,128)(2,1)S(1)} collective-permute-done((bf16[8,32,512]{2,1,0:T(8,128)(2,1)S(1)}, bf16[8,32,512]{2,1,0:T(8,128)(2,1)S(1)}, u32[]{:S(2)}, u32[]{:S(2)}) %collective-permute-start.2) | collective-permute-done | bytes 262176 | tf_op jit(solution)/shard_map/ppermute | solution.py:236
  62.7 0.6 copy-done.10
  63.3 0.7 copy-done.11
  64.0 1.5 %collective-permute-done.5.refs_12_ = bf16[8,32,512]{2,1,0:T(8,128)(2,1)} collective-permute-done((bf16[8,32,512]{2,1,0:T(8,128)(2,1)S(1)}, bf16[8,32,512]{2,1,0:T(8,128)(2,1)}, u32[]{:S(2)}, u32[]{:S(2)}) %collective-permute-start.5) | collective-permute-done | bytes 262176 | tf_op jit(solution)/shard_map/ppermute | solution.py:236
  65.5 3.2 %collective-permute-start.14 = (bf16[8,32,512]{2,1,0:T(8,128)(2,1)}, bf16[8,32,512]{2,1,0:T(8,128)(2,1)S(1)}, u32[]{:S(2)}, u32[]{:S(2)}) collective-permute-start(bf16[8,32,512]{2,1,0:T(8,128)(2,1)} %copy-done.11), channel_id=1, source_target_pairs={{0,224},{32,0},{64,32},{96,64},{128,96},{160,128},{192,160},{224,1... | collective-permute-start | bytes 786440 | tf_op jit(solution)/shard_map/ppermute | solution.py:239
  68.8 5.4 %early.1 = (f32[512,512]{1,0:T(8,128)S(1)}, bf16[14,8,32,512]{3,2,1,0:T(8,128)(2,1)S(1)}) custom-call(bf16[8,6,64,512]{3,2,1,0:T(8,128)(2,1)S(1)} %bitcast.17, bf16[8,32,512]{2,1,0:T(8,128)(2,1)} %get-tuple-element.14.refs_0_, bf16[8,32,512]{2,1,0:T(8,128)(2,1)} %copy-done, bf16[8,32,512]{2,1,0:T(8,128)(2,1)} %copy-done.2, bf16[8,32,512]{2,1,0:T(8,128)(2,1)} %copy-done.1, ...), custom_call_target="tpu_custom_call" | custom-call | flops 2818572288 | bytes 1048576 | tf_op jit(solution)/shard_map/early/pallas_call | solution.py:189
  74.1 1.5 %collective-permute-done.13.refs_0_ = bf16[8,32,512]{2,1,0:T(8,128)(2,1)S(1)} collective-permute-done((bf16[8,32,512]{2,1,0:T(8,128)(2,1)}, bf16[8,32,512]{2,1,0:T(8,128)(2,1)S(1)}, u32[]{:S(2)}, u32[]{:S(2)}) %collective-permute-start.13) | collective-permute-done | bytes 262176 | tf_op jit(solution)/shard_map/ppermute | solution.py:236
  75.7 6.1 %late.1 = (f32[1152,128]{1,0:T(8,128)S(1)}, f32[1152,128]{1,0:T(8,128)S(1)}) custom-call(s32[1]{0:T(128)} %bitcast.2.core_ref, bf16[8,6,64,512]{3,2,1,0:T(8,128)(2,1)S(1)} %bitcast.18, f32[512,512]{1,0:T(8,128)S(1)} %get-tuple-element.18.early_ref, bf16[14,8,32,512]{3,2,1,0:T(8,128)(2,1)S(1)} %get-tuple-element.19.held, ...), custom_call_target="tpu_custom_call" | custom-call | flops 3623878656 | bytes 1048576 | tf_op jit(solution)/shard_map/late/pallas_call | solution.py:208
  81.9 2.0 %collective-permute-done.15 = f32[1152,128]{1,0:T(8,128)S(1)} collective-permute-done((f32[1152,128]{1,0:T(8,128)S(1)}, f32[1152,128]{1,0:T(8,128)S(1)}, u32[]{:S(2)}, u32[]{:S(2)}) %collective-permute-start.15) | collective-permute-done | bytes 589856 | tf_op jit(solution)/shard_map/ppermute | solution.py:319
  83.9 0.9 add.15
  84.7 8.3 %all-to-all-start.2 = ((f32[1152,1,128]{2,1,0:T(1,128)}), f32[1152,1,128]{2,1,0:T(1,128)S(1)}, u32[]{:S(2)}, u32[]{:S(2)}) async-start(f32[1152,1,128]{2,1,0:T(1,128)} %bitcast.7), calls=%async_computation.2 | async-start | bytes 1179648 | tf_op jit(solution)/shard_map/all_to_all | solution.py:293
  93.1 10.6 %all-to-all-done.2 = f32[1152,1,128]{2,1,0:T(1,128)S(1)} async-done(((f32[1152,1,128]{2,1,0:T(1,128)}), f32[1152,1,128]{2,1,0:T(1,128)S(1)}, u32[]{:S(2)}, u32[]{:S(2)}) %all-to-all-start.2) | async-done | bytes 589856 | tf_op jit(solution)/shard_map/all_to_all | solution.py:293
  103.7 0.6 summed.1
  104.3 4.2 %all-to-all-start.3 = ((f32[72,1,128]{2,1,0:T(1,128)}), f32[72,1,128]{2,1,0:T(1,128)S(1)}, u32[]{:S(2)}, u32[]{:S(2)}) async-start(f32[72,1,128]{2,1,0:T(1,128)} %bitcast.22), calls=%async_computation.3 | async-start | bytes 73728 | tf_op jit(solution)/shard_map/all_to_all | solution.py:293
  108.6 0.6 pad_add_fusion.place_ref
  109.2 7.4 %all-to-all-done.3 = f32[72,1,128]{2,1,0:T(1,128)S(1)} async-done(((f32[72,1,128]{2,1,0:T(1,128)}), f32[72,1,128]{2,1,0:T(1,128)S(1)}, u32[]{:S(2)}, u32[]{:S(2)}) %all-to-all-start.3) | async-done | bytes 36896 | tf_op jit(solution)/shard_map/all_to_all | solution.py:293
  116.6 1.3 %finish.1 = (f32[16,64]{1,0:T(8,128)}, f32[1,64]{1,0:T(1,128)}) custom-call(s32[2]{0:T(128)} %pad_add_fusion.place_ref, f32[72,128]{1,0:T(8,128)S(1)} %bitcast.20), custom_call_target="tpu_custom_call" | custom-call | tf_op jit(solution)/shard_map/finish/pallas_call | solution.py:279
  (39 shorter events, 0.2 us)
Async XLA Ops:
  20.3 12.8 %copy-start = (bf16[8,32,512]{2,1,0:T(8,128)(2,1)}, bf16[8,32,512]{2,1,0:T(8,128)(2,1)S(1)}, u32[]{:S(2)}) copy-start(bf16[8,32,512]{2,1,0:T(8,128)(2,1)S(1)} %get-tuple-element.15.refs_1_) | copy-start | bytes 786436
  20.3 45.2 %all-to-all-start.1 = ((bf16[48,64,512]{2,1,0:T(8,128)(2,1)}), bf16[48,64,512]{2,1,0:T(8,128)(2,1)S(1)}, u32[]{:S(2)}, u32[]{:S(2)}) async-start(bf16[48,64,512]{2,1,0:T(8,128)(2,1)} %bitcast.21), calls=%async_computation.1 | async-start | bytes 6291456 | tf_op jit(solution)/shard_map/all_to_all | solution.py:312
  24.0 13.0 %collective-permute-start.6 = (bf16[8,32,512]{2,1,0:T(8,128)(2,1)}, bf16[8,32,512]{2,1,0:T(8,128)(2,1)S(1)}, u32[]{:S(2)}, u32[]{:S(2)}) collective-permute-start(bf16[8,32,512]{2,1,0:T(8,128)(2,1)} %get-tuple-element.14.refs_0_), channel_id=1, source_target_pairs={{0,224},{32,0},{64,32},{96,64},{128,96},{160,128},{192,160},{224,1... | collective-permute-start | bytes 786440 | tf_op jit(solution)/shard_map/ppermute | solution.py:239
  29.9 10.7 %collective-permute-start = (bf16[8,32,512]{2,1,0:T(8,128)(2,1)}, bf16[8,32,512]{2,1,0:T(8,128)(2,1)S(1)}, u32[]{:S(2)}, u32[]{:S(2)}) collective-permute-start(bf16[8,32,512]{2,1,0:T(8,128)(2,1)} %get-tuple-element.14.refs_0_), channel_id=1, source_target_pairs={{0,32},{32,64},{64,96},{96,128},{128,160},{160,192},{192,224},{224... | collective-permute-start | bytes 786440 | tf_op jit(solution)/shard_map/ppermute | solution.py:236
  29.9 12.6 %collective-permute-start.9 = (bf16[8,32,512]{2,1,0:T(8,128)(2,1)S(1)}, bf16[8,32,512]{2,1,0:T(8,128)(2,1)S(1)}, u32[]{:S(2)}, u32[]{:S(2)}) collective-permute-start(bf16[8,32,512]{2,1,0:T(8,128)(2,1)S(1)} %get-tuple-element.15.refs_1_), channel_id=1, source_target_pairs={{0,224},{32,0},{64,32},{96,64},{128,96},{160,128},{192,160},{224,1... | collective-permute-start | bytes 786440 | tf_op jit(solution)/shard_map/ppermute | solution.py:239
  33.1 13.0 %collective-permute-start.3 = (bf16[8,32,512]{2,1,0:T(8,128)(2,1)S(1)}, bf16[8,32,512]{2,1,0:T(8,128)(2,1)S(1)}, u32[]{:S(2)}, u32[]{:S(2)}) collective-permute-start(bf16[8,32,512]{2,1,0:T(8,128)(2,1)S(1)} %get-tuple-element.15.refs_1_), channel_id=1, source_target_pairs={{0,32},{32,64},{64,96},{96,128},{128,160},{160,192},{192,224},{224... | collective-permute-start | bytes 786440 | tf_op jit(solution)/shard_map/ppermute | solution.py:236
  37.0 25.7 %copy-start.1 = (bf16[8,32,512]{2,1,0:T(8,128)(2,1)}, bf16[8,32,512]{2,1,0:T(8,128)(2,1)S(1)}, u32[]{:S(2)}) copy-start(bf16[8,32,512]{2,1,0:T(8,128)(2,1)S(1)} %collective-permute-done.6.refs_3_) | copy-start | bytes 786436
  37.0 11.1 %collective-permute-start.7 = (bf16[8,32,512]{2,1,0:T(8,128)(2,1)S(1)}, bf16[8,32,512]{2,1,0:T(8,128)(2,1)S(1)}, u32[]{:S(2)}, u32[]{:S(2)}) collective-permute-start(bf16[8,32,512]{2,1,0:T(8,128)(2,1)S(1)} %collective-permute-done.6.refs_3_), channel_id=1, source_target_pairs={{0,224},{32,0},{64,32},{96,64},{128,96},{160,128},{192,160},{224,1... | collective-permute-start | bytes 786440 | tf_op jit(solution)/shard_map/ppermute | solution.py:239
  40.5 22.1 %copy-start.2 = (bf16[8,32,512]{2,1,0:T(8,128)(2,1)}, bf16[8,32,512]{2,1,0:T(8,128)(2,1)S(1)}, u32[]{:S(2)}) copy-start(bf16[8,32,512]{2,1,0:T(8,128)(2,1)S(1)} %collective-permute-done.refs_2_) | copy-start | bytes 786436
  40.5 11.2 %collective-permute-start.1 = (bf16[8,32,512]{2,1,0:T(8,128)(2,1)S(1)}, bf16[8,32,512]{2,1,0:T(8,128)(2,1)S(1)}, u32[]{:S(2)}, u32[]{:S(2)}) collective-permute-start(bf16[8,32,512]{2,1,0:T(8,128)(2,1)S(1)} %collective-permute-done.refs_2_), channel_id=1, source_target_pairs={{0,32},{32,64},{64,96},{96,128},{128,160},{160,192},{192,224},{224... | collective-permute-start | bytes 786440 | tf_op jit(solution)/shard_map/ppermute | solution.py:236
  42.5 20.2 %copy-start.3 = (bf16[8,32,512]{2,1,0:T(8,128)(2,1)}, bf16[8,32,512]{2,1,0:T(8,128)(2,1)S(1)}, u32[]{:S(2)}) copy-start(bf16[8,32,512]{2,1,0:T(8,128)(2,1)S(1)} %collective-permute-done.9.refs_5_) | copy-start | bytes 786436
  42.5 11.2 %collective-permute-start.10 = (bf16[8,32,512]{2,1,0:T(8,128)(2,1)S(1)}, bf16[8,32,512]{2,1,0:T(8,128)(2,1)S(1)}, u32[]{:S(2)}, u32[]{:S(2)}) collective-permute-start(bf16[8,32,512]{2,1,0:T(8,128)(2,1)S(1)} %collective-permute-done.9.refs_5_), channel_id=1, source_target_pairs={{0,224},{32,0},{64,32},{96,64},{128,96},{160,128},{192,160},{224,1... | collective-permute-start | bytes 786440 | tf_op jit(solution)/shard_map/ppermute | solution.py:239
  46.2 16.5 %copy-start.4 = (bf16[8,32,512]{2,1,0:T(8,128)(2,1)}, bf16[8,32,512]{2,1,0:T(8,128)(2,1)S(1)}, u32[]{:S(2)}) copy-start(bf16[8,32,512]{2,1,0:T(8,128)(2,1)S(1)} %collective-permute-done.3.refs_4_) | copy-start | bytes 786436
  46.2 11.2 %collective-permute-start.4 = (bf16[8,32,512]{2,1,0:T(8,128)(2,1)S(1)}, bf16[8,32,512]{2,1,0:T(8,128)(2,1)S(1)}, u32[]{:S(2)}, u32[]{:S(2)}) collective-permute-start(bf16[8,32,512]{2,1,0:T(8,128)(2,1)S(1)} %collective-permute-done.3.refs_4_), channel_id=1, source_target_pairs={{0,32},{32,64},{64,96},{96,128},{128,160},{160,192},{192,224},{224... | collective-permute-start | bytes 786440 | tf_op jit(solution)/shard_map/ppermute | solution.py:236
  48.1 14.6 %copy-start.5 = (bf16[8,32,512]{2,1,0:T(8,128)(2,1)}, bf16[8,32,512]{2,1,0:T(8,128)(2,1)S(1)}, u32[]{:S(2)}) copy-start(bf16[8,32,512]{2,1,0:T(8,128)(2,1)S(1)} %collective-permute-done.7.refs_7_) | copy-start | bytes 786436
  48.1 11.1 %collective-permute-start.8 = (bf16[8,32,512]{2,1,0:T(8,128)(2,1)S(1)}, bf16[8,32,512]{2,1,0:T(8,128)(2,1)S(1)}, u32[]{:S(2)}, u32[]{:S(2)}) collective-permute-start(bf16[8,32,512]{2,1,0:T(8,128)(2,1)S(1)} %collective-permute-done.7.refs_7_), channel_id=1, source_target_pairs={{0,224},{32,0},{64,32},{96,64},{128,96},{160,128},{192,160},{224,1... | collective-permute-start | bytes 786440 | tf_op jit(solution)/shard_map/ppermute | solution.py:239
  51.8 10.9 %copy-start.6 = (bf16[8,32,512]{2,1,0:T(8,128)(2,1)}, bf16[8,32,512]{2,1,0:T(8,128)(2,1)S(1)}, u32[]{:S(2)}) copy-start(bf16[8,32,512]{2,1,0:T(8,128)(2,1)S(1)} %collective-permute-done.1.refs_6_) | copy-start | bytes 786436
  51.8 10.8 %collective-permute-start.2 = (bf16[8,32,512]{2,1,0:T(8,128)(2,1)S(1)}, bf16[8,32,512]{2,1,0:T(8,128)(2,1)S(1)}, u32[]{:S(2)}, u32[]{:S(2)}) collective-permute-start(bf16[8,32,512]{2,1,0:T(8,128)(2,1)S(1)} %collective-permute-done.1.refs_6_), channel_id=1, source_target_pairs={{0,32},{32,64},{64,96},{96,128},{128,160},{160,192},{192,224},{224... | collective-permute-start | bytes 786440 | tf_op jit(solution)/shard_map/ppermute | solution.py:236
  53.7 9.0 %copy-start.7 = (bf16[8,32,512]{2,1,0:T(8,128)(2,1)}, bf16[8,32,512]{2,1,0:T(8,128)(2,1)S(1)}, u32[]{:S(2)}) copy-start(bf16[8,32,512]{2,1,0:T(8,128)(2,1)S(1)} %collective-permute-done.10.refs_9_) | copy-start | bytes 786436
  53.7 8.9 %collective-permute-start.11 = (bf16[8,32,512]{2,1,0:T(8,128)(2,1)S(1)}, bf16[8,32,512]{2,1,0:T(8,128)(2,1)S(1)}, u32[]{:S(2)}, u32[]{:S(2)}) collective-permute-start(bf16[8,32,512]{2,1,0:T(8,128)(2,1)S(1)} %collective-permute-done.10.refs_9_), channel_id=1, source_target_pairs={{0,224},{32,0},{64,32},{96,64},{128,96},{160,128},{192,160},{224,1... | collective-permute-start | bytes 786440 | tf_op jit(solution)/shard_map/ppermute | solution.py:239
  57.4 11.4 %copy-start.8 = (bf16[8,32,512]{2,1,0:T(8,128)(2,1)}, bf16[8,32,512]{2,1,0:T(8,128)(2,1)S(1)}, u32[]{:S(2)}) copy-start(bf16[8,32,512]{2,1,0:T(8,128)(2,1)S(1)} %collective-permute-done.4.refs_8_) | copy-start | bytes 786436
  57.4 8.1 %collective-permute-start.5 = (bf16[8,32,512]{2,1,0:T(8,128)(2,1)S(1)}, bf16[8,32,512]{2,1,0:T(8,128)(2,1)}, u32[]{:S(2)}, u32[]{:S(2)}) collective-permute-start(bf16[8,32,512]{2,1,0:T(8,128)(2,1)S(1)} %collective-permute-done.4.refs_8_), channel_id=1, source_target_pairs={{0,32},{32,64},{64,96},{96,128},{128,160},{160,192},{192,224},{224... | collective-permute-start | bytes 786440 | tf_op jit(solution)/shard_map/ppermute | solution.py:236
  59.2 3.5 %copy-start.9 = (bf16[8,32,512]{2,1,0:T(8,128)(2,1)}, bf16[8,32,512]{2,1,0:T(8,128)(2,1)S(1)}, u32[]{:S(2)}) copy-start(bf16[8,32,512]{2,1,0:T(8,128)(2,1)S(1)} %collective-permute-done.8.refs_11_) | copy-start | bytes 786436
  62.6 0.7 copy-start.10
  63.3 0.7 copy-start.11
  65.5 10.2 %collective-permute-start.12 = (bf16[8,6,64,512]{3,2,1,0:T(8,128)(2,1)S(1)}, bf16[8,6,64,512]{3,2,1,0:T(8,128)(2,1)}, u32[]{:S(2)}, u32[]{:S(2)}) collective-permute-start(bf16[8,6,64,512]{3,2,1,0:T(8,128)(2,1)S(1)} %bitcast.16), channel_id=1, source_target_pairs={{0,8},{8,0},{1,9},{9,1},{2,10},{10,2},{3,11},{11,3},{4,12},{12,4},... | collective-permute-start | bytes 9437192 | tf_op jit(solution)/shard_map/ppermute | solution.py:316
  65.5 10.1 %collective-permute-start.13 = (bf16[8,32,512]{2,1,0:T(8,128)(2,1)}, bf16[8,32,512]{2,1,0:T(8,128)(2,1)S(1)}, u32[]{:S(2)}, u32[]{:S(2)}) collective-permute-start(bf16[8,32,512]{2,1,0:T(8,128)(2,1)} %copy-done.10), channel_id=1, source_target_pairs={{0,32},{32,64},{64,96},{96,128},{128,160},{160,192},{192,224},{224... | collective-permute-start | bytes 786440 | tf_op jit(solution)/shard_map/ppermute | solution.py:236
  65.5 10.1 %collective-permute-start.14 = (bf16[8,32,512]{2,1,0:T(8,128)(2,1)}, bf16[8,32,512]{2,1,0:T(8,128)(2,1)S(1)}, u32[]{:S(2)}, u32[]{:S(2)}) collective-permute-start(bf16[8,32,512]{2,1,0:T(8,128)(2,1)} %copy-done.11), channel_id=1, source_target_pairs={{0,224},{32,0},{64,32},{96,64},{128,96},{160,128},{192,160},{224,1... | collective-permute-start | bytes 786440 | tf_op jit(solution)/shard_map/ppermute | solution.py:239
  81.8 2.1 %collective-permute-start.15 = (f32[1152,128]{1,0:T(8,128)S(1)}, f32[1152,128]{1,0:T(8,128)S(1)}, u32[]{:S(2)}, u32[]{:S(2)}) collective-permute-start(f32[1152,128]{1,0:T(8,128)S(1)} %get-tuple-element.23), channel_id=1, source_target_pairs={{0,8},{8,0},{1,9},{9,1},{2,10},{10,2},{3,11},{11,3},{4,12},{12,4},... | collective-permute-start | bytes 1769480 | tf_op jit(solution)/shard_map/ppermute | solution.py:319
  84.7 19.0 %all-to-all-start.2 = ((f32[1152,1,128]{2,1,0:T(1,128)}), f32[1152,1,128]{2,1,0:T(1,128)S(1)}, u32[]{:S(2)}, u32[]{:S(2)}) async-start(f32[1152,1,128]{2,1,0:T(1,128)} %bitcast.7), calls=%async_computation.2 | async-start | bytes 1179648 | tf_op jit(solution)/shard_map/all_to_all | solution.py:293
  104.3 12.3 %all-to-all-start.3 = ((f32[72,1,128]{2,1,0:T(1,128)}), f32[72,1,128]{2,1,0:T(1,128)S(1)}, u32[]{:S(2)}, u32[]{:S(2)}) async-start(f32[72,1,128]{2,1,0:T(1,128)} %bitcast.22), calls=%async_computation.3 | async-start | bytes 73728 | tf_op jit(solution)/shard_map/all_to_all | solution.py:293
